TPU v7x, 32 devices: a whole 2x2x4 slice. The times are simulated.
32 devices in a mesh: dp: 16 (over z, y, core), mp: 2 (over x).
Axes of the slice: x: 2, y: 2, z: 4, core: 2. Of those that a mesh axis runs over, the one named last changes fastest.
Arguments:
- patches: bfloat16 [32, 256, 1152], P('dp'), may hold values from -8 to 8
- time_bins: int32 [32], P('dp'), may hold values from 0 to 999
- class_ids: int32 [32], P('dp'), may hold values from 0 to 1000
- encoder_feats: bfloat16 [32, 256, 768], P('dp'), may hold values from -6 to 6
- cotangent: bfloat16 [32, 256, 1152], P('dp'), may hold values from -2 to 2
- w_qkv: bfloat16 [3, 1152, 1152], P(None, 'dp', 'mp'), may hold values from -0.1875 to 0.1875
- w_out: bfloat16 [1152, 1152], P('mp', 'dp'), may hold values from -0.75 to 0.75
- w_up: bfloat16 [1152, 4608], P('dp', 'mp'), may hold values from -0.1875 to 0.1875
- w_down: bfloat16 [4608, 1152], P('mp', 'dp'), may hold values from -0.09375 to 0.09375
- w_ada: bfloat16 [6, 1152, 1152], P(None, 'dp'), may hold values from -0.1875 to 0.1875
- time_table: bfloat16 [1000, 1152], P(None, 'dp'), may hold values from -4 to 4
- class_table: bfloat16 [1001, 1152], P(None, 'dp'), may hold values from -4 to 4
- inner_bias: float32 [2, 3456], P('mp', 'dp'), may hold values from -1.75 to 1.75
- b_out: float32 [1152], P('dp'), may hold values from -1.75 to 1.75
- b_down: float32 [1152], P('dp'), may hold values from -1.75 to 1.75
- b_ada: float32 [6, 1152], P(None, 'dp'), may hold values from -1.75 to 1.75
- w_first: bfloat16 [1152, 2048], P(None, ('dp', 'mp')), may hold values from -0.1875 to 0.1875
- w_second: bfloat16 [2048, 2048], P(None, ('dp', 'mp')), may hold values from -0.125 to 0.125
- w_third: bfloat16 [2048, 768], P(None, ('dp', 'mp')), may hold values from -0.125 to 0.125
- b_first: float32 [2048], P(('dp', 'mp')), may hold values from -1.75 to 1.75
- b_second: float32 [2048], P(('dp', 'mp')), may hold values from -1.75 to 1.75
- b_third: float32 [768], P(('dp', 'mp')), may hold values from -3 to 3
Outputs:
- block_out: bfloat16 [32, 256, 1152], P('dp')
- grad_patches: float32 [32, 256, 1152], P('dp')
- grad_qkv: float32 [3, 1152, 1152], P(None, 'dp', 'mp')
- grad_wout: float32 [1152, 1152], P('mp', 'dp')
- grad_wup: float32 [1152, 4608], P('dp', 'mp')
- grad_wdown: float32 [4608, 1152], P('mp', 'dp')
- grad_wada: float32 [6, 1152, 1152], P(None, 'dp')
- grad_time: float32 [1000, 1152], P(None, 'dp')
- grad_class: float32 [1001, 1152], P(None, 'dp')
- grad_inner: float32 [2, 3456], P('mp', 'dp')
- grad_bout: float32 [1152], P('dp')
- grad_bdown: float32 [1152], P('dp')
- grad_bada: float32 [6, 1152], P(None, 'dp')
- grad_wfirst: float32 [1152, 2048], P(None, ('dp', 'mp'))
- grad_wsecond: float32 [2048, 2048], P(None, ('dp', 'mp'))
- grad_wthird: float32 [2048, 768], P(None, ('dp', 'mp'))
- grad_bfirst: float32 [2048], P(('dp', 'mp'))
- grad_bsecond: float32 [2048], P(('dp', 'mp'))
- grad_bthird: float32 [768], P(('dp', 'mp'))
All inputs are finite; a program needn't handle non-finite values.
Results may differ from a plain program's by a relative error of at most 0.04.
Values may be sent and summed in bfloat16 or wider, within the bound.
No kernel may reach another device: no remote copies, remote signals or barrier semaphores. Data moves between devices by JAX's collectives and lax.ppermute only.
A program may use at most 320 MiB of HBM per device.

v0:
```python
import jax
import jax.numpy as jnp
from jax import lax
from jax.sharding import PartitionSpec as P

HD = 72


epsilon = 1e-06
gelu_slope = 0.7978845608028654
gelu_cubic = 0.044715


def layer_norm(values):
    center = values - jnp.mean(values, axis=-1, keepdims=True)
    inverse = lax.rsqrt(jnp.mean(center * center, axis=-1, keepdims=True) + epsilon)
    return (center * inverse, inverse)


def norm_back(incoming, normed, inverse):
    return inverse * (
        incoming
        - jnp.mean(incoming, axis=-1, keepdims=True)
        - normed * jnp.mean(incoming * normed, axis=-1, keepdims=True)
    )


def gelu_tanh(values):
    inside = gelu_slope * (values + gelu_cubic * values * values * values)
    return 0.5 * values * (1.0 + jnp.tanh(inside))


def gelu_grad(values):
    tangent = jnp.tanh(gelu_slope * (values + gelu_cubic * values * values * values))
    return 0.5 * (1.0 + tangent) + 0.5 * values * (1.0 - tangent * tangent) * gelu_slope * (
        1.0 + 3.0 * gelu_cubic * values * values
    )


def silu_grad(values):
    sigma = jax.nn.sigmoid(values)
    return sigma * (1.0 + values * (1.0 - sigma))


def layer_sum(partial_sum):
    share = lax.psum_scatter(
        partial_sum.astype(jnp.bfloat16), "mp", scatter_dimension=0, tiled=True
    ).astype(jnp.float32)
    return lax.all_gather(share.astype(jnp.bfloat16), "mp", axis=0, tiled=True).astype(share.dtype)


def feature_sum(partial_sum):
    share = lax.psum_scatter(
        partial_sum.astype(jnp.bfloat16), "mp", scatter_dimension=0, tiled=True
    ).astype(jnp.float32)
    return lax.all_gather(share.astype(jnp.bfloat16), "mp", axis=0, tiled=True).astype(share.dtype)


def lookup(bin_ids, label_ids, bin_rows, class_rows):
    bin_onehot = bin_ids[:, None] == jnp.arange(bin_rows.shape[0], dtype=jnp.int32)[None, :]
    class_onehot = label_ids[:, None] == jnp.arange(class_rows.shape[0], dtype=jnp.int32)[None, :]
    condition = jnp.dot(
        bin_onehot.astype(jnp.bfloat16), bin_rows, preferred_element_type=jnp.float32
    ) + jnp.dot(class_onehot.astype(jnp.bfloat16), class_rows, preferred_element_type=jnp.float32)
    return (bin_onehot, class_onehot, condition)


def shards(
    patches,
    time_bins,
    class_ids,
    encoder_feats,
    cotangent,
    w_qkv,
    w_out,
    w_up,
    w_down,
    w_ada,
    time_table,
    class_table,
    inner_bias,
    b_out,
    b_down,
    b_ada,
    w_first,
    w_second,
    w_third,
    b_first,
    b_second,
    b_third,
):
    f32 = jnp.float32
    bf16 = jnp.bfloat16
    image_count, seq_len, width = patches.shape
    gathered = (
        lax.all_gather(w_qkv, "dp", axis=1, tiled=True),
        lax.all_gather(w_out, "dp", axis=1, tiled=True),
        lax.all_gather(w_up, "dp", axis=0, tiled=True),
        lax.all_gather(w_down, "dp", axis=1, tiled=True),
        lax.all_gather(inner_bias.astype(jnp.bfloat16), "dp", axis=1, tiled=True).astype(
            inner_bias.dtype
        ),
        lax.all_gather(b_out.astype(jnp.bfloat16), "dp", axis=0, tiled=True).astype(b_out.dtype),
        lax.all_gather(b_down.astype(jnp.bfloat16), "dp", axis=0, tiled=True).astype(b_down.dtype),
        lax.all_gather(b_ada.astype(jnp.bfloat16), "dp", axis=1, tiled=True).astype(b_ada.dtype),
    )
    full_qkv, full_out, full_up, full_down, full_inner, full_bout, full_bdown, full_bada = gathered
    every_bin, every_label = (
        lax.all_gather(time_bins, "dp", axis=0, tiled=True),
        lax.all_gather(class_ids, "dp", axis=0, tiled=True),
    )
    bin_onehot, class_onehot, condition = lookup(every_bin, every_label, time_table, class_table)
    cond_act = jax.nn.silu(condition).astype(bf16)
    partial_mods = jnp.einsum("bd,tde->bte", cond_act, w_ada, preferred_element_type=f32)
    modulation = lax.psum_scatter(partial_mods, "dp", scatter_dimension=0, tiled=True) + full_bada
    projector = (
        lax.all_gather(w_first, ("dp", "mp"), axis=1, tiled=True),
        lax.all_gather(w_second, ("dp", "mp"), axis=1, tiled=True),
        lax.all_gather(w_third, ("dp", "mp"), axis=1, tiled=True),
        lax.all_gather(b_first.astype(jnp.bfloat16), ("dp", "mp"), axis=0, tiled=True).astype(
            b_first.dtype
        ),
        lax.all_gather(b_second.astype(jnp.bfloat16), ("dp", "mp"), axis=0, tiled=True).astype(
            b_second.dtype
        ),
        lax.all_gather(b_third.astype(jnp.bfloat16), ("dp", "mp"), axis=0, tiled=True).astype(
            b_third.dtype
        ),
    )
    proj_one, proj_two, proj_three, bias_one, bias_two, bias_three = projector
    local_width = full_qkv.shape[2]
    head_count = local_width // HD
    flat_inner = full_inner.reshape(-1)
    bias_query = flat_inner[:local_width]
    bias_value = flat_inner[local_width : 2 * local_width]
    bias_units = flat_inner[2 * local_width :]
    score_scale = float(HD) ** (-0.5)
    shift_one = modulation[:, 0:1, :]
    scale_one = modulation[:, 1:2, :]
    gate_one = modulation[:, 2:3, :]
    shift_two = modulation[:, 3:4, :]
    scale_two = modulation[:, 4:5, :]
    gate_two = modulation[:, 5:6, :]
    inputs = patches.astype(f32)
    normed_one, inverse_one = layer_norm(inputs)
    act_one = (normed_one * (1.0 + scale_one) + shift_one).astype(bf16)
    qkv_proj = jnp.einsum("bld,tdc->tblc", act_one, full_qkv, preferred_element_type=f32)
    head_shape = (image_count, seq_len, head_count, HD)
    queries = (qkv_proj[0] + bias_query).astype(bf16).reshape(head_shape)
    key_heads = qkv_proj[1].astype(bf16).reshape(head_shape)
    val_heads = (qkv_proj[2] + bias_value).astype(bf16).reshape(head_shape)
    scores = (
        jnp.einsum("bqhd,bkhd->bhqk", queries, key_heads, preferred_element_type=f32) * score_scale
    )
    row_max = jnp.max(scores, axis=-1, keepdims=True)
    shifted = jnp.exp(scores - row_max)
    exp_total = jnp.sum(shifted, axis=-1, keepdims=True)
    log_total = row_max + jnp.log(exp_total)
    attn_probs = (shifted / exp_total).astype(bf16)
    mixed_heads = jnp.einsum("bhqk,bkhd->bqhd", attn_probs, val_heads, preferred_element_type=f32)
    mixed_heads = mixed_heads.reshape(image_count, seq_len, local_width).astype(bf16)
    attention = (
        layer_sum(jnp.einsum("blc,cd->bld", mixed_heads, full_out, preferred_element_type=f32))
        + full_bout
    )
    first_sum = inputs + gate_one * attention
    normed_two, inverse_two = layer_norm(first_sum)
    act_two = (normed_two * (1.0 + scale_two) + shift_two).astype(bf16)
    hidden = jnp.einsum("bld,df->blf", act_two, full_up, preferred_element_type=f32) + bias_units
    active = gelu_tanh(hidden).astype(bf16)
    branch = (
        layer_sum(jnp.einsum("blf,fd->bld", active, full_down, preferred_element_type=f32))
        + full_bdown
    )
    output = first_sum + gate_two * branch
    block_out = output.astype(bf16)
    share_count = image_count // lax.axis_size("mp")
    share_start = lax.axis_index("mp") * share_count
    proj_input = lax.dynamic_slice_in_dim(block_out, share_start, share_count, 0).reshape(
        share_count * seq_len, width
    )
    target = lax.dynamic_slice_in_dim(encoder_feats, share_start, share_count, 0)
    target = target.reshape(share_count * seq_len, -1).astype(f32)
    pre_one = jnp.dot(proj_input, proj_one, preferred_element_type=f32) + bias_one
    act_pone = jax.nn.silu(pre_one).astype(bf16)
    pre_two = jnp.dot(act_pone, proj_two, preferred_element_type=f32) + bias_two
    act_ptwo = jax.nn.silu(pre_two).astype(bf16)
    mapped = jnp.dot(act_ptwo, proj_three, preferred_element_type=f32) + bias_three
    inv_map = lax.rsqrt(jnp.sum(mapped * mapped, axis=-1, keepdims=True) + epsilon)
    inv_target = lax.rsqrt(jnp.sum(target * target, axis=-1, keepdims=True) + epsilon)
    cosine = jnp.sum(mapped * target, axis=-1, keepdims=True) * inv_map * inv_target
    loss_weight = -0.5 * float(width)
    grad_mapped = (
        loss_weight * (target * inv_map * inv_target - cosine * inv_map * inv_map * mapped)
    ).astype(bf16)
    grad_wthird = jnp.einsum("rp,re->pe", act_ptwo, grad_mapped, preferred_element_type=f32)
    grad_bthird = jnp.sum(grad_mapped.astype(f32), axis=0)
    grad_pre_two = (
        jnp.einsum("re,pe->rp", grad_mapped, proj_three, preferred_element_type=f32)
        * silu_grad(pre_two)
    ).astype(bf16)
    grad_wsecond = jnp.einsum("rp,rq->pq", act_pone, grad_pre_two, preferred_element_type=f32)
    grad_bsecond = jnp.sum(grad_pre_two.astype(f32), axis=0)
    grad_pre_one = (
        jnp.einsum("rq,pq->rp", grad_pre_two, proj_two, preferred_element_type=f32)
        * silu_grad(pre_one)
    ).astype(bf16)
    grad_wfirst = jnp.einsum("rd,rp->dp", proj_input, grad_pre_one, preferred_element_type=f32)
    grad_bfirst = jnp.sum(grad_pre_one.astype(f32), axis=0)
    grad_feed = jnp.einsum("rp,dp->rd", grad_pre_one, proj_one, preferred_element_type=f32)
    grad_feed = grad_feed.astype(bf16).reshape(share_count, seq_len, width)
    proj_sums = (
        lax.psum_scatter(grad_wfirst, ("dp", "mp"), scatter_dimension=1, tiled=True),
        lax.psum_scatter(grad_wsecond, ("dp", "mp"), scatter_dimension=1, tiled=True),
        lax.psum_scatter(grad_wthird, ("dp", "mp"), scatter_dimension=1, tiled=True),
        lax.psum_scatter(grad_bfirst, ("dp", "mp"), scatter_dimension=0, tiled=True),
        lax.psum_scatter(grad_bsecond, ("dp", "mp"), scatter_dimension=0, tiled=True),
        lax.psum_scatter(grad_bthird, ("dp", "mp"), scatter_dimension=0, tiled=True),
    )
    all_feed = lax.all_gather(grad_feed, "mp", axis=0, tiled=True)
    grad_output = cotangent.astype(f32) + all_feed.astype(f32)
    grad_branch = (gate_two * grad_output).astype(bf16)
    grad_gate_two = jnp.sum(grad_output * branch, axis=1)
    grad_bdown = jnp.sum(grad_branch.astype(f32), axis=(0, 1))
    grad_wdown = jnp.einsum("blf,bld->fd", active, grad_branch, preferred_element_type=f32)
    grad_active = jnp.einsum("bld,fd->blf", grad_branch, full_down, preferred_element_type=f32)
    grad_hidden = (grad_active * gelu_grad(hidden)).astype(bf16)
    grad_bunits = jnp.sum(grad_hidden.astype(f32), axis=(0, 1))
    grad_wup = jnp.einsum("bld,blf->df", act_two, grad_hidden, preferred_element_type=f32)
    grad_act_two = feature_sum(
        jnp.einsum("blf,df->bld", grad_hidden, full_up, preferred_element_type=f32)
    )
    grad_shift_two = jnp.sum(grad_act_two, axis=1)
    grad_scale_two = jnp.sum(grad_act_two * normed_two, axis=1)
    grad_first_sum = grad_output + norm_back(
        grad_act_two * (1.0 + scale_two), normed_two, inverse_two
    )
    grad_attention = (gate_one * grad_first_sum).astype(bf16)
    grad_gate_one = jnp.sum(grad_first_sum * attention, axis=1)
    grad_bout = jnp.sum(grad_attention.astype(f32), axis=(0, 1))
    grad_wout = jnp.einsum("blc,bld->cd", mixed_heads, grad_attention, preferred_element_type=f32)
    grad_mixed = jnp.einsum("bld,cd->blc", grad_attention, full_out, preferred_element_type=f32)
    grad_mixed = grad_mixed.astype(bf16).reshape(head_shape)
    scores = (
        jnp.einsum("bqhd,bkhd->bhqk", queries, key_heads, preferred_element_type=f32) * score_scale
    )
    probs_again = jnp.exp(scores - log_total)
    grad_values = jnp.einsum(
        "bhqk,bqhd->bkhd", probs_again.astype(bf16), grad_mixed, preferred_element_type=f32
    )
    grad_probs = jnp.einsum("bqhd,bkhd->bhqk", grad_mixed, val_heads, preferred_element_type=f32)
    inner_prod = jnp.sum(probs_again * grad_probs, axis=-1, keepdims=True)
    grad_scores = (probs_again * (grad_probs - inner_prod)).astype(bf16)
    grad_queries = (
        jnp.einsum("bhqk,bkhd->bqhd", grad_scores, key_heads, preferred_element_type=f32)
        * score_scale
    )
    grad_keys = (
        jnp.einsum("bhqk,bqhd->bkhd", grad_scores, queries, preferred_element_type=f32)
        * score_scale
    )
    flat_shape = (image_count, seq_len, local_width)
    grad_qkv_act = jnp.stack(
        (
            grad_queries.reshape(flat_shape),
            grad_keys.reshape(flat_shape),
            grad_values.reshape(flat_shape),
        ),
        axis=0,
    ).astype(bf16)
    grad_bquery = jnp.sum(grad_qkv_act[0].astype(f32), axis=(0, 1))
    grad_bvalue = jnp.sum(grad_qkv_act[2].astype(f32), axis=(0, 1))
    grad_wqkv = jnp.einsum("bld,tblc->tdc", act_one, grad_qkv_act, preferred_element_type=f32)
    grad_act_one = feature_sum(
        jnp.einsum("tblc,tdc->bld", grad_qkv_act, full_qkv, preferred_element_type=f32)
    )
    grad_shift_one = jnp.sum(grad_act_one, axis=1)
    grad_scale_one = jnp.sum(grad_act_one * normed_one, axis=1)
    grad_patches = grad_first_sum + norm_back(
        grad_act_one * (1.0 + scale_one), normed_one, inverse_one
    )
    grad_mods = jnp.stack(
        (
            grad_shift_one,
            grad_scale_one,
            grad_gate_one,
            grad_shift_two,
            grad_scale_two,
            grad_gate_two,
        ),
        axis=1,
    ).astype(bf16)
    grad_inner = jnp.concatenate((grad_bquery, grad_bvalue, grad_bunits)).reshape(1, -1)
    every_mods = lax.all_gather(grad_mods, "dp", axis=0, tiled=True)
    local_rows = w_ada.shape[1]
    mods_total = jnp.sum(every_mods.astype(f32), axis=0)
    sum_bada = lax.dynamic_slice_in_dim(
        mods_total, lax.axis_index("dp") * local_rows, local_rows, 1
    )
    sum_wada = jnp.einsum("bd,bte->tde", cond_act, every_mods, preferred_element_type=f32)
    grad_cond = jnp.einsum("bte,tde->bd", every_mods, w_ada, preferred_element_type=f32)
    grad_cond = grad_cond * silu_grad(condition)
    sum_time = jnp.einsum(
        "bn,bd->nd", bin_onehot.astype(f32), grad_cond, precision=lax.Precision.HIGHEST
    )
    sum_class = jnp.einsum(
        "bn,bd->nd", class_onehot.astype(f32), grad_cond, precision=lax.Precision.HIGHEST
    )
    core_sums = (
        lax.psum_scatter(grad_wqkv, "dp", scatter_dimension=1, tiled=True),
        lax.psum_scatter(grad_wout, "dp", scatter_dimension=1, tiled=True),
        lax.psum_scatter(grad_wup, "dp", scatter_dimension=0, tiled=True),
        lax.psum_scatter(grad_wdown, "dp", scatter_dimension=1, tiled=True),
        lax.psum_scatter(grad_inner, "dp", scatter_dimension=1, tiled=True),
        lax.psum_scatter(grad_bout, "dp", scatter_dimension=0, tiled=True),
        lax.psum_scatter(grad_bdown, "dp", scatter_dimension=0, tiled=True),
    )
    sum_qkv, sum_out, sum_up, sum_down, sum_inner, sum_bout, sum_bdown = core_sums
    return (
        block_out,
        grad_patches,
        sum_qkv,
        sum_out,
        sum_up,
        sum_down,
        sum_wada,
        sum_time,
        sum_class,
        sum_inner,
        sum_bout,
        sum_bdown,
        sum_bada,
        proj_sums[0],
        proj_sums[1],
        proj_sums[2],
        proj_sums[3],
        proj_sums[4],
        proj_sums[5],
    )


def solution(mesh):
    placed = (
        P("dp", None, None),
        P("dp"),
        P("dp"),
        P("dp", None, None),
        P("dp", None, None),
        P(None, "dp", "mp"),
        P("mp", "dp"),
        P("dp", "mp"),
        P("mp", "dp"),
        P(None, "dp", None),
        P(None, "dp"),
        P(None, "dp"),
        P("mp", "dp"),
        P("dp"),
        P("dp"),
        P(None, "dp"),
        P(None, ("dp", "mp")),
        P(None, ("dp", "mp")),
        P(None, ("dp", "mp")),
        P(("dp", "mp")),
        P(("dp", "mp")),
        P(("dp", "mp")),
    )
    return jax.shard_map(
        shards,
        mesh=mesh,
        in_specs=placed,
        out_specs=(
            P("dp", None, None),
            P("dp", None, None),
            P(None, "dp", "mp"),
            P("mp", "dp"),
            P("dp", "mp"),
            P("mp", "dp"),
            P(None, "dp", None),
            P(None, "dp"),
            P(None, "dp"),
            P("mp", "dp"),
            P("dp"),
            P("dp"),
            P(None, "dp"),
            P(None, ("dp", "mp")),
            P(None, ("dp", "mp")),
            P(None, ("dp", "mp")),
            P(("dp", "mp")),
            P(("dp", "mp")),
            P(("dp", "mp")),
        ),
        check_vma=False,
    )
```

profile of v0, /device:TPU:0, one launch (start us, length us, event | category | flops | bytes accessed | tf_op | source)
XLA Modules:
  0.0 1980.4 jit_solution(12507950533219854457)
XLA Ops:
  11.1 13.7 all-reduce.17
  32.7 57.9 %all-reduce.21 = (bf16[3456]{0:T(1024)(128)(2,1)S(1)}, bf16[1152]{0:T(1024)(128)(2,1)S(1)}, bf16[1152]{0:T(1024)(128)(2,1)S(1)}) all-reduce(bf16[3456]{0:T(1024)(128)(2,1)S(1)} %dynamic-update-slice.2, bf16[1152]{0:T(1024)(128)(2,1)S(1)} %dynamic-update-slice.3, ...), channel_id=1, replica_groups=mesh['dp'=16,'mp'=2] {'dp'}, use_global_device_ids=true, to_apply=%add.2 | all-reduce | flops 5760 | bytes 23040
  90.8 17.3 all-gather.1
  108.8 10.2 all-reduce.25.cloned.1.call-done
  119.9 51.9 %all-gather.15.cloned.1.call-done = bf16[3,1152,576]{2,1,0:T(8,128)(2,1)} async-done(((bf16[3,72,576]{2,1,0:T(8,128)(2,1)}), bf16[3,1152,576]{2,1,0:T(8,128)(2,1)}) %all-gather.15.cloned.1.call-update) | async-done | bytes 3981328 | tf_op jit(solution)/shard_map/all_gather | solution.py:96
  171.9 5.0 fusion.70
  181.7 30.2 %all-gather.17.cloned.1.call-done = bf16[576,1152]{0,1:T(8,128)(2,1)} async-done(((bf16[576,72]{0,1:T(8,128)(2,1)}), bf16[576,1152]{0,1:T(8,128)(2,1)}) %all-gather.17.cloned.1.call-update) | async-done | bytes 1327120 | tf_op jit(solution)/shard_map/all_gather | solution.py:97
  211.9 3.6 convolution_convert_fusion
  215.6 20.7 %reduce-scatter.15.cloned.1.call-done = bf16[1,256,1152]{2,1,0:T(8,128)(2,1)} async-done(((bf16[2,256,1152]{2,1,0:T(8,128)(2,1)}), bf16[1,256,1152]{2,1,0:T(8,128)(2,1)}) %reduce-scatter.15.cloned.1.call-update) | async-done | bytes 589840 | tf_op jit(solution)/shard_map/reduce_scatter | solution.py:46
  238.2 22.4 %all-gather.19.cloned.1.call-done = bf16[2,256,1152]{2,1,0:T(8,128)(2,1)} async-done(((bf16[1,256,1152]{2,1,0:T(8,128)(2,1)}), bf16[2,256,1152]{2,1,0:T(8,128)(2,1)}) %all-gather.19.cloned.1.call-update) | async-done | bytes 1179664 | tf_op jit(solution)/shard_map/all_gather | solution.py:49
  263.2 56.0 %all-gather.21.cloned.1.call-done = bf16[1152,2304]{1,0:T(8,128)(2,1)} async-done(((bf16[72,2304]{1,0:T(8,128)(2,1)}), bf16[1152,2304]{1,0:T(8,128)(2,1)}) %all-gather.21.cloned.1.call-update) | async-done | bytes 5308432 | tf_op jit(solution)/shard_map/all_gather | solution.py:98
  319.2 7.8 fusion.11
  327.0 49.6 %all-gather.23.cloned.1.call-done = bf16[2304,1152]{0,1:T(8,128)(2,1)} async-done(((bf16[2304,72]{0,1:T(8,128)(2,1)}), bf16[2304,1152]{0,1:T(8,128)(2,1)}) %all-gather.23.cloned.1.call-update) | async-done | bytes 5308432 | tf_op jit(solution)/shard_map/all_gather | solution.py:99
  376.6 9.0 fusion.36
  385.7 20.4 %reduce-scatter.17.cloned.1.call-done = bf16[1,256,1152]{2,1,0:T(8,128)(2,1)} async-done(((bf16[2,256,1152]{2,1,0:T(8,128)(2,1)}), bf16[1,256,1152]{2,1,0:T(8,128)(2,1)}) %reduce-scatter.17.cloned.1.call-update) | async-done | bytes 589840 | tf_op jit(solution)/shard_map/reduce_scatter | solution.py:46
  408.9 39.9 %all-reduce.20 = (bf16[768]{0:T(1024)(128)(2,1)S(1)}, bf16[2048]{0:T(1024)(128)(2,1)S(1)}, bf16[2048]{0:T(1024)(128)(2,1)S(1)}) all-reduce(bf16[768]{0:T(1024)(128)(2,1)S(1)} %dynamic-update-slice.7, bf16[2048]{0:T(1024)(128)(2,1)S(1)} %dynamic-update-slice.6, ...), channel_id=1, replica_groups=mesh['dp'=16,'mp'=2] {'dp','mp'}, use_global_device_ids=true, to_apply=%add.7 | all-reduce | flops 4864 | bytes 19456
  452.0 45.2 %all-gather.27.cloned.1.call-done = bf16[1152,2048]{0,1:T(8,128)(2,1)} async-done(((bf16[1152,64]{0,1:T(8,128)(2,1)}), bf16[1152,2048]{0,1:T(8,128)(2,1)}) %all-gather.27.cloned.1.call-update) | async-done | bytes 4718608 | tf_op jit(solution)/shard_map/all_gather | solution.py:117
  497.2 5.5 convolution_add_fusion.1
  502.6 73.8 %all-gather.29.cloned.1.call-done = bf16[2048,2048]{0,1:T(8,128)(2,1)} async-done(((bf16[2048,64]{0,1:T(8,128)(2,1)}), bf16[2048,2048]{0,1:T(8,128)(2,1)}) %all-gather.29.cloned.1.call-update) | async-done | bytes 8388624 | tf_op jit(solution)/shard_map/all_gather | solution.py:118
  576.4 7.7 convolution_add_fusion
  584.1 52.7 %all-gather.31.cloned.1.call-done = bf16[2048,768]{0,1:T(8,128)(2,1)} async-done(((bf16[2048,24]{0,1:T(8,128)(2,1)}), bf16[2048,768]{0,1:T(8,128)(2,1)}) %all-gather.31.cloned.1.call-update) | async-done | bytes 3145744 | tf_op jit(solution)/shard_map/all_gather | solution.py:119
  636.9 4.1 fusion.91
  652.0 21.5 %all-gather.37.cloned.1.call-done = bf16[512,1152]{1,0:T(8,128)(2,1)} async-done(((bf16[256,1152]{1,0:T(8,128)(2,1)}), bf16[512,1152]{1,0:T(8,128)(2,1)}) %all-gather.37.cloned.1.call-update) | async-done | bytes 1179664 | tf_op jit(solution)/shard_map/all_gather | solution.py:220
  675.7 8.7 convert_reduce_fusion
  685.8 4.2 fusion.33
  690.1 21.9 %reduce-scatter.19.cloned.1.call-done = bf16[1,256,1152]{2,1,0:T(8,128)(2,1)} async-done(((bf16[2,256,1152]{2,1,0:T(8,128)(2,1)}), bf16[1,256,1152]{2,1,0:T(8,128)(2,1)}) %reduce-scatter.19.cloned.1.call-update) | async-done | bytes 589840 | tf_op jit(solution)/shard_map/reduce_scatter | solution.py:53
  712.1 24.2 %all-gather.33.cloned.1.call-done = bf16[2,256,1152]{2,1,0:T(8,128)(2,1)} async-done(((bf16[1,256,1152]{2,1,0:T(8,128)(2,1)}), bf16[2,256,1152]{2,1,0:T(8,128)(2,1)}) %all-gather.33.cloned.1.call-update) | async-done | bytes 1179664 | tf_op jit(solution)/shard_map/all_gather | solution.py:56
  739.2 4.4 convert_reduce_fusion.3
  752.7 4.0 fusion.30
  756.8 21.9 %reduce-scatter.21.cloned.1.call-done = bf16[1,256,1152]{2,1,0:T(8,128)(2,1)} async-done(((bf16[2,256,1152]{2,1,0:T(8,128)(2,1)}), bf16[1,256,1152]{2,1,0:T(8,128)(2,1)}) %reduce-scatter.21.cloned.1.call-update) | async-done | bytes 589840 | tf_op jit(solution)/shard_map/reduce_scatter | solution.py:53
  779.2 7.2 convolution_bitcast_fusion.2
  786.4 13.8 copy.105
  800.3 5.4 fusion.124
  805.8 4.3 convolution_bitcast_fusion.3
  810.1 6.6 fusion.93
  816.7 9.8 convolution_bitcast_fusion
  826.8 8.9 convolution_bitcast_fusion.1
  835.8 10.3 fusion.123
  847.5 41.2 %all-reduce.18 = (f32[2048]{0:T(1024)S(1)}, f32[2048]{0:T(1024)S(1)}, f32[768]{0:T(1024)S(1)}) all-reduce(f32[2048]{0:T(1024)S(1)} %get-tuple-element.169, f32[2048]{0:T(1024)S(1)} %get-tuple-element.171, f32[768]{0:T(1024)S(1)} %get-tuple-element.139), channel_id=18, replica_groups=mesh['dp'=16,'mp'=2] {'dp','mp'}, use_global_device_ids=true, to_apply=%region_42.43.clone | all-reduce | flops 4864 | bytes 38912
  892.9 61.6 %all-reduce.19 = (f32[1,3456]{1,0:T(1,128)S(1)}, f32[1152]{0:T(1024)S(1)}, f32[1152]{0:T(1024)S(1)}) all-reduce(f32[1,3456]{1,0:T(1,128)S(1)} %reshape.166, f32[1152]{0:T(1024)S(1)} %get-tuple-element.143, f32[1152]{0:T(1024)S(1)} %get-tuple-element.141), channel_id=12, replica_groups=mesh['dp'=16,'mp'=2] {'dp'}, use_global_device_ids=true, to_apply=%region_32.33.clone | all-reduce | flops 5760 | bytes 46080
  965.6 22.5 %all_gather.87 = bf16[32,6,1152]{2,1,0:T(8,128)(2,1)S(1)} all-gather(bf16[2,6,1152]{2,1,0:T(8,128)(2,1)S(1)} %copy.109), channel_id=1, replica_groups=mesh['dp'=16,'mp'=2] {'dp'}, dimensions={0}, use_global_device_ids=true | all-gather | bytes 470016 | tf_op jit(solution)/shard_map/all_gather | solution.py:294
  993.2 38.6 %all-reduce.27.cloned.1.call-done = f32[3,1152,576]{2,0,1:T(4,128)} async-done(((f32[3,1152,576]{2,0,1:T(4,128)}), f32[3,1152,576]{2,0,1:T(4,128)}) %all-reduce.27.cloned.1.call-update) | async-done | bytes 7962640
  1033.8 119.7 %reduce-scatter.31.cloned.1.call-done = f32[2048,24]{0,1:T(8,128)} async-done(((f32[2048,768]{0,1:T(8,128)}), f32[2048,24]{0,1:T(8,128)}) %reduce-scatter.31.cloned.1.call-update) | async-done | bytes 196624 | tf_op jit(solution)/shard_map/reduce_scatter | solution.py:215
  1153.5 69.3 %reduce-scatter.33.cloned.1.call-done = f32[576,72]{0,1:T(8,128)} async-done(((f32[576,1152]{0,1:T(8,128)}), f32[576,72]{0,1:T(8,128)}) %reduce-scatter.33.cloned.1.call-update) | async-done | bytes 165904
  1222.8 142.0 %reduce-scatter.27.cloned.1.call-done = f32[1152,64]{0,1:T(8,128)} async-done(((f32[1152,2048]{0,1:T(8,128)}), f32[1152,64]{0,1:T(8,128)}) %reduce-scatter.27.cloned.1.call-update) | async-done | bytes 294928 | tf_op jit(solution)/shard_map/reduce_scatter | solution.py:213
  1364.8 124.0 %reduce-scatter.25.cloned.1.call-done = f32[2304,72]{0,1:T(8,128)} async-done(((f32[2304,1152]{0,1:T(8,128)}), f32[2304,72]{0,1:T(8,128)}) %reduce-scatter.25.cloned.1.call-update) | async-done | bytes 663568 | tf_op jit(solution)/shard_map/reduce_scatter | solution.py:313
  1488.8 124.7 %reduce-scatter.23.cloned.1.call-done = f32[72,2304]{1,0:T(8,128)} async-done(((f32[1152,2304]{1,0:T(8,128)}), f32[72,2304]{1,0:T(8,128)}) %reduce-scatter.23.cloned.1.call-update) | async-done | bytes 663568 | tf_op jit(solution)/shard_map/reduce_scatter | solution.py:312
  1613.5 359.9 %reduce-scatter.29.cloned.1.call-done = f32[2048,64]{0,1:T(8,128)} async-done(((f32[2048,2048]{0,1:T(8,128)}), f32[2048,64]{0,1:T(8,128)}) %reduce-scatter.29.cloned.1.call-update) | async-done | bytes 524304 | tf_op jit(solution)/shard_map/reduce_scatter | solution.py:214
  (257 shorter events, 76.0 us)
Async XLA Ops:
  7.2 19.9 %copy-start = (bf16[6,72,1152]{2,1,0:T(8,128)(2,1)S(1)}, bf16[6,72,1152]{2,1,0:T(8,128)(2,1)}, u32[]{:S(2)}) copy-start(bf16[6,72,1152]{2,1,0:T(8,128)(2,1)} %param.31) | copy-start | bytes 2985988
  7.2 24.0 %copy-start.35 = (f32[1,216]{1,0:T(1,128)S(1)}, f32[1,216]{1,0:T(1,128)}, u32[]{:S(2)}) copy-start(f32[1,216]{1,0:T(1,128)} %param.34) | copy-start | bytes 2596
  7.2 24.0 %copy-start.36 = (f32[72]{0:T(128)S(1)}, f32[72]{0:T(128)}, u32[]{:S(2)}) copy-start(f32[72]{0:T(128)} %param.35) | copy-start | bytes 868
  7.2 24.0 %copy-start.37 = (f32[72]{0:T(128)S(1)}, f32[72]{0:T(128)}, u32[]{:S(2)}) copy-start(f32[72]{0:T(128)} %param.36) | copy-start | bytes 868
  7.2 24.0 %copy-start.28 = (f32[6,72]{1,0:T(8,128)S(1)}, f32[6,72]{1,0:T(8,128)}, u32[]{:S(2)}) copy-start(f32[6,72]{1,0:T(8,128)} %param.37) | copy-start | bytes 5188
  7.2 24.0 %copy-start.3 = (bf16[2,256,1152]{2,1,0:T(8,128)(2,1)S(1)}, bf16[2,256,1152]{2,1,0:T(8,128)(2,1)}, u32[]{:S(2)}) copy-start(bf16[2,256,1152]{2,1,0:T(8,128)(2,1)} %param.22) | copy-start | bytes 3538948
  7.3 111.7 %all-reduce.25.cloned.1.call-start = ((), (), s32[]{:S(2)}) async-start(), calls=%async_computation.31 | async-start | bytes 1769472
  24.8 7.2 copy-start.29
  27.1 4.9 copy-start.25
  28.3 143.5 %all-gather.15.cloned.1.call-start = ((), (), s32[]{:S(2)}) async-start(), calls=%async_computation.10 | async-start | bytes 4700160 | tf_op jit(solution)/shard_map/all_gather | solution.py:96
  29.1 182.8 %all-gather.17.cloned.1.call-start = ((), (), s32[]{:S(2)}) async-start(), calls=%async_computation.11 | async-start | bytes 1566720 | tf_op jit(solution)/shard_map/all_gather | solution.py:97
  29.8 206.5 %reduce-scatter.15.cloned.1.call-start = ((), (), s32[]{:S(2)}) async-start(), calls=%async_computation.12 | async-start | bytes 1769472 | tf_op jit(solution)/shard_map/reduce_scatter | solution.py:46
  181.7 33.9 %copy-start.22 = (bf16[2,8,72,256]{3,2,1,0:T(8,128)(2,1)}, bf16[2,8,72,256]{3,2,1,0:T(8,128)(2,1)S(1)}, u32[]{:S(2)}) copy-start(bf16[2,8,72,256]{3,2,1,0:T(8,128)(2,1)S(1)} %fusion.76) | copy-start | bytes 1769476
  215.6 45.0 %all-gather.19.cloned.1.call-start = ((), (), s32[]{:S(2)}) async-start(), calls=%async_computation.13 | async-start | bytes 1769472 | tf_op jit(solution)/shard_map/all_gather | solution.py:49
  236.3 82.9 %all-gather.21.cloned.1.call-start = ((), (), s32[]{:S(2)}) async-start(), calls=%async_computation.14 | async-start | bytes 5640192 | tf_op jit(solution)/shard_map/all_gather | solution.py:98
  236.9 139.7 %all-gather.23.cloned.1.call-start = ((), (), s32[]{:S(2)}) async-start(), calls=%async_computation.15 | async-start | bytes 5640192 | tf_op jit(solution)/shard_map/all_gather | solution.py:99
  237.6 168.5 %reduce-scatter.17.cloned.1.call-start = ((), (), s32[]{:S(2)}) async-start(), calls=%async_computation.16 | async-start | bytes 1769472 | tf_op jit(solution)/shard_map/reduce_scatter | solution.py:46
  327.0 81.1 %copy-start.38 = (f32[64]{0:T(128)S(1)}, f32[64]{0:T(128)}, u32[]{:S(2)}) copy-start(f32[64]{0:T(128)} %param.41) | copy-start | bytes 772
  327.0 81.1 %copy-start.39 = (f32[64]{0:T(128)S(1)}, f32[64]{0:T(128)}, u32[]{:S(2)}) copy-start(f32[64]{0:T(128)} %param.42) | copy-start | bytes 772
  327.0 81.1 %copy-start.40 = (f32[24]{0:T(128)S(1)}, f32[24]{0:T(128)}, u32[]{:S(2)}) copy-start(f32[24]{0:T(128)} %param.43) | copy-start | bytes 292
  385.7 63.2 %all-gather.25.cloned.1.call-start = ((), (), s32[]{:S(2)}) async-start(), calls=%async_computation.17 | async-start | bytes 1769472 | tf_op jit(solution)/shard_map/all_gather | solution.py:49
  406.2 91.0 %all-gather.27.cloned.1.call-start = ((), (), s32[]{:S(2)}) async-start(), calls=%async_computation.18 | async-start | bytes 4866048 | tf_op jit(solution)/shard_map/all_gather | solution.py:117
  406.7 169.7 %all-gather.29.cloned.1.call-start = ((), (), s32[]{:S(2)}) async-start(), calls=%async_computation.19 | async-start | bytes 8650752 | tf_op jit(solution)/shard_map/all_gather | solution.py:118
  407.5 229.4 %all-gather.31.cloned.1.call-start = ((), (), s32[]{:S(2)}) async-start(), calls=%async_computation.20 | async-start | bytes 3244032 | tf_op jit(solution)/shard_map/all_gather | solution.py:119
  408.1 265.4 %all-gather.37.cloned.1.call-start = ((), (), s32[]{:S(2)}) async-start(), calls=%async_computation.30 | async-start | bytes 1769472 | tf_op jit(solution)/shard_map/all_gather | solution.py:220
  636.9 4.5 copy-start.33
  636.9 4.5 copy-start.41
  641.4 8.0 slice-start.4
  642.7 5.6 copy-start.20
  651.7 60.3 %reduce-scatter.19.cloned.1.call-start = ((), (), s32[]{:S(2)}) async-start(), calls=%async_computation.21 | async-start | bytes 1769472 | tf_op jit(solution)/shard_map/reduce_scatter | solution.py:53
  673.5 12.4 slice-start.2
  675.7 8.7 copy-start.19
  675.7 10.1 slice-start.3
  690.1 46.2 %all-gather.33.cloned.1.call-start = ((), (), s32[]{:S(2)}) async-start(), calls=%async_computation.22 | async-start | bytes 1769472 | tf_op jit(solution)/shard_map/all_gather | solution.py:56
  712.0 66.6 %reduce-scatter.21.cloned.1.call-start = ((), (), s32[]{:S(2)}) async-start(), calls=%async_computation.23 | async-start | bytes 1769472 | tf_op jit(solution)/shard_map/reduce_scatter | solution.py:53
  739.2 4.5 copy-start.34
  747.5 5.2 slice-start.6
  756.7 201.1 %all-gather.35.cloned.1.call-start = ((), (), s32[]{:S(2)}) async-start(), calls=%async_computation.24 | async-start | bytes 1769472 | tf_op jit(solution)/shard_map/all_gather | solution.py:56
  778.7 253.0 %all-reduce.27.cloned.1.call-start = ((), (), s32[]{:S(2)}) async-start(), calls=%async_computation.32 | async-start | bytes 23592960
  800.3 353.2 %reduce-scatter.31.cloned.1.call-start = ((), (), s32[]{:S(2)}) async-start(), calls=%async_computation.29 | async-start | bytes 6488064 | tf_op jit(solution)/shard_map/reduce_scatter | solution.py:215
  805.7 417.1 %reduce-scatter.33.cloned.1.call-start = ((), (), s32[]{:S(2)}) async-start(), calls=%async_computation.33 | async-start | bytes 3133440
  810.1 554.7 %reduce-scatter.27.cloned.1.call-start = ((), (), s32[]{:S(2)}) async-start(), calls=%async_computation.27 | async-start | bytes 9732096 | tf_op jit(solution)/shard_map/reduce_scatter | solution.py:213
  816.7 672.1 %reduce-scatter.25.cloned.1.call-start = ((), (), s32[]{:S(2)}) async-start(), calls=%async_computation.26 | async-start | bytes 11280384 | tf_op jit(solution)/shard_map/reduce_scatter | solution.py:313
  826.6 786.9 %reduce-scatter.23.cloned.1.call-start = ((), (), s32[]{:S(2)}) async-start(), calls=%async_computation.25 | async-start | bytes 11280384 | tf_op jit(solution)/shard_map/reduce_scatter | solution.py:312
  835.7 1137.6 %reduce-scatter.29.cloned.1.call-start = ((), (), s32[]{:S(2)}) async-start(), calls=%async_computation.28 | async-start | bytes 17301504 | tf_op jit(solution)/shard_map/reduce_scatter | solution.py:214
  961.9 27.0 %copy-start.26 = (f32[32,72]{1,0:T(8,128)S(1)}, f32[32,72]{1,0:T(8,128)}, u32[]{:S(2)}) copy-start(f32[32,72]{1,0:T(8,128)} %copy-done.25) | copy-start | bytes 27652
  965.5 23.8 %copy-start.30 = (s32[32]{0:T(128)S(1)}, s32[32]{0:T(128)}, u32[]{:S(2)}) copy-start(s32[32]{0:T(128)} %copy-done.29) | copy-start | bytes 388
  965.5 24.9 %copy-start.32 = (s32[32]{0:T(128)S(1)}, s32[32]{0:T(128)}, u32[]{:S(2)}) copy-start(s32[32]{0:T(128)} %copy-done.31) | copy-start | bytes 388
  (27 other events, 61.6 us)
Sparse Core Ops, SparseCore 0:
  28.4 90.4 all-reduce.24
  121.1 50.6 all-gather.14
  174.0 37.8 all-gather.16
  215.7 20.5 reduce-scatter.14
  237.8 22.7 all-gather.18
  262.8 56.3 all-gather.20
  321.6 54.9 all-gather.22
  385.8 20.3 reduce-scatter.16
  407.7 23.1 all-gather.24
  433.6 63.5 all-gather.26
  500.2 76.2 all-gather.28
  579.2 57.6 all-gather.30
  651.8 21.5 all-gather.36
  690.2 21.7 reduce-scatter.18
  713.5 22.7 all-gather.32
  756.9 21.7 reduce-scatter.20
  780.0 22.7 all-gather.34
  806.4 225.2 all-reduce.26
  1037.9 115.5 reduce-scatter.30
  1158.3 64.4 reduce-scatter.32
  1230.3 134.4 reduce-scatter.26
  1369.4 119.3 reduce-scatter.24
  1493.5 119.9 reduce-scatter.22
  1616.2 357.0 reduce-scatter.28
where the time goes:
time: 1990 us; the launch traced here: 1980 us
  waiting for transfers between devices  1510 us (76%)
  blocking collectives  254 us (13%)
  matrix products  133 us (7%)
  local copies, waits for them, and re-layouts  36 us (2%)
  other arithmetic  30.7 us (2%)
    reduce_scatter x1, waiting for transfers between devices, shards(): lax.psum_scatter(grad_wsecond, ('dp', 'mp'), scatter_dimension=1, tiled=T...  360 us
    unnamed x5, blocking collectives  214 us
    reduce_scatter x1, waiting for transfers between devices, shards(): lax.psum_scatter(grad_wfirst, ('dp', 'mp'), scatter_dimension=1, tiled=True)  142 us
    reduce_scatter x1, waiting for transfers between devices, shards(): lax.psum_scatter(grad_wup, 'dp', scatter_dimension=0, tiled=True)  125 us
    reduce_scatter x1, waiting for transfers between devices, shards(): lax.psum_scatter(grad_wdown, 'dp', scatter_dimension=1, tiled=True)  124 us
    unnamed x27, waiting for transfers between devices  123 us
    reduce_scatter x1, waiting for transfers between devices, shards(): lax.psum_scatter(grad_wthird, ('dp', 'mp'), scatter_dimension=1, tiled=True)  120 us
    all_gather x1, waiting for transfers between devices, shards(): lax.all_gather(w_second, ('dp', 'mp'), axis=1, tiled=True)  73.8 us
  transfers between devices with their start and end apart: 24, of which 22 were waited for; matrix products, arithmetic and copies ran while one was open for 6% of the time, Pallas kernels for 0%

commit v1 on v0

v1 whole, which is shorter than its diff:
```python
import jax
import jax.numpy as jnp
from jax import lax
from jax.experimental import pallas as pl
from jax.experimental.pallas import tpu as pltpu
from jax.sharding import PartitionSpec as P

HD = 72
ROWS = 2
CORES = 2


epsilon = 1e-06
gelu_slope = 0.7978845608028654
gelu_cubic = 0.044715


def layer_norm(values):
    center = values - jnp.mean(values, axis=-1, keepdims=True)
    inverse = lax.rsqrt(jnp.mean(center * center, axis=-1, keepdims=True) + epsilon)
    return (center * inverse, inverse)


def norm_back(incoming, normed, inverse):
    return inverse * (
        incoming
        - jnp.mean(incoming, axis=-1, keepdims=True)
        - normed * jnp.mean(incoming * normed, axis=-1, keepdims=True)
    )


def gelu_tanh(values):
    inside = gelu_slope * (values + gelu_cubic * values * values * values)
    return 0.5 * values * (1.0 + jnp.tanh(inside))


def gelu_grad(values):
    tangent = jnp.tanh(gelu_slope * (values + gelu_cubic * values * values * values))
    return 0.5 * (1.0 + tangent) + 0.5 * values * (1.0 - tangent * tangent) * gelu_slope * (
        1.0 + 3.0 * gelu_cubic * values * values
    )


def silu_grad(values):
    sigma = jax.nn.sigmoid(values)
    return sigma * (1.0 + values * (1.0 - sigma))


def place_pieces(pieces, place, planes, with_side, cuts):
    count = len(pieces)
    _, held, part_rows, columns = pieces[0].shape

    def body(place_ref, *refs):
        turn = pl.program_id(0)
        sources, targets = refs[:count], refs[count:]
        for k in range(count):

            @pl.when(turn == k)
            def _(k=k):
                for target, (start, end) in zip(targets, cuts):
                    target[...] = sources[k][0, start:end].reshape(target.shape)

    def source_map(k):
        def index_map(turn, s, place_ref):
            return jnp.where(turn == k, s, jnp.where(turn < k, 0, planes - 1)), 0, 0, 0

        return index_map

    def target_map(turn, s, place_ref):
        at_row = place_ref[planes] ^ (turn & 1)
        if with_side:
            at_side = place_ref[planes + 2] ^ ((turn >> 1) & 1)
            at_core = place_ref[planes + 1] ^ (turn >> 2)
            return 0, place_ref[s], at_row, at_core, at_side, 0, 0
        return 0, place_ref[s], at_row, place_ref[planes + 1] ^ (turn >> 1), 0, 0

    middle = (2,) if with_side else ()
    blank = (1,) if with_side else ()
    kind = pieces[0].dtype
    return pl.pallas_call(
        body,
        grid_spec=pltpu.PrefetchScalarGridSpec(
            num_scalar_prefetch=1,
            grid=(count, planes),
            in_specs=[
                pl.BlockSpec((1, held, part_rows, columns), source_map(k)) for k in range(count)
            ],
            out_specs=tuple(
                pl.BlockSpec((end - start, 1, 1, 1) + blank + (part_rows, columns), target_map)
                for start, end in cuts
            ),
        ),
        out_shape=tuple(
            jax.ShapeDtypeStruct(
                (end - start, planes, ROWS, CORES) + middle + (part_rows, columns), kind
            )
            for start, end in cuts
        ),
        cost_estimate=pl.CostEstimate(
            flops=0,
            bytes_accessed=4 * count * planes * held * part_rows * columns,
            transcendentals=0,
        ),
    )(place, *pieces)


def solution(mesh):
    dp, mp = mesh.shape["dp"], mesh.shape["mp"]
    planes = dp // (ROWS * CORES)

    def swap_x(value):
        return lax.ppermute(value, "mp", [(k, k ^ 1) for k in range(mp)])

    def swap_c(value):
        return lax.ppermute(value, "dp", [(k, k ^ 1) for k in range(dp)])

    def swap_y(value):
        return lax.ppermute(value, "dp", [(k, k ^ CORES) for k in range(dp)])

    def shift_z(value, step):
        inner = ROWS * CORES
        pairs = [(k, (k // inner + step) % planes * inner + k % inner) for k in range(dp)]
        return lax.ppermute(value, "dp", pairs)

    def shards(
        patches,
        time_bins,
        class_ids,
        encoder_feats,
        cotangent,
        w_qkv,
        w_out,
        w_up,
        w_down,
        w_ada,
        time_table,
        class_table,
        inner_bias,
        b_out,
        b_down,
        b_ada,
        w_first,
        w_second,
        w_third,
        b_first,
        b_second,
        b_third,
    ):
        f32 = jnp.float32
        bf16 = jnp.bfloat16
        image_count, seq_len, width = patches.shape
        me = lax.axis_index("dp")
        side = lax.axis_index("mp")
        core = lax.rem(me, CORES)
        row = lax.rem(me // CORES, ROWS)
        plane = me // (ROWS * CORES)
        place = jnp.stack(
            [lax.rem(plane - s + planes, planes) for s in range(planes)] + [row, core, side]
        ).astype(jnp.int32)

        def pick(values, index, axis=0):
            return lax.dynamic_index_in_dim(values, index, axis, keepdims=False)

        def both(own):
            other = swap_x(own)
            first = side == 0
            return jnp.stack((jnp.where(first, own, other), jnp.where(first, other, own)), axis=0)

        def gather(shard, following, with_side, cuts):
            held, part_rows, columns = shard.shape
            near = jnp.stack([shard] + [shift_z(shard, s) for s in range(1, planes)], axis=0)
            if following is not None:
                near, following = lax.optimization_barrier((near, following))
            pieces = [near, swap_y(near)]
            if with_side:
                pieces = pieces + [swap_x(piece) for piece in pieces]
            pieces = pieces + [swap_c(piece) for piece in pieces]
            placed = place_pieces(pieces, place, planes, with_side, cuts)
            total = dp * (mp if with_side else 1)
            full = [
                out.reshape(end - start, total * part_rows, columns)
                for out, (start, end) in zip(placed, cuts)
            ]
            return full, following

        def scatter(sums, with_side):
            columns = sums.shape[-1]
            middle = (mp,) if with_side else ()
            cut = sums.reshape((planes, ROWS, CORES) + middle + (-1, columns))
            from_core = swap_c(pick(cut, 1 - core, 2))
            mine = pick(cut, core, 2)
            terms = [mine, from_core]
            if with_side:
                outgoing = sum(pick(term, 1 - side, 2).astype(f32) for term in terms).astype(bf16)
                terms = [pick(term, side, 2) for term in terms] + [swap_x(outgoing)]
            outgoing = sum(pick(term, 1 - row, 1).astype(f32) for term in terms).astype(bf16)
            terms = [pick(term, row, 1) for term in terms] + [swap_y(outgoing)]

            def total(index):
                return sum(pick(term, index, 0).astype(f32) for term in terms)

            result = total(plane)
            for s in range(1, planes):
                outgoing = total(lax.rem(plane + s, planes)).astype(bf16)
                result = result + shift_z(outgoing, s).astype(f32)
            return result

        def gather_near(value, axis):
            value = jnp.concatenate(
                [value] + [shift_z(value, s) for s in range(1, planes)], axis=axis
            )
            value = jnp.concatenate((value, swap_y(value)), axis=axis)
            return jnp.concatenate((value, swap_c(value)), axis=axis)

        lanes = 128
        numbers = jnp.concatenate((time_bins, class_ids)).astype(f32)
        packed = jnp.concatenate(
            (
                jnp.pad(numbers, (0, lanes - numbers.shape[0])),
                inner_bias.reshape(-1),
                b_out,
                b_down,
                b_first,
                b_second,
                b_third,
            )
        ).reshape(1, -1)
        near_packed = gather_near(packed, 0)
        near_ids = near_packed[:, : 2 * image_count].astype(jnp.int32)
        near_bins = near_ids[:, :image_count].reshape(-1)
        near_labels = near_ids[:, image_count:].reshape(-1)
        order = jnp.arange(dp)
        distance = (
            (core ^ (order % CORES)) * ROWS + (row ^ (order // CORES % ROWS))
        ) * planes + (plane - order // (CORES * ROWS)) % planes
        spread = (distance[:, None] == order[None, :]).astype(bf16)
        biases = jnp.dot(
            spread, near_packed[:, lanes:].astype(bf16), preferred_element_type=f32
        )
        inner_size = inner_bias.shape[1]
        thin = b_out.shape[0]
        flat_inner = biases[:, :inner_size].reshape(-1)
        full_bout = biases[:, inner_size : inner_size + thin].reshape(-1)
        full_bdown = biases[:, inner_size + thin : inner_size + 2 * thin].reshape(-1)
        proj_biases = biases[:, inner_size + 2 * thin :].astype(bf16)
        proj_biases = jnp.moveaxis(both(proj_biases), 0, 1).astype(f32)
        hidden_size = b_first.shape[0]
        bias_one = proj_biases[:, :, :hidden_size].reshape(-1)
        bias_two = proj_biases[:, :, hidden_size : 2 * hidden_size].reshape(-1)
        bias_three = proj_biases[:, :, 2 * hidden_size :].reshape(-1)

        bin_onehot = near_bins[:, None] == jnp.arange(time_table.shape[0], dtype=jnp.int32)[None, :]
        class_onehot = (
            near_labels[:, None] == jnp.arange(class_table.shape[0], dtype=jnp.int32)[None, :]
        )
        condition = jnp.dot(
            bin_onehot.astype(bf16), time_table, preferred_element_type=f32
        ) + jnp.dot(class_onehot.astype(bf16), class_table, preferred_element_type=f32)
        cond_act = jax.nn.silu(condition).astype(bf16)
        local_rows = w_ada.shape[1]
        wide_bias = lax.dynamic_update_slice(
            jnp.zeros((b_ada.shape[0], width), f32), b_ada, (0, me * local_rows)
        )
        partial_mods = (
            jnp.einsum("bd,tde->tbe", cond_act, w_ada, preferred_element_type=f32)
            + wide_bias[:, None, :]
        ).astype(bf16)
        half = partial_mods.shape[1] // 2
        mods = partial_mods[:, :half].astype(f32) + swap_c(partial_mods[:, half:]).astype(f32)
        half = half // 2
        mods = mods[:, :half] + swap_y(mods[:, half:].astype(bf16)).astype(f32)
        modulation = mods[:, :image_count]
        for s in range(1, planes):
            start = (planes - s) * image_count
            outgoing = mods[:, start : start + image_count].astype(bf16)
            modulation = modulation + shift_z(outgoing, s).astype(f32)
        shift_one, scale_one, gate_one, shift_two, scale_two, gate_two = (
            modulation[t][:, None, :] for t in range(6)
        )
        scale_own = pick(scale_one, side)
        gate_one = pick(gate_one, side)
        shift_two = pick(shift_two, side)
        scale_two = pick(scale_two, side)
        gate_two = pick(gate_two, side)

        shard_attn = jnp.concatenate((w_qkv, w_out.T[None]), axis=0)
        shard_up = w_up[None]
        shard_down = w_down.T[None]
        shard_one = w_first.T[None]
        shard_two = w_second.T[None]
        shard_three = w_third.T[None]
        (full_qkv, full_out), shard_up = gather(shard_attn, shard_up, False, ((0, 3), (3, 4)))
        (full_up,), shard_down = gather(shard_up, shard_down, False, ((0, 1),))
        (full_down,), shard_one = gather(shard_down, shard_one, False, ((0, 1),))
        (proj_one,), shard_two = gather(shard_one, shard_two, True, ((0, 1),))
        (proj_two,), shard_three = gather(shard_two, shard_three, True, ((0, 1),))
        (proj_three,), _ = gather(shard_three, None, True, ((0, 1),))
        full_out, full_up, full_down = full_out[0], full_up[0], full_down[0]
        proj_one, proj_two, proj_three = proj_one[0], proj_two[0], proj_three[0]

        local_width = full_qkv.shape[2]
        head_count = local_width // HD
        bias_query = flat_inner[:local_width]
        bias_value = flat_inner[local_width : 2 * local_width]
        bias_units = flat_inner[2 * local_width :]
        score_scale = float(HD) ** (-0.5)

        inputs = patches.astype(f32)
        normed_one, inverse_one = layer_norm(inputs)
        act_one = (normed_one * (1.0 + scale_one) + shift_one).astype(bf16)
        qkv_proj = jnp.einsum("bld,tdc->tblc", act_one, full_qkv, preferred_element_type=f32)
        head_shape = (image_count, seq_len, head_count, HD)
        queries = (qkv_proj[0] + bias_query).astype(bf16).reshape(head_shape)
        key_heads = qkv_proj[1].astype(bf16).reshape(head_shape)
        val_heads = (qkv_proj[2] + bias_value).astype(bf16).reshape(head_shape)
        scores = (
            jnp.einsum("bqhd,bkhd->bhqk", queries, key_heads, preferred_element_type=f32)
            * score_scale
        )
        row_max = jnp.max(scores, axis=-1, keepdims=True)
        shifted = jnp.exp(scores - row_max)
        exp_total = jnp.sum(shifted, axis=-1, keepdims=True)
        log_total = row_max + jnp.log(exp_total)
        attn_probs = (shifted / exp_total).astype(bf16)
        mixed_heads = jnp.einsum(
            "bhqk,bkhd->bqhd", attn_probs, val_heads, preferred_element_type=f32
        )
        mixed_heads = mixed_heads.reshape(image_count, seq_len, local_width).astype(bf16)

        def shared(values, weights, contract):
            def part(image):
                return lax.dot_general(
                    pick(values, image),
                    weights,
                    (((1,), (contract,)), ((), ())),
                    preferred_element_type=f32,
                )

            arrived = swap_x(part(1 - side).astype(bf16))
            return part(side) + arrived.astype(f32)

        attention = shared(mixed_heads, full_out, 1) + full_bout
        first_sum = pick(inputs, side) + gate_one * attention
        normed_two, inverse_two = layer_norm(first_sum)
        act_two = both((normed_two * (1.0 + scale_two) + shift_two).astype(bf16))
        hidden = (
            jnp.einsum("bld,df->blf", act_two, full_up, preferred_element_type=f32) + bias_units
        )
        active = gelu_tanh(hidden).astype(bf16)
        branch = shared(active, full_down, 1) + full_bdown
        output = first_sum + gate_two * branch
        block_out = output.astype(bf16)

        target = pick(encoder_feats, side).astype(f32)

        def dot(left, right, left_axis, right_axis):
            return lax.dot_general(
                left, right, (((left_axis,), (right_axis,)), ((), ())), preferred_element_type=f32
            )

        pre_one = dot(block_out, proj_one, 1, 1) + bias_one
        act_pone = jax.nn.silu(pre_one).astype(bf16)
        pre_two = dot(act_pone, proj_two, 1, 1) + bias_two
        act_ptwo = jax.nn.silu(pre_two).astype(bf16)
        mapped = dot(act_ptwo, proj_three, 1, 1) + bias_three
        inv_map = lax.rsqrt(jnp.sum(mapped * mapped, axis=-1, keepdims=True) + epsilon)
        inv_target = lax.rsqrt(jnp.sum(target * target, axis=-1, keepdims=True) + epsilon)
        cosine = jnp.sum(mapped * target, axis=-1, keepdims=True) * inv_map * inv_target
        loss_weight = -0.5 * float(width)
        grad_mapped = (
            loss_weight * (target * inv_map * inv_target - cosine * inv_map * inv_map * mapped)
        ).astype(bf16)
        sum_wthird = scatter(dot(grad_mapped, act_ptwo, 0, 0).astype(bf16), True)
        grad_bthird = jnp.sum(grad_mapped.astype(f32), axis=0)
        grad_pre_two = (dot(grad_mapped, proj_three, 1, 0) * silu_grad(pre_two)).astype(bf16)
        sum_wsecond = scatter(dot(grad_pre_two, act_pone, 0, 0).astype(bf16), True)
        grad_bsecond = jnp.sum(grad_pre_two.astype(f32), axis=0)
        grad_pre_one = (dot(grad_pre_two, proj_two, 1, 0) * silu_grad(pre_one)).astype(bf16)
        sum_wfirst = scatter(dot(grad_pre_one, block_out, 0, 0).astype(bf16), True)
        grad_bfirst = jnp.sum(grad_pre_one.astype(f32), axis=0)
        grad_feed = dot(grad_pre_one, proj_one, 1, 0).astype(bf16)

        grad_output = pick(cotangent, side).astype(f32) + grad_feed.astype(f32)
        grad_branch = (gate_two * grad_output).astype(bf16)
        grad_gate_two = jnp.sum(grad_output * branch, axis=0)
        grad_bdown = jnp.sum(grad_branch.astype(f32), axis=0)
        grad_branch = both(grad_branch)
        tokens = image_count * seq_len
        grad_active = jnp.einsum("bld,df->blf", grad_branch, full_down, preferred_element_type=f32)
        grad_hidden = (grad_active * gelu_grad(hidden)).astype(bf16)
        grad_bunits = jnp.sum(grad_hidden.astype(f32), axis=(0, 1))

        def flat(values):
            return values.reshape(tokens, values.shape[-1])

        sum_down = scatter(dot(flat(grad_branch), flat(active), 0, 0).astype(bf16), False)
        grad_act_two = shared(grad_hidden, full_up, 1)
        sum_up = scatter(dot(flat(act_two), flat(grad_hidden), 0, 0).astype(bf16), False)
        grad_shift_two = jnp.sum(grad_act_two, axis=0)
        grad_scale_two = jnp.sum(grad_act_two * normed_two, axis=0)
        grad_first_sum = grad_output + norm_back(
            grad_act_two * (1.0 + scale_two), normed_two, inverse_two
        )

        grad_attention = (gate_one * grad_first_sum).astype(bf16)
        grad_gate_one = jnp.sum(grad_first_sum * attention, axis=0)
        grad_bout = jnp.sum(grad_attention.astype(f32), axis=0)
        grad_attention = both(grad_attention)
        sum_out = scatter(dot(flat(grad_attention), flat(mixed_heads), 0, 0).astype(bf16), False)
        grad_mixed = jnp.einsum("bld,dc->blc", grad_attention, full_out, preferred_element_type=f32)
        grad_mixed = grad_mixed.astype(bf16).reshape(head_shape)
        scores = (
            jnp.einsum("bqhd,bkhd->bhqk", queries, key_heads, preferred_element_type=f32)
            * score_scale
        )
        probs_again = jnp.exp(scores - log_total)
        grad_values = jnp.einsum(
            "bhqk,bqhd->bkhd", probs_again.astype(bf16), grad_mixed, preferred_element_type=f32
        )
        grad_probs = jnp.einsum(
            "bqhd,bkhd->bhqk", grad_mixed, val_heads, preferred_element_type=f32
        )
        inner_prod = jnp.sum(probs_again * grad_probs, axis=-1, keepdims=True)
        grad_scores = (probs_again * (grad_probs - inner_prod)).astype(bf16)
        grad_queries = (
            jnp.einsum("bhqk,bkhd->bqhd", grad_scores, key_heads, preferred_element_type=f32)
            * score_scale
        )
        grad_keys = (
            jnp.einsum("bhqk,bqhd->bkhd", grad_scores, queries, preferred_element_type=f32)
            * score_scale
        )
        grad_three = [
            grad.reshape(image_count, seq_len, local_width).astype(bf16)
            for grad in (grad_queries, grad_keys, grad_values)
        ]
        grad_bquery = jnp.sum(grad_three[0].astype(f32), axis=(0, 1))
        grad_bvalue = jnp.sum(grad_three[2].astype(f32), axis=(0, 1))
        grad_wide = jnp.concatenate(grad_three, axis=-1)

        def part_one(image):
            picked = pick(grad_wide, image)
            return sum(
                dot(
                    picked[:, t * local_width : (t + 1) * local_width], full_qkv[t], 1, 1
                )
                for t in range(3)
            )

        arrived = swap_x(part_one(1 - side).astype(bf16))
        grad_act_one = part_one(side) + arrived.astype(f32)
        sum_qkv = scatter(dot(flat(act_one), flat(grad_wide), 0, 0).astype(bf16), False)
        sum_qkv = jnp.stack(
            [sum_qkv[:, t * local_width : (t + 1) * local_width] for t in range(3)], axis=0
        )
        normed_own, inverse_own = pick(normed_one, side), pick(inverse_one, side)
        grad_shift_one = jnp.sum(grad_act_one, axis=0)
        grad_scale_one = jnp.sum(grad_act_one * normed_own, axis=0)
        grad_own = grad_first_sum + norm_back(
            grad_act_one * (1.0 + scale_own), normed_own, inverse_own
        )
        grad_other = swap_x(grad_own.astype(bf16)).astype(f32)
        grad_patches = jnp.stack(
            (
                jnp.where(side == 0, grad_own, grad_other),
                jnp.where(side == 0, grad_other, grad_own),
            ),
            axis=0,
        )

        grad_mods = jnp.stack(
            (
                grad_shift_one,
                grad_scale_one,
                grad_gate_one,
                grad_shift_two,
                grad_scale_two,
                grad_gate_two,
            ),
            axis=0,
        ).astype(bf16)
        near_mods = gather_near(jnp.moveaxis(both(grad_mods), 0, 1), 1)
        mods_total = jnp.sum(near_mods.astype(f32), axis=1)
        sum_bada = lax.dynamic_slice_in_dim(mods_total, me * local_rows, local_rows, 1)
        sum_wada = jnp.einsum("bd,tbe->tde", cond_act, near_mods, preferred_element_type=f32)
        grad_cond = jnp.einsum("tbe,tde->bd", near_mods, w_ada, preferred_element_type=f32)
        grad_cond = grad_cond * silu_grad(condition)
        sum_time = jnp.einsum(
            "bn,bd->nd", bin_onehot.astype(f32), grad_cond, precision=lax.Precision.HIGHEST
        )
        sum_class = jnp.einsum(
            "bn,bd->nd", class_onehot.astype(f32), grad_cond, precision=lax.Precision.HIGHEST
        )

        own_sums = jnp.concatenate(
            (grad_bout, grad_bdown, grad_bfirst, grad_bsecond, grad_bthird)
        )
        own_sums = own_sums + swap_x(own_sums)
        sizes = [thin * dp, thin * dp, grad_bfirst.size, grad_bsecond.size, grad_bthird.size]
        rows_of = []
        start = 0
        for k, size in enumerate(sizes):
            piece = own_sums[start : start + size]
            start += size
            if k < 2:
                rows_of.append(piece.reshape(dp, -1))
            else:
                rows_of.append(pick(piece.reshape(dp, mp, -1), side, 1))
        grad_inner = jnp.concatenate((grad_bquery, grad_bvalue, grad_bunits))
        sums = jnp.concatenate([grad_inner.reshape(dp, -1)] + rows_of, axis=1)
        sums = sums.reshape(planes, ROWS, CORES, 1, -1)
        sums = pick(sums, core, 2) + swap_c(pick(sums, 1 - core, 2))
        sums = pick(sums, row, 1) + swap_y(pick(sums, 1 - row, 1))
        total = pick(sums, plane, 0)
        for s in range(1, planes):
            total = total + shift_z(pick(sums, lax.rem(plane + s, planes), 0), s)
        pieces = []
        start = 0
        for size in (inner_size, thin, thin, hidden_size, hidden_size, b_third.shape[0]):
            pieces.append(total[:, start : start + size])
            start += size
        return (
            both(block_out),
            grad_patches,
            sum_qkv,
            sum_out.T,
            sum_up,
            sum_down.T,
            sum_wada,
            sum_time,
            sum_class,
            pieces[0],
            pieces[1][0],
            pieces[2][0],
            sum_bada,
            sum_wfirst.T,
            sum_wsecond.T,
            sum_wthird.T,
            pieces[3][0],
            pieces[4][0],
            pieces[5][0],
        )

    placed = (
        P("dp", None, None),
        P("dp"),
        P("dp"),
        P("dp", None, None),
        P("dp", None, None),
        P(None, "dp", "mp"),
        P("mp", "dp"),
        P("dp", "mp"),
        P("mp", "dp"),
        P(None, "dp", None),
        P(None, "dp"),
        P(None, "dp"),
        P("mp", "dp"),
        P("dp"),
        P("dp"),
        P(None, "dp"),
        P(None, ("dp", "mp")),
        P(None, ("dp", "mp")),
        P(None, ("dp", "mp")),
        P(("dp", "mp")),
        P(("dp", "mp")),
        P(("dp", "mp")),
    )
    return jax.shard_map(
        shards,
        mesh=mesh,
        in_specs=placed,
        out_specs=(
            P("dp", None, None),
            P("dp", None, None),
            P(None, "dp", "mp"),
            P("mp", "dp"),
            P("dp", "mp"),
            P("mp", "dp"),
            P(None, "dp", None),
            P(None, "dp"),
            P(None, "dp"),
            P("mp", "dp"),
            P("dp"),
            P("dp"),
            P(None, "dp"),
            P(None, ("dp", "mp")),
            P(None, ("dp", "mp")),
            P(None, ("dp", "mp")),
            P(("dp", "mp")),
            P(("dp", "mp")),
            P(("dp", "mp")),
        ),
        check_vma=False,
    )
```

time: 1990 us -> 790 us (0.40)
  waiting for transfers between devices: 1510 us -> 336 us
  blocking collectives: 254 us -> 0 us
  starting transfers between devices: 2.28 us -> 122 us
  Pallas kernels: 0 us -> 107 us
  matrix products: 133 us -> 91.2 us
  other arithmetic: 30.7 us -> 70.6 us
    reduce_scatter x9 -> x0, waiting for transfers between devices: 955 us -> none  [the longest x1 360 us: shards(): lax.psum_scatter(grad_wsecond, ('dp', 'mp'), scatter_dimension=1, tiled=T...]
    all_gather x12 -> x0, waiting for transfers between devices: 428 us -> none  [the longest x1 73.8 us: shards(): lax.all_gather(w_second, ('dp', 'mp'), axis=1, tiled=True)]
    ppermute x0 -> x118, waiting for transfers between devices: none -> 336 us  [the longest x51 177 us: shift_z(): return lax.ppermute(value, 'dp', pairs)]
    unnamed x5 -> x0, blocking collectives: 214 us -> none
    unnamed x27 -> x0, waiting for transfers between devices: 123 us -> none
    ppermute x0 -> x118, starting transfers between devices: none -> 122 us  [the longest x51 74.4 us: shift_z(): return lax.ppermute(value, 'dp', pairs)]
    pallas_call x0 -> x6, Pallas kernels: none -> 107 us  [place_pieces(): pl.pallas_call(body, grid_spec=pltpu.PrefetchScalarGridSpec(num_scalar_pr...]
    dot_general x24 -> x33, matrix products: 112 us -> 69.1 us  [the longest x19 39.9 us: dot(): lax.dot_general(left, right, (((left_axis,), (right_axis,)), ((), ())), p...]
  transfers between devices with their start and end apart: 24 -> 118, of which waited for: 22 -> 50; matrix products, arithmetic and copies ran while one was open for 6% -> 24% of each run, Pallas kernels for 0% -> 14%
where the time goes in v1:
time: 790 us; the launch traced here: 781 us
  waiting for transfers between devices  336 us (43%)
  starting transfers between devices  122 us (15%)
  Pallas kernels  107 us (14%)
  matrix products  91.2 us (12%)
  other arithmetic  70.6 us (9%)
  local copies, waits for them, and re-layouts  51.9 us (7%)
    ppermute x51, waiting for transfers between devices, shift_z(): return lax.ppermute(value, 'dp', pairs)  177 us
    pallas_call x6, Pallas kernels, place_pieces(): pl.pallas_call(body, grid_spec=pltpu.PrefetchScalarGridSpec(num_scalar_pr...  107 us
    ppermute x17, waiting for transfers between devices, swap_y(): return lax.ppermute(value, 'dp', [(k, k ^ CORES) for k in range(dp)])  90.5 us
    ppermute x51, starting transfers between devices, shift_z(): return lax.ppermute(value, 'dp', pairs)  74.4 us
    ppermute x21, waiting for transfers between devices, swap_x(): return lax.ppermute(value, 'mp', [(k, k ^ 1) for k in range(mp)])  67.9 us
    dot_general x19, matrix products, dot(): lax.dot_general(left, right, (((left_axis,), (right_axis,)), ((), ())), p...  39.9 us
    ppermute x21, starting transfers between devices, swap_x(): return lax.ppermute(value, 'mp', [(k, k ^ 1) for k in range(mp)])  26.6 us
    dot_general x6, matrix products, part(): lax.dot_general(pick(values, image), weights, (((1,), (contract,)), ((),...  16.4 us
  transfers between devices with their start and end apart: 118, of which 50 were waited for; matrix products, arithmetic and copies ran while one was open for 24% of the time, Pallas kernels for 14%

profile of v1, /device:TPU:0, one launch (start us, length us, event | category | flops | bytes accessed | tf_op | source)
XLA Modules:
  0.0 781.5 jit_solution(7542651385967209740)
XLA Ops:
  24.5 20.3 %collective-permute-done.11 = bf16[4,72,576]{2,1,0:T(8,128)(2,1)} collective-permute-done((bf16[4,72,576]{2,1,0:T(8,128)(2,1)}, bf16[4,72,576]{2,1,0:T(8,128)(2,1)}, u32[]{:S(2)}, u32[]{:S(2)}) %collective-permute-start.11) | collective-permute-done | bytes 331808 | tf_op jit(solution)/shard_map/ppermute | solution.py:123
  54.7 22.2 %collective-permute-done.19 = bf16[1,72,2304]{2,1,0:T(8,128)(2,1)S(1)} collective-permute-done((bf16[1,72,2304]{2,1,0:T(8,128)(2,1)S(1)}, bf16[1,72,2304]{2,1,0:T(8,128)(2,1)S(1)}, u32[]{:S(2)}, u32[]{:S(2)}) %collective-permute-start.19) | collective-permute-done | bytes 331808 | tf_op jit(solution)/shard_map/ppermute | solution.py:123
  79.3 8.4 %collective-permute-done.26 = bf16[1,72,2304]{2,1,0:T(8,128)(2,1)S(1)} collective-permute-done((bf16[1,72,2304]{2,1,0:T(8,128)(2,1)S(1)}, bf16[1,72,2304]{2,1,0:T(8,128)(2,1)S(1)}, u32[]{:S(2)}, u32[]{:S(2)}) %collective-permute-start.26) | collective-permute-done | bytes 331808 | tf_op jit(solution)/shard_map/ppermute | solution.py:123
  87.7 18.6 %collective-permute-done.25 = bf16[1,72,2304]{2,1,0:T(8,128)(2,1)S(1)} collective-permute-done((bf16[1,72,2304]{2,1,0:T(8,128)(2,1)S(1)}, bf16[1,72,2304]{2,1,0:T(8,128)(2,1)S(1)}, u32[]{:S(2)}, u32[]{:S(2)}) %collective-permute-start.25) | collective-permute-done | bytes 331808 | tf_op jit(solution)/shard_map/ppermute | solution.py:123
  115.9 8.7 %collective-permute-done.33 = bf16[1,64,1152]{2,1,0:T(8,128)(2,1)S(1)} collective-permute-done((bf16[1,64,1152]{2,1,0:T(8,128)(2,1)S(1)}, bf16[1,64,1152]{2,1,0:T(8,128)(2,1)S(1)}, u32[]{:S(2)}, u32[]{:S(2)}) %collective-permute-start.33) | collective-permute-done | bytes 147488 | tf_op jit(solution)/shard_map/ppermute | solution.py:123
  125.5 3.8 collective-permute-start.45
  130.7 5.5 collective-permute-done.45
  136.2 16.0 %collective-permute-done.44 = bf16[1,64,2048]{2,1,0:T(8,128)(2,1)S(1)} collective-permute-done((bf16[1,64,2048]{2,1,0:T(8,128)(2,1)S(1)}, bf16[1,64,2048]{2,1,0:T(8,128)(2,1)S(1)}, u32[]{:S(2)}, u32[]{:S(2)}) %collective-permute-start.44) | collective-permute-done | bytes 262176 | tf_op jit(solution)/shard_map/ppermute | solution.py:123
  159.8 3.9 collective-permute-done.54
  169.2 23.7 %shard_map.357 = (bf16[3,4,2,2,72,576]{5,4,3,2,1,0:T(8,128)(2,1)}, bf16[1,4,2,2,72,576]{5,4,3,2,1,0:T(8,128)(2,1)}) custom-call(s32[7]{0:T(128)} %stack.224.place_ref, bf16[4,4,72,576]{3,2,1,0:T(8,128)(2,1)} %copy-done.17, bf16[4,4,72,576]{3,2,1,0:T(8,128)(2,1)} %copy-done.31, bf16[4,4,72,576]{3,2,1,0:T(8,128)(2,1)} %copy-done.32, ...), custom_call_target="tpu_custom_call" | custom-call | bytes 10616832 | tf_op jit(solution)/shard_map/pallas_call | solution.py:80
  192.9 5.3 convolution_bitcast_fusion.5
  199.2 4.6 collective-permute-done.35.refs_1_
  229.6 14.3 %collective-permute-done.27.refs_1_ = bf16[4,1,72,2304]{3,2,1,0:T(8,128)(2,1)} collective-permute-done((bf16[4,1,72,2304]{3,2,1,0:T(8,128)(2,1)}, bf16[4,1,72,2304]{3,2,1,0:T(8,128)(2,1)}, u32[]{:S(2)}, u32[]{:S(2)}) %collective-permute-start.27) | collective-permute-done | bytes 1327136 | tf_op jit(solution)/shard_map/ppermute | solution.py:118
  243.9 6.2 collective-permute-done.16
  251.0 3.8 fusion.187
  255.8 7.5 collective-permute-done.46.refs_1_
  272.3 18.2 %shard_map.362 = bf16[1,4,2,2,2,24,2048]{6,5,4,3,2,1,0:T(8,128)(2,1)} custom-call(s32[7]{0:T(128)} %stack.224.place_ref, bf16[4,1,24,2048]{3,2,1,0:T(8,128)(2,1)} %pad_maximum_fusion.18.refs_0_, bf16[4,1,24,2048]{3,2,1,0:T(8,128)(2,1)} %copy-done.46, bf16[4,1,24,2048]{3,2,1,0:T(8,128)(2,1)} %copy-done.47, bf16[4,1,24,2048]{3,2,1,0:T(8,128)(2,1)} %copy-done.49, ...), custom_call_target="tpu_custom_call" | custom-call | bytes 6291456 | tf_op jit(solution)/shard_map/pallas_call | solution.py:80
  290.5 19.6 %shard_map.360 = bf16[1,4,2,2,2,64,1152]{6,5,4,3,2,1,0:T(8,128)(2,1)} custom-call(s32[7]{0:T(128)} %stack.224.place_ref, bf16[4,1,64,1152]{3,2,1,0:T(8,128)(2,1)} %pad_maximum_fusion.16.refs_0_, bf16[4,1,64,1152]{3,2,1,0:T(8,128)(2,1)} %collective-permute-done.35.refs_1_, bf16[4,1,64,1152]{3,2,1,0:T(8,128)(2,1)} %collective-permute-done.36.refs_2_, ...), custom_call_target="tpu_custom_call" | custom-call | bytes 9437184 | tf_op jit(solution)/shard_map/pallas_call | solution.py:80
  310.1 11.9 %shard_map.358 = bf16[1,4,2,2,72,2304]{5,4,3,2,1,0:T(8,128)(2,1)} custom-call(s32[7]{0:T(128)} %stack.224.place_ref, bf16[4,1,72,2304]{3,2,1,0:T(8,128)(2,1)} %copy-done.22, bf16[4,1,72,2304]{3,2,1,0:T(8,128)(2,1)} %collective-permute-done.21.refs_1_, bf16[4,1,72,2304]{3,2,1,0:T(8,128)(2,1)} %copy-done.34, ...), custom_call_target="tpu_custom_call" | custom-call | bytes 10616832 | tf_op jit(solution)/shard_map/pallas_call | solution.py:80
  323.1 12.0 %shard_map.359 = bf16[1,4,2,2,72,2304]{5,4,3,2,1,0:T(8,128)(2,1)} custom-call(s32[7]{0:T(128)} %stack.224.place_ref, bf16[4,1,72,2304]{3,2,1,0:T(8,128)(2,1)} %pad_maximum_fusion.4.refs_0_, bf16[4,1,72,2304]{3,2,1,0:T(8,128)(2,1)} %collective-permute-done.27.refs_1_, bf16[4,1,72,2304]{3,2,1,0:T(8,128)(2,1)} %collective-permute-done.28.refs_2_, ...), custom_call_target="tpu_custom_call" | custom-call | bytes 10616832 | tf_op jit(solution)/shard_map/pallas_call | solution.py:80
  336.8 8.5 %multiply_convert_fusion = (bf16[2,256,2304]{2,1,0:T(8,128)(2,1)S(1)}, f32[2,256,2304]{2,1,0:T(8,128)}) fusion(f32[2304]{0:T(1024)S(1)} %copy-done.83, bf16[1152,2304,1]{1,0,2:T(8,128)(2,1)} %bitcast.764, bf16[1,256,1152]{2,1,0:T(8,128)(2,1)S(1)} %get-tuple-element.106, bf16[1,256,1152]{2,1,0:T(8,128)(2,1)S(1)} %get-tuple-element.105), kind=kOutput, calls=%fused_computation.18 | convolution fusion | flops 2730295296 | bytes 13575168 | tf_op jit(solution)/shard_map/bld,df->blf/dot_general | solution.py:347
  351.0 21.1 %shard_map.361 = bf16[1,4,2,2,2,64,2048]{6,5,4,3,2,1,0:T(8,128)(2,1)} custom-call(s32[7]{0:T(128)} %stack.224.place_ref, bf16[4,1,64,2048]{3,2,1,0:T(8,128)(2,1)} %pad_maximum_fusion.9.refs_0_, bf16[4,1,64,2048]{3,2,1,0:T(8,128)(2,1)} %collective-permute-done.46.refs_1_, bf16[4,1,64,2048]{3,2,1,0:T(8,128)(2,1)} %collective-permute-done.47.refs_2_, ...), custom_call_target="tpu_custom_call" | custom-call | bytes 16777216 | tf_op jit(solution)/shard_map/pallas_call | solution.py:80
  372.1 4.8 add_convert_fusion.1
  378.2 4.1 convolution_add_fusion.10
  405.9 7.8 %collective-permute-done.63 = bf16[256,1152]{1,0:T(8,128)(2,1)S(1)} collective-permute-done((bf16[256,1152]{1,0:T(8,128)(2,1)S(1)}, bf16[256,1152]{1,0:T(8,128)(2,1)S(1)}, u32[]{:S(2)}, u32[]{:S(2)}) %collective-permute-start.63) | collective-permute-done | bytes 589856 | tf_op jit(solution)/shard_map/ppermute | solution.py:112
  413.9 3.5 fusion.1
  417.5 8.7 %convert_reduce_fusion = (f32[2304]{0:T(1024)S(1)}, bf16[2,256,2304]{2,1,0:T(8,128)(2,1)S(1)}) fusion(f32[2,256,2304]{2,1,0:T(8,128)} %get-tuple-element.152, bf16[1152,2304,1]{1,0,2:T(8,128)(2,1)S(1)} %bitcast.775, bf16[1,256,1152]{2,1,0:T(8,128)(2,1)S(1)} %get-tuple-element.102, bf16[1,256,1152]{2,1,0:T(8,128)(2,1)S(1)} %get-tuple-element.101), kind=kOutput, calls=%fused_computation.17 | convolution fusion | flops 2743269120 | bytes 13575168 | tf_op jit(solution)/shard_map/bld,df->blf/dot_general | solution.py:389
  426.3 3.7 fusion
  436.2 9.4 %collective-permute-done.64 = bf16[256,1152]{1,0:T(8,128)(2,1)S(1)} collective-permute-done((bf16[256,1152]{1,0:T(8,128)(2,1)S(1)}, bf16[256,1152]{1,0:T(8,128)(2,1)S(1)}, u32[]{:S(2)}, u32[]{:S(2)}) %collective-permute-start.64) | collective-permute-done | bytes 589856 | tf_op jit(solution)/shard_map/ppermute | solution.py:112
  457.2 7.9 %collective-permute-done.65 = bf16[256,1152]{1,0:T(8,128)(2,1)S(1)} collective-permute-done((bf16[256,1152]{1,0:T(8,128)(2,1)}, bf16[256,1152]{1,0:T(8,128)(2,1)S(1)}, u32[]{:S(2)}, u32[]{:S(2)}) %collective-permute-start.65) | collective-permute-done | bytes 589856 | tf_op jit(solution)/shard_map/ppermute | solution.py:112
  475.8 4.6 fusion.2
  488.1 6.4 copy.109
  504.8 7.1 collective-permute-start.99
  524.4 10.1 %collective-permute-done.88 = bf16[6,1152]{1,0:T(8,128)(2,1)S(1)} collective-permute-done((bf16[6,1152]{1,0:T(8,128)(2,1)S(1)}, bf16[6,1152]{1,0:T(8,128)(2,1)S(1)}, u32[]{:S(2)}, u32[]{:S(2)}) %collective-permute-start.88) | collective-permute-done | bytes 13856 | tf_op jit(solution)/shard_map/ppermute | solution.py:112
  561.7 8.5 %collective-permute-done.74 = bf16[4,72,576]{2,1,0:T(8,128)(2,1)} collective-permute-done((bf16[4,72,576]{2,1,0:T(8,128)(2,1)}, bf16[4,72,576]{2,1,0:T(8,128)(2,1)}, u32[]{:S(2)}, u32[]{:S(2)}) %collective-permute-start.74) | collective-permute-done | bytes 331808 | tf_op jit(solution)/shard_map/ppermute | solution.py:118
  571.4 3.3 collective-permute-start.77
  593.8 4.6 collective-permute-done.115
  606.1 22.7 %collective-permute-done.101 = bf16[4,2,64,1152]{3,2,1,0:T(8,128)(2,1)S(1)} collective-permute-done((bf16[4,2,64,1152]{3,2,1,0:T(8,128)(2,1)}, bf16[4,2,64,1152]{3,2,1,0:T(8,128)(2,1)S(1)}, u32[]{:S(2)}, u32[]{:S(2)}) %collective-permute-start.101) | collective-permute-done | bytes 1179680 | tf_op jit(solution)/shard_map/ppermute | solution.py:112
  634.6 15.7 %collective-permute-done.102 = bf16[4,64,1152]{2,1,0:T(8,128)(2,1)S(1)} collective-permute-done((bf16[4,64,1152]{2,1,0:T(8,128)(2,1)S(1)}, bf16[4,64,1152]{2,1,0:T(8,128)(2,1)S(1)}, u32[]{:S(2)}, u32[]{:S(2)}) %collective-permute-start.102) | collective-permute-done | bytes 589856 | tf_op jit(solution)/shard_map/ppermute | solution.py:118
  658.1 7.1 collective-permute-done.104
  670.6 8.1 %collective-permute-done.84 = bf16[4,72,2304]{2,1,0:T(8,128)(2,1)S(1)} collective-permute-done((bf16[4,72,2304]{2,1,0:T(8,128)(2,1)S(1)}, bf16[4,72,2304]{2,1,0:T(8,128)(2,1)S(1)}, u32[]{:S(2)}, u32[]{:S(2)}) %collective-permute-start.84) | collective-permute-done | bytes 1327136 | tf_op jit(solution)/shard_map/ppermute | solution.py:118
  680.4 19.8 %collective-permute-done.69 = bf16[4,72,1728]{2,1,0:T(8,128)(2,1)S(1)} collective-permute-done((bf16[4,72,1728]{2,1,0:T(8,128)(2,1)S(1)}, bf16[4,72,1728]{2,1,0:T(8,128)(2,1)S(1)}, u32[]{:S(2)}, u32[]{:S(2)}) %collective-permute-start.69) | collective-permute-done | bytes 995360 | tf_op jit(solution)/shard_map/ppermute | solution.py:118
  712.2 9.9 %collective-permute-start.70 = (bf16[72,1728]{1,0:T(8,128)(2,1)S(1)}, bf16[72,1728]{1,0:T(8,128)(2,1)S(1)}, u32[]{:S(2)}, u32[]{:S(2)}) collective-permute-start(bf16[72,1728]{1,0:T(8,128)(2,1)S(1)} %get-tuple-element.79), channel_id=1, source_target_pairs={{0,8},{2,10},{4,12},{6,14},{8,16},{10,18},{12,20},{14,22},{16,24},... | collective-permute-start | bytes 746504 | tf_op jit(solution)/shard_map/ppermute | solution.py:123
  722.1 19.0 %collective-permute-done.86 = bf16[72,2304]{1,0:T(8,128)(2,1)S(1)} collective-permute-done((bf16[72,2304]{1,0:T(8,128)(2,1)S(1)}, bf16[72,2304]{1,0:T(8,128)(2,1)S(1)}, u32[]{:S(2)}, u32[]{:S(2)}) %collective-permute-start.86) | collective-permute-done | bytes 331808 | tf_op jit(solution)/shard_map/ppermute | solution.py:123
  743.5 7.0 collective-permute-done.71
  750.7 5.2 collective-permute-done.108
  760.5 4.4 collective-permute-done.111
  764.9 14.3 %collective-permute-done.110 = bf16[64,2048]{1,0:T(8,128)(2,1)S(1)} collective-permute-done((bf16[64,2048]{1,0:T(8,128)(2,1)S(1)}, bf16[64,2048]{1,0:T(8,128)(2,1)S(1)}, u32[]{:S(2)}, u32[]{:S(2)}) %collective-permute-start.110) | collective-permute-done | bytes 262176 | tf_op jit(solution)/shard_map/ppermute | solution.py:123
  (641 shorter events, 286.3 us)
Async XLA Ops:
  11.7 33.2 %collective-permute-start.11 = (bf16[4,72,576]{2,1,0:T(8,128)(2,1)}, bf16[4,72,576]{2,1,0:T(8,128)(2,1)}, u32[]{:S(2)}, u32[]{:S(2)}) collective-permute-start(bf16[4,72,576]{2,1,0:T(8,128)(2,1)} %get-tuple-element.111), channel_id=1, source_target_pairs={{0,16},{2,18},{4,20},{6,22},{8,24},{10,26},{12,28},{14,30},{16,0},... | collective-permute-start | bytes 995336 | tf_op jit(solution)/shard_map/ppermute | solution.py:123
  15.4 29.5 %collective-permute-start.10 = (bf16[4,72,576]{2,1,0:T(8,128)(2,1)}, bf16[4,72,576]{2,1,0:T(8,128)(2,1)}, u32[]{:S(2)}, u32[]{:S(2)}) collective-permute-start(bf16[4,72,576]{2,1,0:T(8,128)(2,1)} %get-tuple-element.111), channel_id=1, source_target_pairs={{0,8},{2,10},{4,12},{6,14},{8,16},{10,18},{12,20},{14,22},{16,24},... | collective-permute-start | bytes 995336 | tf_op jit(solution)/shard_map/ppermute | solution.py:123
  46.4 30.6 %collective-permute-start.19 = (bf16[1,72,2304]{2,1,0:T(8,128)(2,1)S(1)}, bf16[1,72,2304]{2,1,0:T(8,128)(2,1)S(1)}, u32[]{:S(2)}, u32[]{:S(2)}) collective-permute-start(bf16[1,72,2304]{2,1,0:T(8,128)(2,1)S(1)} %bitcast.805), channel_id=1, source_target_pairs={{0,16},{2,18},{4,20},{6,22},{8,24},{10,26},{12,28},{14,30},{16,0},... | collective-permute-start | bytes 995336 | tf_op jit(solution)/shard_map/ppermute | solution.py:123
  47.7 29.2 %collective-permute-start.18 = (bf16[1,72,2304]{2,1,0:T(8,128)(2,1)S(1)}, bf16[1,72,2304]{2,1,0:T(8,128)(2,1)S(1)}, u32[]{:S(2)}, u32[]{:S(2)}) collective-permute-start(bf16[1,72,2304]{2,1,0:T(8,128)(2,1)S(1)} %bitcast.806), channel_id=1, source_target_pairs={{0,8},{2,10},{4,12},{6,14},{8,16},{10,18},{12,20},{14,22},{16,24},... | collective-permute-start | bytes 995336 | tf_op jit(solution)/shard_map/ppermute | solution.py:123
  52.3 78.3 %collective-permute-start.13 = (bf16[4,4,72,576]{3,2,1,0:T(8,128)(2,1)S(1)}, bf16[4,4,72,576]{3,2,1,0:T(8,128)(2,1)S(1)}, u32[]{:S(2)}, u32[]{:S(2)}) collective-permute-start(bf16[4,4,72,576]{3,2,1,0:T(8,128)(2,1)S(1)} %pad_maximum_fusion.2.refs_0_), channel_id=1, source_target_pairs={{0,4},{2,6},{4,0},{6,2},{8,12},{10,14},{12,8},{14,10},{16,20},{18,... | collective-permute-start | bytes 3981320 | tf_op jit(solution)/shard_map/ppermute | solution.py:118
  54.7 111.8 %collective-permute-start.14 = (bf16[4,4,72,576]{3,2,1,0:T(8,128)(2,1)S(1)}, bf16[4,4,72,576]{3,2,1,0:T(8,128)(2,1)S(1)}, u32[]{:S(2)}, u32[]{:S(2)}) collective-permute-start(bf16[4,4,72,576]{3,2,1,0:T(8,128)(2,1)S(1)} %pad_maximum_fusion.2.refs_0_), channel_id=1, source_target_pairs={{0,2},{2,0},{4,6},{6,4},{8,10},{10,8},{12,14},{14,12},{16,18},{18,... | collective-permute-start | bytes 3981320 | tf_op jit(solution)/shard_map/ppermute | solution.py:115
  77.2 29.0 %collective-permute-start.25 = (bf16[1,72,2304]{2,1,0:T(8,128)(2,1)S(1)}, bf16[1,72,2304]{2,1,0:T(8,128)(2,1)S(1)}, u32[]{:S(2)}, u32[]{:S(2)}) collective-permute-start(bf16[1,72,2304]{2,1,0:T(8,128)(2,1)S(1)} %bitcast.809), channel_id=1, source_target_pairs={{0,16},{2,18},{4,20},{6,22},{8,24},{10,26},{12,28},{14,30},{16,0},... | collective-permute-start | bytes 995336 | tf_op jit(solution)/shard_map/ppermute | solution.py:123
  77.3 29.0 %collective-permute-start.24 = (bf16[1,72,2304]{2,1,0:T(8,128)(2,1)S(1)}, bf16[1,72,2304]{2,1,0:T(8,128)(2,1)S(1)}, u32[]{:S(2)}, u32[]{:S(2)}) collective-permute-start(bf16[1,72,2304]{2,1,0:T(8,128)(2,1)S(1)} %bitcast.810), channel_id=1, source_target_pairs={{0,8},{2,10},{4,12},{6,14},{8,16},{10,18},{12,20},{14,22},{16,24},... | collective-permute-start | bytes 995336 | tf_op jit(solution)/shard_map/ppermute | solution.py:123
  130.6 37.5 %collective-permute-start.15 = (bf16[4,4,72,576]{3,2,1,0:T(8,128)(2,1)S(1)}, bf16[4,4,72,576]{3,2,1,0:T(8,128)(2,1)S(1)}, u32[]{:S(2)}, u32[]{:S(2)}) collective-permute-start(bf16[4,4,72,576]{3,2,1,0:T(8,128)(2,1)S(1)} %collective-permute-done.13.refs_1_), channel_id=1, source_target_pairs={{0,2},{2,0},{4,6},{6,4},{8,10},{10,8},{12,14},{14,12},{16,18},{18,... | collective-permute-start | bytes 3981320 | tf_op jit(solution)/shard_map/ppermute | solution.py:115
  158.3 40.2 %collective-permute-start.42 = (bf16[16,152]{1,0:T(8,128)(2,1)S(1)}, bf16[16,152]{1,0:T(8,128)(2,1)}, u32[]{:S(2)}, u32[]{:S(2)}) collective-permute-start(bf16[16,152]{1,0:T(8,128)(2,1)S(1)} %slice.344), channel_id=1, source_target_pairs={{0,1},{1,0},{2,3},{3,2},{4,5},{5,4},{6,7},{7,6},{8,9},{9,8},{10,11... | collective-permute-start | bytes 14600 | tf_op jit(solution)/shard_map/ppermute | solution.py:112
  163.7 53.7 %collective-permute-start.21 = (bf16[4,1,72,2304]{3,2,1,0:T(8,128)(2,1)S(1)}, bf16[4,1,72,2304]{3,2,1,0:T(8,128)(2,1)}, u32[]{:S(2)}, u32[]{:S(2)}) collective-permute-start(bf16[4,1,72,2304]{3,2,1,0:T(8,128)(2,1)S(1)} %pad_maximum_fusion.3.refs_0_), channel_id=1, source_target_pairs={{0,4},{2,6},{4,0},{6,2},{8,12},{10,14},{12,8},{14,10},{16,20},{18,... | collective-permute-start | bytes 3981320 | tf_op jit(solution)/shard_map/ppermute | solution.py:118
  165.2 38.6 %collective-permute-start.35 = (bf16[4,1,64,1152]{3,2,1,0:T(8,128)(2,1)}, bf16[4,1,64,1152]{3,2,1,0:T(8,128)(2,1)}, u32[]{:S(2)}, u32[]{:S(2)}) collective-permute-start(bf16[4,1,64,1152]{3,2,1,0:T(8,128)(2,1)} %pad_maximum_fusion.16.refs_0_), channel_id=1, source_target_pairs={{0,4},{2,6},{4,0},{6,2},{8,12},{10,14},{12,8},{14,10},{16,20},{18,... | collective-permute-start | bytes 1769480 | tf_op jit(solution)/shard_map/ppermute | solution.py:118
  166.5 38.8 %collective-permute-start.36 = (bf16[4,1,64,1152]{3,2,1,0:T(8,128)(2,1)}, bf16[4,1,64,1152]{3,2,1,0:T(8,128)(2,1)}, u32[]{:S(2)}, u32[]{:S(2)}) collective-permute-start(bf16[4,1,64,1152]{3,2,1,0:T(8,128)(2,1)} %pad_maximum_fusion.16.refs_0_), channel_id=1, source_target_pairs={{0,1},{1,0},{2,3},{3,2},{4,5},{5,4},{6,7},{7,6},{8,9},{9,8},{10,11... | collective-permute-start | bytes 1769480 | tf_op jit(solution)/shard_map/ppermute | solution.py:112
  169.2 38.0 %collective-permute-start.38 = (bf16[4,1,64,1152]{3,2,1,0:T(8,128)(2,1)}, bf16[4,1,64,1152]{3,2,1,0:T(8,128)(2,1)}, u32[]{:S(2)}, u32[]{:S(2)}) collective-permute-start(bf16[4,1,64,1152]{3,2,1,0:T(8,128)(2,1)} %pad_maximum_fusion.16.refs_0_), channel_id=1, source_target_pairs={{0,2},{2,0},{4,6},{6,4},{8,10},{10,8},{12,14},{14,12},{16,18},{18,... | collective-permute-start | bytes 1769480 | tf_op jit(solution)/shard_map/ppermute | solution.py:115
  211.5 32.4 %collective-permute-start.27 = (bf16[4,1,72,2304]{3,2,1,0:T(8,128)(2,1)}, bf16[4,1,72,2304]{3,2,1,0:T(8,128)(2,1)}, u32[]{:S(2)}, u32[]{:S(2)}) collective-permute-start(bf16[4,1,72,2304]{3,2,1,0:T(8,128)(2,1)} %pad_maximum_fusion.4.refs_0_), channel_id=1, source_target_pairs={{0,4},{2,6},{4,0},{6,2},{8,12},{10,14},{12,8},{14,10},{16,20},{18,... | collective-permute-start | bytes 3981320 | tf_op jit(solution)/shard_map/ppermute | solution.py:118
  222.1 41.2 %collective-permute-start.46 = (bf16[4,1,64,2048]{3,2,1,0:T(8,128)(2,1)}, bf16[4,1,64,2048]{3,2,1,0:T(8,128)(2,1)}, u32[]{:S(2)}, u32[]{:S(2)}) collective-permute-start(bf16[4,1,64,2048]{3,2,1,0:T(8,128)(2,1)} %pad_maximum_fusion.9.refs_0_), channel_id=1, source_target_pairs={{0,4},{2,6},{4,0},{6,2},{8,12},{10,14},{12,8},{14,10},{16,20},{18,... | collective-permute-start | bytes 3145736 | tf_op jit(solution)/shard_map/ppermute | solution.py:118
  223.1 31.6 %collective-permute-start.37 = (bf16[4,1,64,1152]{3,2,1,0:T(8,128)(2,1)}, bf16[4,1,64,1152]{3,2,1,0:T(8,128)(2,1)}, u32[]{:S(2)}, u32[]{:S(2)}) collective-permute-start(bf16[4,1,64,1152]{3,2,1,0:T(8,128)(2,1)} %collective-permute-done.35.refs_1_), channel_id=1, source_target_pairs={{0,1},{1,0},{2,3},{3,2},{4,5},{5,4},{6,7},{7,6},{8,9},{9,8},{10,11... | collective-permute-start | bytes 1769480 | tf_op jit(solution)/shard_map/ppermute | solution.py:112
  225.2 29.7 %collective-permute-start.39 = (bf16[4,1,64,1152]{3,2,1,0:T(8,128)(2,1)}, bf16[4,1,64,1152]{3,2,1,0:T(8,128)(2,1)}, u32[]{:S(2)}, u32[]{:S(2)}) collective-permute-start(bf16[4,1,64,1152]{3,2,1,0:T(8,128)(2,1)} %collective-permute-done.35.refs_1_), channel_id=1, source_target_pairs={{0,2},{2,0},{4,6},{6,4},{8,10},{10,8},{12,14},{14,12},{16,18},{18,... | collective-permute-start | bytes 1769480 | tf_op jit(solution)/shard_map/ppermute | solution.py:115
  255.6 66.4 %collective-permute-start.28 = (bf16[4,1,72,2304]{3,2,1,0:T(8,128)(2,1)}, bf16[4,1,72,2304]{3,2,1,0:T(8,128)(2,1)}, u32[]{:S(2)}, u32[]{:S(2)}) collective-permute-start(bf16[4,1,72,2304]{3,2,1,0:T(8,128)(2,1)} %pad_maximum_fusion.4.refs_0_), channel_id=1, source_target_pairs={{0,2},{2,0},{4,6},{6,4},{8,10},{10,8},{12,14},{14,12},{16,18},{18,... | collective-permute-start | bytes 3981320 | tf_op jit(solution)/shard_map/ppermute | solution.py:115
  263.3 59.3 %collective-permute-start.29 = (bf16[4,1,72,2304]{3,2,1,0:T(8,128)(2,1)}, bf16[4,1,72,2304]{3,2,1,0:T(8,128)(2,1)}, u32[]{:S(2)}, u32[]{:S(2)}) collective-permute-start(bf16[4,1,72,2304]{3,2,1,0:T(8,128)(2,1)} %collective-permute-done.27.refs_1_), channel_id=1, source_target_pairs={{0,2},{2,0},{4,6},{6,4},{8,10},{10,8},{12,14},{14,12},{16,18},{18,... | collective-permute-start | bytes 3981320 | tf_op jit(solution)/shard_map/ppermute | solution.py:115
  264.1 58.0 %collective-permute-start.47 = (bf16[4,1,64,2048]{3,2,1,0:T(8,128)(2,1)}, bf16[4,1,64,2048]{3,2,1,0:T(8,128)(2,1)}, u32[]{:S(2)}, u32[]{:S(2)}) collective-permute-start(bf16[4,1,64,2048]{3,2,1,0:T(8,128)(2,1)} %pad_maximum_fusion.9.refs_0_), channel_id=1, source_target_pairs={{0,1},{1,0},{2,3},{3,2},{4,5},{5,4},{6,7},{7,6},{8,9},{9,8},{10,11... | collective-permute-start | bytes 3145736 | tf_op jit(solution)/shard_map/ppermute | solution.py:112
  265.2 57.3 %collective-permute-start.48 = (bf16[4,1,64,2048]{3,2,1,0:T(8,128)(2,1)}, bf16[4,1,64,2048]{3,2,1,0:T(8,128)(2,1)}, u32[]{:S(2)}, u32[]{:S(2)}) collective-permute-start(bf16[4,1,64,2048]{3,2,1,0:T(8,128)(2,1)} %collective-permute-done.46.refs_1_), channel_id=1, source_target_pairs={{0,1},{1,0},{2,3},{3,2},{4,5},{5,4},{6,7},{7,6},{8,9},{9,8},{10,11... | collective-permute-start | bytes 3145736 | tf_op jit(solution)/shard_map/ppermute | solution.py:112
  267.2 67.8 %collective-permute-start.17 = (bf16[256,1152]{1,0:T(8,128)(2,1)}, bf16[256,1152]{1,0:T(8,128)(2,1)}, u32[]{:S(2)}, u32[]{:S(2)}) collective-permute-start(bf16[256,1152]{1,0:T(8,128)(2,1)} %add_convert_fusion.2), channel_id=1, source_target_pairs={{0,1},{1,0},{2,3},{3,2},{4,5},{5,4},{6,7},{7,6},{8,9},{9,8},{10,11... | collective-permute-start | bytes 1769480 | tf_op jit(solution)/shard_map/ppermute | solution.py:112
  322.1 28.9 %collective-permute-start.49 = (bf16[4,1,64,2048]{3,2,1,0:T(8,128)(2,1)}, bf16[4,1,64,2048]{3,2,1,0:T(8,128)(2,1)}, u32[]{:S(2)}, u32[]{:S(2)}) collective-permute-start(bf16[4,1,64,2048]{3,2,1,0:T(8,128)(2,1)} %pad_maximum_fusion.9.refs_0_), channel_id=1, source_target_pairs={{0,2},{2,0},{4,6},{6,4},{8,10},{10,8},{12,14},{14,12},{16,18},{18,... | collective-permute-start | bytes 3145736 | tf_op jit(solution)/shard_map/ppermute | solution.py:115
  322.1 28.9 %collective-permute-start.50 = (bf16[4,1,64,2048]{3,2,1,0:T(8,128)(2,1)}, bf16[4,1,64,2048]{3,2,1,0:T(8,128)(2,1)}, u32[]{:S(2)}, u32[]{:S(2)}) collective-permute-start(bf16[4,1,64,2048]{3,2,1,0:T(8,128)(2,1)} %collective-permute-done.46.refs_1_), channel_id=1, source_target_pairs={{0,2},{2,0},{4,6},{6,4},{8,10},{10,8},{12,14},{14,12},{16,18},{18,... | collective-permute-start | bytes 3145736 | tf_op jit(solution)/shard_map/ppermute | solution.py:115
  322.6 28.4 %collective-permute-start.51 = (bf16[4,1,64,2048]{3,2,1,0:T(8,128)(2,1)}, bf16[4,1,64,2048]{3,2,1,0:T(8,128)(2,1)}, u32[]{:S(2)}, u32[]{:S(2)}) collective-permute-start(bf16[4,1,64,2048]{3,2,1,0:T(8,128)(2,1)} %collective-permute-done.47.refs_2_), channel_id=1, source_target_pairs={{0,2},{2,0},{4,6},{6,4},{8,10},{10,8},{12,14},{14,12},{16,18},{18,... | collective-permute-start | bytes 3145736 | tf_op jit(solution)/shard_map/ppermute | solution.py:115
  322.7 28.4 %collective-permute-start.52 = (bf16[4,1,64,2048]{3,2,1,0:T(8,128)(2,1)}, bf16[4,1,64,2048]{3,2,1,0:T(8,128)(2,1)}, u32[]{:S(2)}, u32[]{:S(2)}) collective-permute-start(bf16[4,1,64,2048]{3,2,1,0:T(8,128)(2,1)} %collective-permute-done.48.refs_3_), channel_id=1, source_target_pairs={{0,2},{2,0},{4,6},{6,4},{8,10},{10,8},{12,14},{14,12},{16,18},{18,... | collective-permute-start | bytes 3145736 | tf_op jit(solution)/shard_map/ppermute | solution.py:115
  376.9 59.2 %collective-permute-start.31 = (bf16[256,1152]{1,0:T(8,128)(2,1)S(1)}, bf16[256,1152]{1,0:T(8,128)(2,1)S(1)}, u32[]{:S(2)}, u32[]{:S(2)}) collective-permute-start(bf16[256,1152]{1,0:T(8,128)(2,1)S(1)} %get-tuple-element.153), channel_id=1, source_target_pairs={{0,1},{1,0},{2,3},{3,2},{4,5},{5,4},{6,7},{7,6},{8,9},{9,8},{10,11... | collective-permute-start | bytes 1769480 | tf_op jit(solution)/shard_map/ppermute | solution.py:112
  401.5 141.1 %collective-permute-start.100 = (bf16[4,2,2,64,1152]{4,3,2,1,0:T(8,128)(2,1)}, bf16[4,2,2,64,1152]{4,3,2,1,0:T(8,128)(2,1)}, u32[]{:S(2)}, u32[]{:S(2)}) collective-permute-start(bf16[4,2,2,64,1152]{4,3,2,1,0:T(8,128)(2,1)} %dynamic-slice_bitcast_fusion.3), channel_id=1, source_target_pairs={{0,2},{2,0},{4,6},{6,4},{8,10},{10,8},{12,14},{14,12},{16,18},{18,... | collective-permute-start | bytes 7077896 | tf_op jit(solution)/shard_map/ppermute | solution.py:115
  402.8 51.7 %collective-permute-start.112 = (bf16[4,2,2,24,2048]{4,3,2,1,0:T(8,128)(2,1)}, bf16[4,2,2,24,2048]{4,3,2,1,0:T(8,128)(2,1)}, u32[]{:S(2)}, u32[]{:S(2)}) collective-permute-start(bf16[4,2,2,24,2048]{4,3,2,1,0:T(8,128)(2,1)} %dynamic-slice_bitcast_fusion.5), channel_id=1, source_target_pairs={{0,2},{2,0},{4,6},{6,4},{8,10},{10,8},{12,14},{14,12},{16,18},{18,... | collective-permute-start | bytes 4718600 | tf_op jit(solution)/shard_map/ppermute | solution.py:115
  485.7 32.4 %collective-permute-start.66 = (bf16[256,1152]{1,0:T(8,128)(2,1)}, bf16[256,1152]{1,0:T(8,128)(2,1)}, u32[]{:S(2)}, u32[]{:S(2)}) collective-permute-start(bf16[256,1152]{1,0:T(8,128)(2,1)} %fusion.20), channel_id=1, source_target_pairs={{0,1},{1,0},{2,3},{3,2},{4,5},{5,4},{6,7},{7,6},{8,9},{9,8},{10,11... | collective-permute-start | bytes 1769480 | tf_op jit(solution)/shard_map/ppermute | solution.py:112
  514.8 33.4 %collective-permute-start.113 = (bf16[4,2,24,2048]{3,2,1,0:T(8,128)(2,1)}, bf16[4,2,24,2048]{3,2,1,0:T(8,128)(2,1)}, u32[]{:S(2)}, u32[]{:S(2)}) collective-permute-start(bf16[4,2,24,2048]{3,2,1,0:T(8,128)(2,1)} %fusion.33), channel_id=1, source_target_pairs={{0,1},{1,0},{2,3},{3,2},{4,5},{5,4},{6,7},{7,6},{8,9},{9,8},{10,11... | collective-permute-start | bytes 2359304 | tf_op jit(solution)/shard_map/ppermute | solution.py:112
  541.0 112.9 %collective-permute-start.106 = (bf16[4,2,2,64,2048]{4,3,2,1,0:T(8,128)(2,1)}, bf16[4,2,2,64,2048]{4,3,2,1,0:T(8,128)(2,1)}, u32[]{:S(2)}, u32[]{:S(2)}) collective-permute-start(bf16[4,2,2,64,2048]{4,3,2,1,0:T(8,128)(2,1)} %dynamic-slice_bitcast_fusion), channel_id=1, source_target_pairs={{0,2},{2,0},{4,6},{6,4},{8,10},{10,8},{12,14},{14,12},{16,18},{18,... | collective-permute-start | bytes 12582920 | tf_op jit(solution)/shard_map/ppermute | solution.py:115
  542.0 61.3 %collective-permute-start.78 = (bf16[4,2,72,2304]{3,2,1,0:T(8,128)(2,1)}, bf16[4,2,72,2304]{3,2,1,0:T(8,128)(2,1)}, u32[]{:S(2)}, u32[]{:S(2)}) collective-permute-start(bf16[4,2,72,2304]{3,2,1,0:T(8,128)(2,1)} %dynamic-slice_bitcast_fusion.2), channel_id=1, source_target_pairs={{0,2},{2,0},{4,6},{6,4},{8,10},{10,8},{12,14},{14,12},{16,18},{18,... | collective-permute-start | bytes 7962632 | tf_op jit(solution)/shard_map/ppermute | solution.py:115
  548.0 82.8 %collective-permute-start.83 = (bf16[4,2,72,2304]{3,2,1,0:T(8,128)(2,1)}, bf16[4,2,72,2304]{3,2,1,0:T(8,128)(2,1)}, u32[]{:S(2)}, u32[]{:S(2)}) collective-permute-start(bf16[4,2,72,2304]{3,2,1,0:T(8,128)(2,1)} %dynamic-slice_bitcast_fusion.1), channel_id=1, source_target_pairs={{0,2},{2,0},{4,6},{6,4},{8,10},{10,8},{12,14},{14,12},{16,18},{18,... | collective-permute-start | bytes 7962632 | tf_op jit(solution)/shard_map/ppermute | solution.py:115
  598.4 35.9 %collective-permute-start.68 = (bf16[4,2,72,1728]{3,2,1,0:T(8,128)(2,1)}, bf16[4,2,72,1728]{3,2,1,0:T(8,128)(2,1)S(1)}, u32[]{:S(2)}, u32[]{:S(2)}) collective-permute-start(bf16[4,2,72,1728]{3,2,1,0:T(8,128)(2,1)} %dynamic-slice_bitcast_fusion.4), channel_id=1, source_target_pairs={{0,2},{2,0},{4,6},{6,4},{8,10},{10,8},{12,14},{14,12},{16,18},{18,... | collective-permute-start | bytes 5971976 | tf_op jit(solution)/shard_map/ppermute | solution.py:115
  600.2 28.6 %collective-permute-start.101 = (bf16[4,2,64,1152]{3,2,1,0:T(8,128)(2,1)}, bf16[4,2,64,1152]{3,2,1,0:T(8,128)(2,1)S(1)}, u32[]{:S(2)}, u32[]{:S(2)}) collective-permute-start(bf16[4,2,64,1152]{3,2,1,0:T(8,128)(2,1)} %fusion.25), channel_id=1, source_target_pairs={{0,1},{1,0},{2,3},{3,2},{4,5},{5,4},{6,7},{7,6},{8,9},{9,8},{10,11... | collective-permute-start | bytes 3538952 | tf_op jit(solution)/shard_map/ppermute | solution.py:112
  605.7 62.1 %collective-permute-start.79 = (bf16[4,72,2304]{2,1,0:T(8,128)(2,1)S(1)}, bf16[4,72,2304]{2,1,0:T(8,128)(2,1)S(1)}, u32[]{:S(2)}, u32[]{:S(2)}) collective-permute-start(bf16[4,72,2304]{2,1,0:T(8,128)(2,1)S(1)} %fusion.17), channel_id=1, source_target_pairs={{0,4},{2,6},{4,0},{6,2},{8,12},{10,14},{12,8},{14,10},{16,20},{18,... | collective-permute-start | bytes 3981320 | tf_op jit(solution)/shard_map/ppermute | solution.py:118
  632.5 46.2 %collective-permute-start.84 = (bf16[4,72,2304]{2,1,0:T(8,128)(2,1)S(1)}, bf16[4,72,2304]{2,1,0:T(8,128)(2,1)S(1)}, u32[]{:S(2)}, u32[]{:S(2)}) collective-permute-start(bf16[4,72,2304]{2,1,0:T(8,128)(2,1)S(1)} %fusion.16), channel_id=1, source_target_pairs={{0,4},{2,6},{4,0},{6,2},{8,12},{10,14},{12,8},{14,10},{16,20},{18,... | collective-permute-start | bytes 3981320 | tf_op jit(solution)/shard_map/ppermute | solution.py:118
  657.9 42.3 %collective-permute-start.69 = (bf16[4,72,1728]{2,1,0:T(8,128)(2,1)S(1)}, bf16[4,72,1728]{2,1,0:T(8,128)(2,1)S(1)}, u32[]{:S(2)}, u32[]{:S(2)}) collective-permute-start(bf16[4,72,1728]{2,1,0:T(8,128)(2,1)S(1)} %fusion.32), channel_id=1, source_target_pairs={{0,4},{2,6},{4,0},{6,2},{8,12},{10,14},{12,8},{14,10},{16,20},{18,... | collective-permute-start | bytes 2985992 | tf_op jit(solution)/shard_map/ppermute | solution.py:118
  665.2 42.7 %collective-permute-start.107 = (bf16[4,2,64,2048]{3,2,1,0:T(8,128)(2,1)S(1)}, bf16[4,2,64,2048]{3,2,1,0:T(8,128)(2,1)S(1)}, u32[]{:S(2)}, u32[]{:S(2)}) collective-permute-start(bf16[4,2,64,2048]{3,2,1,0:T(8,128)(2,1)S(1)} %fusion.9), channel_id=1, source_target_pairs={{0,1},{1,0},{2,3},{3,2},{4,5},{5,4},{6,7},{7,6},{8,9},{9,8},{10,11... | collective-permute-start | bytes 6291464 | tf_op jit(solution)/shard_map/ppermute | solution.py:112
  669.3 32.3 %collective-permute-start.82 = (bf16[72,2304]{1,0:T(8,128)(2,1)S(1)}, bf16[72,2304]{1,0:T(8,128)(2,1)S(1)}, u32[]{:S(2)}, u32[]{:S(2)}) collective-permute-start(bf16[72,2304]{1,0:T(8,128)(2,1)S(1)} %get-tuple-element.74), channel_id=1, source_target_pairs={{0,24},{2,26},{4,28},{6,30},{8,0},{10,2},{12,4},{14,6},{16,8},{18,... | collective-permute-start | bytes 995336 | tf_op jit(solution)/shard_map/ppermute | solution.py:123
  669.4 32.3 %collective-permute-start.81 = (bf16[72,2304]{1,0:T(8,128)(2,1)S(1)}, bf16[72,2304]{1,0:T(8,128)(2,1)S(1)}, u32[]{:S(2)}, u32[]{:S(2)}) collective-permute-start(bf16[72,2304]{1,0:T(8,128)(2,1)S(1)} %get-tuple-element.75), channel_id=1, source_target_pairs={{0,16},{2,18},{4,20},{6,22},{8,24},{10,26},{12,28},{14,30},{16,0},... | collective-permute-start | bytes 995336 | tf_op jit(solution)/shard_map/ppermute | solution.py:123
  701.6 39.5 %collective-permute-start.86 = (bf16[72,2304]{1,0:T(8,128)(2,1)S(1)}, bf16[72,2304]{1,0:T(8,128)(2,1)S(1)}, u32[]{:S(2)}, u32[]{:S(2)}) collective-permute-start(bf16[72,2304]{1,0:T(8,128)(2,1)S(1)} %get-tuple-element.72), channel_id=1, source_target_pairs={{0,16},{2,18},{4,20},{6,22},{8,24},{10,26},{12,28},{14,30},{16,0},... | collective-permute-start | bytes 995336 | tf_op jit(solution)/shard_map/ppermute | solution.py:123
  701.7 39.7 %collective-permute-start.85 = (bf16[72,2304]{1,0:T(8,128)(2,1)S(1)}, bf16[72,2304]{1,0:T(8,128)(2,1)S(1)}, u32[]{:S(2)}, u32[]{:S(2)}) collective-permute-start(bf16[72,2304]{1,0:T(8,128)(2,1)S(1)} %get-tuple-element.70), channel_id=1, source_target_pairs={{0,8},{2,10},{4,12},{6,14},{8,16},{10,18},{12,20},{14,22},{16,24},... | collective-permute-start | bytes 995336 | tf_op jit(solution)/shard_map/ppermute | solution.py:123
  702.7 40.8 %collective-permute-start.72 = (bf16[72,1728]{1,0:T(8,128)(2,1)S(1)}, bf16[72,1728]{1,0:T(8,128)(2,1)S(1)}, u32[]{:S(2)}, u32[]{:S(2)}) collective-permute-start(bf16[72,1728]{1,0:T(8,128)(2,1)S(1)} %get-tuple-element.80), channel_id=1, source_target_pairs={{0,24},{2,26},{4,28},{6,30},{8,0},{10,2},{12,4},{14,6},{16,8},{18,... | collective-permute-start | bytes 746504 | tf_op jit(solution)/shard_map/ppermute | solution.py:123
  707.9 42.5 %collective-permute-start.71 = (bf16[72,1728]{1,0:T(8,128)(2,1)S(1)}, bf16[72,1728]{1,0:T(8,128)(2,1)S(1)}, u32[]{:S(2)}, u32[]{:S(2)}) collective-permute-start(bf16[72,1728]{1,0:T(8,128)(2,1)S(1)} %get-tuple-element.81), channel_id=1, source_target_pairs={{0,16},{2,18},{4,20},{6,22},{8,24},{10,26},{12,28},{14,30},{16,0},... | collective-permute-start | bytes 746504 | tf_op jit(solution)/shard_map/ppermute | solution.py:123
  712.2 38.2 %collective-permute-start.70 = (bf16[72,1728]{1,0:T(8,128)(2,1)S(1)}, bf16[72,1728]{1,0:T(8,128)(2,1)S(1)}, u32[]{:S(2)}, u32[]{:S(2)}) collective-permute-start(bf16[72,1728]{1,0:T(8,128)(2,1)S(1)} %get-tuple-element.79), channel_id=1, source_target_pairs={{0,8},{2,10},{4,12},{6,14},{8,16},{10,18},{12,20},{14,22},{16,24},... | collective-permute-start | bytes 746504 | tf_op jit(solution)/shard_map/ppermute | solution.py:123
  (183 other events, 2483.8 us)

commit v2 on v1

v2 whole, which is shorter than its diff:
```python
import jax
import jax.numpy as jnp
from jax import lax
from jax.experimental import pallas as pl
from jax.experimental.pallas import tpu as pltpu
from jax.sharding import PartitionSpec as P

HD = 72
ROWS = 2
CORES = 2


epsilon = 1e-06
gelu_slope = 0.7978845608028654
gelu_cubic = 0.044715


def layer_norm(values):
    center = values - jnp.mean(values, axis=-1, keepdims=True)
    inverse = lax.rsqrt(jnp.mean(center * center, axis=-1, keepdims=True) + epsilon)
    return (center * inverse, inverse)


def norm_back(incoming, normed, inverse):
    return inverse * (
        incoming
        - jnp.mean(incoming, axis=-1, keepdims=True)
        - normed * jnp.mean(incoming * normed, axis=-1, keepdims=True)
    )


def gelu_tanh(values):
    inside = gelu_slope * (values + gelu_cubic * values * values * values)
    return 0.5 * values * (1.0 + jnp.tanh(inside))


def gelu_grad(values):
    tangent = jnp.tanh(gelu_slope * (values + gelu_cubic * values * values * values))
    return 0.5 * (1.0 + tangent) + 0.5 * values * (1.0 - tangent * tangent) * gelu_slope * (
        1.0 + 3.0 * gelu_cubic * values * values
    )


def silu_grad(values):
    sigma = jax.nn.sigmoid(values)
    return sigma * (1.0 + values * (1.0 - sigma))


def place_pieces(pieces, place, planes, with_side, cuts):
    count = len(pieces)
    _, held, part_rows, columns = pieces[0].shape
    kind = pieces[0].dtype

    def body(place_ref, *refs):
        sources, targets = refs[:count], refs[count : count + len(cuts)]
        slots, in_sems, out_sems = refs[count + len(cuts) :]
        arriving = [
            pltpu.make_async_copy(sources[k], slots.at[k], in_sems.at[k]) for k in range(count)
        ]
        for copy in arriving:
            copy.start()
        leaving = []
        for k in range(count):
            arriving[k].wait()
            at_row = place_ref[planes] ^ (k & 1)
            if with_side:
                at_side = place_ref[planes + 2] ^ ((k >> 1) & 1)
                at_core = place_ref[planes + 1] ^ (k >> 2)
            else:
                at_core = place_ref[planes + 1] ^ (k >> 1)
            for s in range(planes):
                for j, (start, end) in enumerate(cuts):
                    for t in range(start, end):
                        target = targets[j].at[t - start, place_ref[s], at_row, at_core]
                        if with_side:
                            target = target.at[at_side]
                        copy = pltpu.make_async_copy(
                            slots.at[k, s, t], target, out_sems.at[k, s, t]
                        )
                        copy.start()
                        leaving.append(copy)
        for copy in leaving:
            copy.wait()

    middle = (2,) if with_side else ()
    moved = count * planes * held * part_rows * columns * kind.itemsize
    return pl.pallas_call(
        body,
        in_specs=[pl.BlockSpec(memory_space=pltpu.SMEM)]
        + [pl.BlockSpec(memory_space=pl.ANY)] * count,
        out_specs=tuple(pl.BlockSpec(memory_space=pl.ANY) for _ in cuts),
        out_shape=tuple(
            jax.ShapeDtypeStruct(
                (end - start, planes, ROWS, CORES) + middle + (part_rows, columns), kind
            )
            for start, end in cuts
        ),
        scratch_shapes=[
            pltpu.VMEM((count, planes, held, part_rows, columns), kind),
            pltpu.SemaphoreType.DMA((count,)),
            pltpu.SemaphoreType.DMA((count, planes, held)),
        ],
        compiler_params=pltpu.CompilerParams(vmem_limit_bytes=moved * 5 // 4 + (4 << 20)),
        cost_estimate=pl.CostEstimate(flops=0, bytes_accessed=2 * moved, transcendentals=0),
    )(place, *pieces)


def split_grads(left, rights, core, pairs):
    count, tokens, columns = rights.shape
    rows = left.shape[1]
    part = rows // (pairs * CORES)
    kind = left.dtype

    def body(core_ref, left_ref, right_ref, mine_ref, other_ref, sums):
        sums[...] = lax.dot_general(
            left_ref[...],
            right_ref[0],
            (((0,), (0,)), ((), ())),
            preferred_element_type=jnp.float32,
        )
        mine = core_ref[0]
        for j in range(pairs):
            start = pl.multiple_of((CORES * j + mine) * part, 8)
            mine_ref[0, j] = sums[pl.ds(start, part), :].astype(kind)
            start = pl.multiple_of((CORES * j + 1 - mine) * part, 8)
            other_ref[0, j] = sums[pl.ds(start, part), :].astype(kind)

    out = jax.ShapeDtypeStruct((count, pairs, part, columns), kind)
    spec = pl.BlockSpec((1, pairs, part, columns), lambda k, core_ref: (k, 0, 0, 0))
    return pl.pallas_call(
        body,
        grid_spec=pltpu.PrefetchScalarGridSpec(
            num_scalar_prefetch=1,
            grid=(count,),
            in_specs=[
                pl.BlockSpec((tokens, rows), lambda k, core_ref: (0, 0)),
                pl.BlockSpec((1, tokens, columns), lambda k, core_ref: (k, 0, 0)),
            ],
            out_specs=(spec, spec),
            scratch_shapes=[pltpu.VMEM((rows, columns), jnp.float32)],
        ),
        out_shape=(out, out),
        compiler_params=pltpu.CompilerParams(vmem_limit_bytes=32 << 20),
        cost_estimate=pl.CostEstimate(
            flops=2 * count * tokens * rows * columns,
            bytes_accessed=2 * count * (tokens + rows) * columns,
            transcendentals=0,
        ),
    )(core, left, rights)


def heads_dot(left, right, left_axis, right_axis):
    return lax.dot_general(
        left, right, (((left_axis,), (right_axis,)), ((), ())), preferred_element_type=jnp.float32
    )


def attend(queries, keys, values, seq_len):
    tokens, width = queries.shape
    heads = width // HD
    scale = float(HD) ** (-0.5)

    def body(q_ref, k_ref, v_ref, out_ref, lse_ref):
        for head in range(heads):
            at = pl.ds(head * HD, HD)
            scores = heads_dot(q_ref[:, at], k_ref[:, at], 1, 1) * scale
            top = jnp.max(scores, axis=-1, keepdims=True)
            shifted = jnp.exp(scores - top)
            total = jnp.sum(shifted, axis=-1, keepdims=True)
            lse_ref[:, pl.ds(head, 1)] = top + jnp.log(total)
            probs = (shifted / total).astype(out_ref.dtype)
            out_ref[:, at] = heads_dot(probs, v_ref[:, at], 1, 0).astype(out_ref.dtype)

    block = pl.BlockSpec((seq_len, width), lambda image: (image, 0))
    return pl.pallas_call(
        body,
        grid=(tokens // seq_len,),
        in_specs=[block] * 3,
        out_specs=(block, pl.BlockSpec((seq_len, heads), lambda image: (image, 0))),
        out_shape=(
            jax.ShapeDtypeStruct((tokens, width), queries.dtype),
            jax.ShapeDtypeStruct((tokens, heads), jnp.float32),
        ),
        compiler_params=pltpu.CompilerParams(vmem_limit_bytes=32 << 20),
        cost_estimate=pl.CostEstimate(
            flops=16 * tokens * seq_len * width,
            bytes_accessed=8 * tokens * width,
            transcendentals=tokens * seq_len * heads,
        ),
    )(queries, keys, values)


def attend_back(queries, keys, values, lse, incoming, seq_len):
    tokens, width = queries.shape
    heads = width // HD
    scale = float(HD) ** (-0.5)

    def body(q_ref, k_ref, v_ref, lse_ref, in_ref, out_ref):
        kind = out_ref.dtype
        for head in range(heads):
            at = pl.ds(head * HD, HD)
            q, k, v, g = q_ref[:, at], k_ref[:, at], v_ref[:, at], in_ref[:, at]
            probs = jnp.exp(heads_dot(q, k, 1, 1) * scale - lse_ref[:, pl.ds(head, 1)])
            out_ref[2, :, at] = heads_dot(probs.astype(kind), g, 0, 0).astype(kind)
            grad = heads_dot(g, v, 1, 1)
            inner = jnp.sum(probs * grad, axis=-1, keepdims=True)
            grad = (probs * (grad - inner)).astype(kind)
            out_ref[0, :, at] = (heads_dot(grad, k, 1, 0) * scale).astype(kind)
            out_ref[1, :, at] = (heads_dot(grad, q, 0, 0) * scale).astype(kind)

    block = pl.BlockSpec((seq_len, width), lambda image: (image, 0))
    return pl.pallas_call(
        body,
        grid=(tokens // seq_len,),
        in_specs=[block] * 3
        + [pl.BlockSpec((seq_len, heads), lambda image: (image, 0)), block],
        out_specs=pl.BlockSpec((3, seq_len, width), lambda image: (0, image, 0)),
        out_shape=jax.ShapeDtypeStruct((3, tokens, width), queries.dtype),
        compiler_params=pltpu.CompilerParams(vmem_limit_bytes=32 << 20),
        cost_estimate=pl.CostEstimate(
            flops=32 * tokens * seq_len * width,
            bytes_accessed=16 * tokens * width,
            transcendentals=tokens * seq_len * heads,
        ),
    )(queries, keys, values, lse, incoming)


def solution(mesh):
    dp, mp = mesh.shape["dp"], mesh.shape["mp"]
    planes = dp // (ROWS * CORES)

    far = [1 << k for k in range(dp.bit_length() - 2, 1, -1)]
    near_order = [CORES] + far + [1]

    def swap_x(value):
        return lax.ppermute(value, "mp", [(k, k ^ 1) for k in range(mp)])

    def swap(value, mask):
        return lax.ppermute(value, "dp", [(k, k ^ mask) for k in range(dp)])

    def swap_c(value):
        return swap(value, 1)

    def swap_y(value):
        return swap(value, CORES)

    def shards(
        patches,
        time_bins,
        class_ids,
        encoder_feats,
        cotangent,
        w_qkv,
        w_out,
        w_up,
        w_down,
        w_ada,
        time_table,
        class_table,
        inner_bias,
        b_out,
        b_down,
        b_ada,
        w_first,
        w_second,
        w_third,
        b_first,
        b_second,
        b_third,
    ):
        f32 = jnp.float32
        bf16 = jnp.bfloat16
        image_count, seq_len, width = patches.shape
        me = lax.axis_index("dp")
        side = lax.axis_index("mp")
        core = lax.rem(me, CORES)
        row = lax.rem(me // CORES, ROWS)
        plane = me // (ROWS * CORES)

        def spot(index):
            return sum(mask for k, mask in enumerate(far) if index >> k & 1)

        place = jnp.stack(
            [plane ^ (spot(s) // (ROWS * CORES)) for s in range(planes)] + [row, core, side]
        ).astype(jnp.int32)

        def pick(values, index, axis=0):
            return lax.dynamic_index_in_dim(values, index, axis, keepdims=False)

        def ordered(own, other):
            first = side == 0
            return jnp.stack((jnp.where(first, own, other), jnp.where(first, other, own)), axis=0)

        last = [me]
        air = []

        def tie(value, *arrived):
            return lax.optimization_barrier((value,) + arrived)[0]

        def after(value, *arrived):
            return tie(value, *last, *arrived)

        def mark(value):
            last[:] = [value]
            return value

        def fly(value):
            air.append(value)
            return value

        def land():
            last.extend(air)
            air.clear()

        def join(value, arrived, axis=0):
            value = lax.optimization_barrier((value, arrived, *last))
            return mark(jnp.concatenate(value[:2], axis=axis))

        def gather_place(pieces, with_side, cuts):
            _, _, part_rows, columns = pieces[0].shape
            placed = place_pieces(pieces, place, planes, with_side, cuts)
            total = dp * (mp if with_side else 1)
            return [
                out.reshape(end - start, total * part_rows, columns)
                for out, (start, end) in zip(placed, cuts)
            ]

        class Scatter:
            def __init__(self, sums, with_side):
                self.axes = [mask for mask in far] + [CORES, 1] + ([0] if with_side else [])
                shape = (2,) * len(self.axes) + (-1, sums[0].shape[-1])
                self.terms = [[part.reshape(shape)] for part in sums]

            @classmethod
            def from_halves(cls, mine, other):
                self = cls.__new__(cls)
                self.axes = [mask for mask in far] + [CORES]
                shape = (2,) * len(self.axes) + mine.shape[2:]
                arrived = fly(swap_c(other))
                self.terms = [
                    [mine[k].reshape(shape), arrived[k].reshape(shape)]
                    for k in range(mine.shape[0])
                ]
                return self

            def send(self, mask, turn=0, turns=1):
                at = self.axes.index(mask)
                mine = lax.rem(me // mask, 2) if mask else side
                move = (lambda value: swap(value, mask)) if mask else swap_x
                planes_left = 1 << sum(1 for axis in self.axes if axis in far and axis != mask)
                if turn == 0:
                    self.flying = []
                self.terms[0][-1] = after(self.terms[0][-1])
                outgoing = []
                for terms in self.terms:
                    halves = [pick(term, 1 - mine, at) for term in terms]
                    shape = halves[0].shape
                    if turns > 1:
                        size = planes_left // turns
                        halves = [
                            half.reshape((planes_left, -1) + shape[-2:])[
                                turn * size : (turn + 1) * size
                            ]
                            for half in halves
                        ]
                    outgoing.append(sum(half.astype(f32) for half in halves).astype(bf16))
                self.flying.append(fly(move(mark(jnp.stack(outgoing, axis=0)))))
                if turn < turns - 1:
                    return
                arrived = self.flying[0]
                if turns > 1:
                    arrived = jnp.concatenate(self.flying, axis=1)
                    arrived = arrived.reshape((-1,) + shape)
                self.axes.pop(at)
                self.terms = [
                    [pick(term, mine, at) for term in terms] + [arrived[k]]
                    for k, terms in enumerate(self.terms)
                ]

            def finish(self):
                return [sum(term.astype(f32) for term in terms) for terms in self.terms]

        def gather_near(value, axis):
            for mask in near_order:
                value = jnp.concatenate((value, swap(value, mask)), axis=axis)
            return value

        hidden_size = b_first.shape[0]
        shard_late = jnp.concatenate((w_second.T, w_third.T), axis=0)

        lanes = 128
        numbers = jnp.concatenate((time_bins, class_ids)).astype(f32)
        packed = jnp.concatenate(
            (
                jnp.pad(numbers, (0, lanes - numbers.shape[0])),
                inner_bias.reshape(-1),
                b_out,
                b_down,
                b_first,
                b_second,
                b_third,
            )
        ).reshape(1, -1)
        near_packed = packed
        pair_a = tie(w_qkv[None, :2], packed)
        ways_a = list(far)
        arrived = swap(pair_a, ways_a[0])
        for mask in near_order[:-1]:
            near_packed = join(near_packed, swap(near_packed, mask))
            if mask in far and len(ways_a) > 1:
                pair_a = join(pair_a, arrived)
                ways_a.pop(0)
                arrived = swap(pair_a, ways_a[0])
        near_packed = join(near_packed, swap(near_packed, near_order[-1]))
        near_ids = near_packed[:, : 2 * image_count].astype(jnp.int32)
        near_bins = near_ids[:, :image_count].reshape(-1)
        near_labels = near_ids[:, image_count:].reshape(-1)
        order = jnp.arange(dp)
        distance = sum(
            ((me ^ order) // mask % 2) << k for k, mask in enumerate(near_order)
        )
        spread = (distance[:, None] == order[None, :]).astype(bf16)
        biases = jnp.dot(
            spread, near_packed[:, lanes:].astype(bf16), preferred_element_type=f32
        )
        inner_size = inner_bias.shape[1]
        thin = b_out.shape[0]
        flat_inner = biases[:, :inner_size].reshape(-1)
        full_bout = biases[:, inner_size : inner_size + thin].reshape(-1)
        full_bdown = biases[:, inner_size + thin : inner_size + 2 * thin].reshape(-1)
        proj_biases = biases[:, inner_size + 2 * thin :].astype(bf16)
        proj_biases = jnp.moveaxis(ordered(proj_biases, swap_x(proj_biases)), 0, 1).astype(f32)
        bias_one = proj_biases[:, :, :hidden_size].reshape(-1)
        bias_two = proj_biases[:, :, hidden_size : 2 * hidden_size].reshape(-1)
        bias_three = proj_biases[:, :, 2 * hidden_size :].reshape(-1)

        bin_onehot = near_bins[:, None] == jnp.arange(time_table.shape[0], dtype=jnp.int32)[None, :]
        class_onehot = (
            near_labels[:, None] == jnp.arange(class_table.shape[0], dtype=jnp.int32)[None, :]
        )
        condition = jnp.dot(
            bin_onehot.astype(bf16), time_table, preferred_element_type=f32
        ) + jnp.dot(class_onehot.astype(bf16), class_table, preferred_element_type=f32)
        cond_act = jax.nn.silu(condition).astype(bf16)
        local_rows = w_ada.shape[1]
        wide_bias = lax.dynamic_update_slice(
            jnp.zeros((b_ada.shape[0], width), f32), b_ada, (0, me * local_rows)
        )
        partial_mods = (
            jnp.einsum("bd,tde->tbe", cond_act, w_ada, preferred_element_type=f32)
            + wide_bias[:, None, :]
        ).astype(bf16)
        mods = partial_mods.astype(f32)
        near_a = join(pair_a, arrived)
        row_a = swap_y(near_a)
        late = lax.all_gather(tie(shard_late, near_a), ("dp", "mp"), axis=0, tiled=False)
        proj_one = lax.all_gather(tie(w_first.T, near_a), ("dp", "mp"), axis=0, tiled=True)

        class Wide:
            def __init__(self, shard):
                self.value = shard
                self.left = list(far)
                self.arrived = swap(shard, self.left[0])

            def step(self):
                while len(self.left) > 1:
                    self.value = join(self.value, self.arrived)
                    self.left.pop(0)
                    self.arrived = swap(self.value, self.left[0])
                return self.value

            def end(self):
                return join(self.step(), self.arrived)

        wide_b = Wide(tie(jnp.concatenate((w_qkv[2:], w_out.T[None]), axis=0)[None], near_a))
        for mask in near_order[::-1]:
            half = mods.shape[1] // 2
            outgoing = mark(after(mods[:, half:]).astype(bf16))
            if mask == far[0]:
                pair_b = wide_b.step()
            mods = mods[:, :half] + after(swap(outgoing, mask)).astype(f32)
        modulation = after(mods)

        near_mods = jnp.stack((pick(modulation, side, 1), pick(modulation, 1 - side, 1)), axis=1)
        shift_one, scale_one = near_mods[0][:, None, :], near_mods[1][:, None, :]
        scale_own = scale_one[0]
        gate_one, shift_two, scale_two, gate_two = (near_mods[t][0:1] for t in range(2, 6))
        inputs = jnp.stack((pick(patches, side), pick(patches, 1 - side)), axis=0).astype(f32)

        near_b = wide_b.end()
        row_b = swap_y(near_b)
        wide_up = Wide(tie(w_up[None, None], pair_b))
        normed_one, inverse_one = layer_norm(inputs)
        act_one = mark((normed_one * (1.0 + scale_one) + shift_one).astype(bf16))

        def four(near, with_row):
            with_row = mark(after(with_row))
            return [near, with_row, swap_c(tie(near, with_row)), swap_c(with_row)]

        def dot(left, right, left_axis, right_axis):
            return lax.dot_general(
                left, right, (((left_axis,), (right_axis,)), ((), ())), preferred_element_type=f32
            )

        pieces_a = four(near_a, row_a)
        pair_up = wide_up.step()
        wide_down = Wide(tie(w_down.T[None, None], pair_up))
        (w_qk,) = gather_place(pieces_a, False, ((0, 2),))
        local_width = w_qk.shape[2]
        bias_query = flat_inner[:local_width]
        bias_value = flat_inner[local_width : 2 * local_width]
        bias_units = flat_inner[2 * local_width :]
        tokens = image_count * seq_len

        def flat(values):
            return values.reshape(tokens, values.shape[-1])

        act_flat = flat(act_one)
        qk_in = after(act_flat, w_qk)
        queries = (dot(qk_in, w_qk[0], 1, 0) + bias_query).astype(bf16)
        key_heads = dot(qk_in, w_qk[1], 1, 0).astype(bf16)
        mark(key_heads)
        pieces_b = four(near_b, row_b)
        near_up = wide_up.end()
        row_up = swap_y(near_up)
        w_value, full_out = gather_place(
            four(near_b, row_b), False, ((0, 1), (1, 2))
        )
        w_value, full_out = w_value[0], full_out[0]
        v_in = after(act_flat, w_value)
        val_heads = mark((dot(v_in, w_value, 1, 0) + bias_value).astype(bf16))
        wide_down.step()
        mixed_heads, log_total = attend(after(queries), key_heads, val_heads, seq_len)
        mixed_heads = mark(mixed_heads).reshape(image_count, seq_len, local_width)

        arrived = swap_x(mark(dot(after(mixed_heads[1]), full_out, 1, 1).astype(bf16)))
        attention = dot(after(mixed_heads[0]), full_out, 1, 1) + full_bout
        attention = mark(attention)
        near_down = wide_down.end()
        row_down = swap_y(near_down)
        pieces_up = four(near_up, row_up)
        attention = attention + after(arrived).astype(f32)
        first_sum = inputs[0] + gate_one * attention
        normed_two, inverse_two = layer_norm(first_sum)
        act_two = mark((normed_two * (1.0 + scale_two) + shift_two).astype(bf16))
        other_two = swap_x(act_two)
        (full_up,) = gather_place(pieces_up, False, ((0, 1),))
        full_up = mark(full_up[0])

        def feed(values):
            hidden = dot(after(values), full_up, 1, 0) + bias_units
            return hidden, mark(gelu_tanh(hidden).astype(bf16))

        hidden_own, active_own = feed(act_two)
        late_two = after(late)
        proj_two = mark(late_two[:, :hidden_size].reshape(dp * mp * hidden_size, -1))
        proj_three = mark(late_two[:, hidden_size:].reshape(dp * mp * b_third.shape[0], -1))
        hidden_other, active_other = feed(other_two)
        (full_down,) = gather_place(
            four(near_down, row_down), False, ((0, 1),)
        )
        full_down = mark(full_down[0])
        arrived = swap_x(mark(dot(after(active_other), full_down, 1, 1).astype(bf16)))
        branch = mark(dot(after(active_own), full_down, 1, 1))
        branch = branch + full_bdown + after(arrived).astype(f32)
        output = first_sum + gate_two * branch
        block_out = mark(output.astype(bf16))
        other_out = swap_x(block_out)

        target = pick(encoder_feats, side).astype(f32)
        pre_one = dot(after(block_out), proj_one, 1, 1) + bias_one
        act_pone = mark(jax.nn.silu(pre_one).astype(bf16))
        pre_two = dot(after(act_pone), proj_two, 1, 1) + bias_two
        act_ptwo = mark(jax.nn.silu(pre_two).astype(bf16))
        mapped = dot(after(act_ptwo), proj_three, 1, 1) + bias_three
        inv_map = lax.rsqrt(jnp.sum(mapped * mapped, axis=-1, keepdims=True) + epsilon)
        inv_target = lax.rsqrt(jnp.sum(target * target, axis=-1, keepdims=True) + epsilon)
        cosine = jnp.sum(mapped * target, axis=-1, keepdims=True) * inv_map * inv_target
        loss_weight = -0.5 * float(width)
        grad_mapped = mark(
            (
                loss_weight
                * (target * inv_map * inv_target - cosine * inv_map * inv_map * mapped)
            ).astype(bf16)
        )
        grad_bthird = jnp.sum(grad_mapped.astype(f32), axis=0)
        three = Scatter([mark(dot(after(grad_mapped), act_ptwo, 0, 0).astype(bf16))], True)
        fly(other_out)
        land()
        three.send(1)
        grad_pre_two = mark(
            (dot(after(grad_mapped), proj_three, 1, 0) * silu_grad(pre_two)).astype(bf16)
        )
        grad_bsecond = jnp.sum(grad_pre_two.astype(f32), axis=0)
        two = Scatter([mark(dot(after(grad_pre_two), act_pone, 0, 0).astype(bf16))], True)
        land()
        two.send(1)
        three.send(CORES)
        grad_pre_one = mark(
            (dot(after(grad_pre_two), proj_two, 1, 0) * silu_grad(pre_one)).astype(bf16)
        )
        grad_bfirst = jnp.sum(grad_pre_one.astype(f32), axis=0)
        grad_feed = mark(dot(after(grad_pre_one), proj_one, 1, 0))

        grad_output = pick(cotangent, side).astype(f32) + grad_feed.astype(bf16).astype(f32)
        grad_branch = mark((gate_two * grad_output).astype(bf16))
        grad_gate_two = jnp.sum(grad_output * branch, axis=0)
        grad_bdown = jnp.sum(grad_branch.astype(f32), axis=0)
        land()
        other_branch = fly(swap_x(grad_branch))
        two.send(CORES, 0, 4)
        one = Scatter([mark(dot(after(grad_pre_one), block_out, 0, 0).astype(bf16))], True)

        def feed_back(incoming, hidden):
            grad_active = dot(after(incoming), full_down, 1, 0)
            return mark((grad_active * gelu_grad(hidden)).astype(bf16))

        hidden_grad_own = feed_back(grad_branch, hidden_own)
        land()
        three.send(0)
        two.send(CORES, 1, 4)
        one.send(1)
        hidden_grad_other = feed_back(other_branch, hidden_other)
        outgoing = mark(dot(after(hidden_grad_other), full_up, 1, 1).astype(bf16))
        land()
        arrived = fly(swap_x(outgoing))
        three.send(far[-1])
        two.send(CORES, 2, 4)
        grad_act_two = mark(dot(after(hidden_grad_own), full_up, 1, 1))
        grad_bunits = jnp.sum(hidden_grad_own.astype(f32), axis=0) + jnp.sum(
            hidden_grad_other.astype(f32), axis=0
        )
        branch_both = jnp.concatenate((grad_branch, other_branch), axis=0)
        active_both = jnp.concatenate((active_own, active_other), axis=0)
        grad_wdown = mark(dot(after(branch_both), active_both, 0, 0).astype(bf16))
        own_down = lax.psum_scatter(grad_wdown, "dp", scatter_dimension=0, tiled=True)
        land()
        two.send(CORES, 3, 4)
        for mask in far[-2::-1]:
            three.send(mask)
        grad_act_two = after(grad_act_two) + arrived.astype(f32)
        grad_shift_two = jnp.sum(grad_act_two, axis=0)
        grad_scale_two = jnp.sum(grad_act_two * normed_two, axis=0)
        grad_first_sum = grad_output + norm_back(
            grad_act_two * (1.0 + scale_two), normed_two, inverse_two
        )

        grad_attention = mark((gate_one * grad_first_sum).astype(bf16))
        grad_gate_one = jnp.sum(grad_first_sum * attention, axis=0)
        grad_bout = jnp.sum(grad_attention.astype(f32), axis=0)
        land()
        other_attention = fly(swap_x(grad_attention))
        act_both = jnp.concatenate((act_two, other_two), axis=0)
        hidden_both = jnp.concatenate((hidden_grad_own, hidden_grad_other), axis=0)
        grad_wup = mark(dot(after(act_both), hidden_both, 0, 0).astype(bf16))
        own_up = lax.psum_scatter(grad_wup, "dp", scatter_dimension=0, tiled=True)
        land()
        two.send(0, 0, 2)
        attention_both = mark(
            jnp.concatenate((after(grad_attention), other_attention), axis=0)
        )
        grad_mixed = mark(dot(after(attention_both), full_out, 1, 0).astype(bf16))
        my_core = core[None].astype(jnp.int32)
        halves = split_grads(
            after(attention_both), flat(mixed_heads)[None], my_core, planes * ROWS
        )
        out = Scatter.from_halves(halves[0], mark(halves[1]))
        land()
        two.send(0, 1, 2)
        grad_three = mark(
            attend_back(queries, key_heads, val_heads, log_total, after(grad_mixed), seq_len)
        )
        grad_bquery = jnp.sum(grad_three[0].astype(f32), axis=0)
        grad_bvalue = jnp.sum(grad_three[2].astype(f32), axis=0)
        land()
        out.send(CORES)
        two.send(far[-1])

        def part_one(start):
            held = after(grad_three)
            return sum(
                dot(held[t, start : start + seq_len], weight, 1, 1)
                for t, weight in enumerate((w_qk[0], w_qk[1], w_value))
            )

        outgoing = mark(part_one(seq_len).astype(bf16))
        grad_act_one = mark(part_one(0))
        land()
        arrived = fly(swap_x(outgoing))
        one.send(CORES, 0, 2)
        halves = split_grads(act_flat, after(grad_three), my_core, planes * ROWS)
        qkv = Scatter.from_halves(halves[0], mark(halves[1]))
        land()
        one.send(CORES, 1, 2)
        out.send(far[-1])
        normed_own, inverse_own = normed_one[0], inverse_one[0]
        grad_act_one = after(grad_act_one) + arrived.astype(f32)
        grad_shift_one = jnp.sum(grad_act_one, axis=0)
        grad_scale_one = jnp.sum(grad_act_one * normed_own, axis=0)
        grad_own = grad_first_sum + norm_back(
            grad_act_one * (1.0 + scale_own), normed_own, inverse_own
        )
        def rows_of(values):
            short = -values.size % width
            return jnp.pad(values, (0, short)).reshape(-1, width)

        grad_inner = jnp.concatenate((grad_bquery, grad_bvalue, grad_bunits))
        sent = [
            jnp.stack(
                (
                    grad_shift_one,
                    grad_scale_one,
                    grad_gate_one,
                    grad_shift_two,
                    grad_scale_two,
                    grad_gate_two,
                ),
                axis=0,
            )
        ] + [
            rows_of(values)
            for values in (
                grad_bout,
                grad_bdown,
                grad_bfirst,
                grad_bsecond,
                grad_bthird,
                grad_inner,
            )
        ]
        heights = [piece.shape[0] for piece in sent]
        sent = jnp.concatenate(sent, axis=0).astype(bf16)
        mark(sent)
        land()
        row_sent = fly(swap(sent, near_order[0]))
        land()
        qkv.send(CORES)
        near_sent = mark(jnp.stack((after(sent), row_sent), axis=1))
        side_sent = swap_x(near_sent)
        grad_other = fly(swap_x(tie(grad_own.astype(bf16), near_sent)))
        near_sent = ordered(near_sent, after(side_sent))
        near_sent = mark(jnp.moveaxis(near_sent, 0, 2).reshape(sent.shape[0], -1, width))
        arrived = swap(near_sent, near_order[1])
        for mask in far[-2::-1]:
            two.send(mask)
        near_sent = mark(jnp.concatenate((near_sent, after(arrived)), axis=1))
        land()
        arrived = fly(swap(near_sent, near_order[2]))
        one.send(0)
        qkv.send(far[-1])
        for mask in far[-2::-1]:
            out.send(mask)
        land()
        near_sent = mark(jnp.concatenate((after(near_sent), arrived), axis=1))
        for mask in near_order[3:]:
            arrived = fly(swap(near_sent, mask))
            near_sent = mark(jnp.concatenate((near_sent, after(arrived)), axis=1))
        one.send(far[-1])
        for mask in far[-2::-1]:
            qkv.send(mask)
        land()
        for mask in far[-2::-1]:
            one.send(mask)
        near_sent = after(near_sent)
        every_mods = near_sent[: heights[0]]
        totals = jnp.sum(near_sent.astype(f32), axis=1)
        by_side = near_sent.reshape(near_sent.shape[0], dp, mp, width)[-heights[-1] :]
        inner_total = jnp.sum(pick(by_side, side, 2).astype(f32), axis=1).reshape(-1)
        sum_bada = lax.dynamic_slice_in_dim(
            totals[: heights[0]], me * local_rows, local_rows, 1
        )

        def own_part(index, count, parts):
            start = sum(heights[: index + 1])
            values = totals[start : start + heights[index + 1]].reshape(-1)
            at = me if parts == dp else me * mp + side
            return lax.dynamic_slice_in_dim(values, at * count, count, 0)

        sum_bout = own_part(0, thin, dp)
        sum_bdown = own_part(1, thin, dp)
        sum_bfirst = own_part(2, hidden_size, dp * mp)
        sum_bsecond = own_part(3, hidden_size, dp * mp)
        sum_bthird = own_part(4, b_third.shape[0], dp * mp)
        sum_inner = lax.dynamic_slice_in_dim(inner_total, me * inner_size, inner_size, 0)[None]
        sum_wada = jnp.einsum("bd,tbe->tde", cond_act, every_mods, preferred_element_type=f32)
        grad_cond = jnp.einsum("tbe,tde->bd", every_mods, w_ada, preferred_element_type=f32)
        grad_cond = grad_cond * silu_grad(condition)
        sum_time = jnp.einsum(
            "bn,bd->nd", bin_onehot.astype(f32), grad_cond, precision=lax.Precision.HIGHEST
        )
        sum_class = jnp.einsum(
            "bn,bd->nd", class_onehot.astype(f32), grad_cond, precision=lax.Precision.HIGHEST
        )

        (sum_wfirst,) = one.finish()
        sum_down = after(own_down).astype(f32)
        sum_up = after(own_up).astype(f32)
        (sum_wsecond,) = two.finish()
        (sum_wthird,) = three.finish()
        sum_attn = qkv.finish() + out.finish()
        return (
            ordered(block_out, tie(other_out, sum_wada)),
            ordered(grad_own, grad_other.astype(f32)),
            jnp.stack(sum_attn[:3], axis=0),
            sum_attn[3].T,
            sum_up,
            sum_down.T,
            sum_wada,
            sum_time,
            sum_class,
            sum_inner,
            sum_bout,
            sum_bdown,
            sum_bada,
            sum_wfirst.T,
            sum_wsecond.T,
            sum_wthird.T,
            sum_bfirst,
            sum_bsecond,
            sum_bthird,
        )

    placed = (
        P("dp", None, None),
        P("dp"),
        P("dp"),
        P("dp", None, None),
        P("dp", None, None),
        P(None, "dp", "mp"),
        P("mp", "dp"),
        P("dp", "mp"),
        P("mp", "dp"),
        P(None, "dp", None),
        P(None, "dp"),
        P(None, "dp"),
        P("mp", "dp"),
        P("dp"),
        P("dp"),
        P(None, "dp"),
        P(None, ("dp", "mp")),
        P(None, ("dp", "mp")),
        P(None, ("dp", "mp")),
        P(("dp", "mp")),
        P(("dp", "mp")),
        P(("dp", "mp")),
    )
    return jax.shard_map(
        shards,
        mesh=mesh,
        in_specs=placed,
        out_specs=(
            P("dp", None, None),
            P("dp", None, None),
            P(None, "dp", "mp"),
            P("mp", "dp"),
            P("dp", "mp"),
            P("mp", "dp"),
            P(None, "dp", None),
            P(None, "dp"),
            P(None, "dp"),
            P("mp", "dp"),
            P("dp"),
            P("dp"),
            P(None, "dp"),
            P(None, ("dp", "mp")),
            P(None, ("dp", "mp")),
            P(None, ("dp", "mp")),
            P(("dp", "mp")),
            P(("dp", "mp")),
            P(("dp", "mp")),
        ),
        check_vma=False,
    )
```

time: 790 us -> 627 us (0.79)
  waiting for transfers between devices: 336 us -> 239 us
  Pallas kernels: 107 us -> 44.7 us
  starting transfers between devices: 122 us -> 79.7 us
  local copies, waits for them, and re-layouts: 51.9 us -> 69.3 us
  between operations: 3 us -> 16.2 us
  other arithmetic: 70.6 us -> 81.8 us
    pallas_call x6 -> x8, Pallas kernels: 107 us -> 44.7 us  [the longest x4 19.5 us: place_pieces(): pl.pallas_call(body, in_specs=[pl.BlockSpec(memory_space=pltpu.SMEM)] + [...]
    ppermute x97 -> x56, waiting for transfers between devices: 268 us -> 207 us  [swap(): return lax.ppermute(value, 'dp', [(k, k ^ mask) for k in range(dp)])]
    dot_general x18 -> x2, matrix products: 48.3 us -> 2.12 us  [the longest x1 1.76 us: shards(): jnp.einsum('bd,tbe->tde', cond_act, every_mods, preferred_element_type=f32)]
    dot_general x19 -> x31, matrix products: 39.9 us -> 86 us  [dot(): lax.dot_general(left, right, (((left_axis,), (right_axis,)), ((), ())), p...]
    ppermute x21 -> x15, waiting for transfers between devices: 67.9 us -> 31.7 us  [swap_x(): return lax.ppermute(value, 'mp', [(k, k ^ 1) for k in range(mp)])]
    ppermute x97 -> x56, starting transfers between devices: 95.6 us -> 59.6 us  [swap(): return lax.ppermute(value, 'dp', [(k, k ^ mask) for k in range(dp)])]
    squeeze x14 -> x2, local copies, waits for them, and re-layouts: 16 us -> 1.35 us  [send(): arrived[k]]
    dynamic_slice x5 -> x9, local copies, waits for them, and re-layouts: 0.8 us -> 15.3 us  [pick(): return lax.dynamic_index_in_dim(values, index, axis, keepdims=False)]
  transfers between devices with their start and end apart: 118 -> 75, of which waited for: 50 -> 37; matrix products, arithmetic and copies ran while one was open for 24% -> 35% of each run, Pallas kernels for 14% -> 7%
where the time goes in v2:
time: 627 us; the launch traced here: 622 us
  waiting for transfers between devices  239 us (38%)
  matrix products  92.1 us (15%)
  other arithmetic  81.8 us (13%)
  starting transfers between devices  79.7 us (13%)
  local copies, waits for them, and re-layouts  69.3 us (11%)
  Pallas kernels  44.7 us (7%)
  between operations  16.2 us (3%)
    ppermute x56, waiting for transfers between devices, swap(): return lax.ppermute(value, 'dp', [(k, k ^ mask) for k in range(dp)])  207 us
    dot_general x31, matrix products, dot(): lax.dot_general(left, right, (((left_axis,), (right_axis,)), ((), ())), p...  86 us
    ppermute x56, starting transfers between devices, swap(): return lax.ppermute(value, 'dp', [(k, k ^ mask) for k in range(dp)])  59.6 us
    ppermute x15, waiting for transfers between devices, swap_x(): return lax.ppermute(value, 'mp', [(k, k ^ 1) for k in range(mp)])  31.7 us
    convert_element_type x25, other arithmetic, send(): outgoing.append(sum((half.astype(f32) for half in halves)).astype(bf16))  26.7 us
    ppermute x15, starting transfers between devices, swap_x(): return lax.ppermute(value, 'mp', [(k, k ^ 1) for k in range(mp)])  19.7 us
    pallas_call x4, Pallas kernels, place_pieces(): pl.pallas_call(body, in_specs=[pl.BlockSpec(memory_space=pltpu.SMEM)] + [...  19.5 us
    unnamed x263, local copies, waits for them, and re-layouts  16.4 us
  transfers between devices with their start and end apart: 75, of which 37 were waited for; matrix products, arithmetic and copies ran while one was open for 35% of the time, Pallas kernels for 7%

profile of v2, /device:TPU:0, one launch (start us, length us, event | category | flops | bytes accessed | tf_op | source)
XLA Modules:
  0.0 622.4 jit_solution(8766870832168422675)
XLA Ops:
  8.9 3.0 collective-permute-start
  16.7 7.4 %collective-permute-done.1 = f32[2,640]{1,0:T(2,128)S(1)} collective-permute-done((f32[2,640]{1,0:T(2,128)S(1)}, f32[2,640]{1,0:T(2,128)S(1)}, u32[]{:S(2)}, u32[]{:S(2)}) %collective-permute-start.1) | collective-permute-done | bytes 5152 | tf_op jit(solution)/shard_map/ppermute | solution.py:239
  29.7 5.6 collective-permute-done.5
  46.3 3.4 collective-permute-start.9
  49.7 8.6 %collective-permute-done.7 = bf16[6,8,1152]{2,1,0:T(8,128)(2,1)S(1)} collective-permute-done((bf16[6,8,1152]{2,1,0:T(8,128)(2,1)S(1)}, bf16[6,8,1152]{2,1,0:T(8,128)(2,1)S(1)}, u32[]{:S(2)}, u32[]{:S(2)}) %collective-permute-start.7) | collective-permute-done | bytes 110624 | tf_op jit(solution)/shard_map/ppermute | solution.py:239
  58.4 7.1 %collective-permute-done.9 = bf16[1,2,72,576]{3,2,1,0:T(8,128)(2,1)S(1)} collective-permute-done((bf16[1,2,72,576]{3,2,1,0:T(8,128)(2,1)S(1)}, bf16[1,2,72,576]{3,2,1,0:T(8,128)(2,1)S(1)}, u32[]{:S(2)}, u32[]{:S(2)}) %collective-permute-start.9) | collective-permute-done | bytes 165920 | tf_op jit(solution)/shard_map/ppermute | solution.py:239
  68.5 3.3 collective-permute-start.11
  71.9 28.2 %collective-permute-done.11 = bf16[1,1,72,2304]{3,2,1,0:T(8,128)(2,1)S(1)} collective-permute-done((bf16[1,1,72,2304]{3,2,1,0:T(8,128)(2,1)}, bf16[1,1,72,2304]{3,2,1,0:T(8,128)(2,1)S(1)}, u32[]{:S(2)}, u32[]{:S(2)}) %collective-permute-start.11) | collective-permute-done | bytes 331808 | tf_op jit(solution)/shard_map/ppermute | solution.py:239
  110.5 31.3 %collective-permute-done.18 = bf16[2,1,72,2304]{3,2,1,0:T(8,128)(2,1)S(1)} collective-permute-done((bf16[2,1,72,2304]{3,2,1,0:T(8,128)(2,1)S(1)}, bf16[2,1,72,2304]{3,2,1,0:T(8,128)(2,1)S(1)}, u32[]{:S(2)}, u32[]{:S(2)}) %collective-permute-start.18) | collective-permute-done | bytes 663584 | tf_op jit(solution)/shard_map/ppermute | solution.py:239
  141.9 3.0 collective-permute-done.17.refs_1_
  145.5 6.0 shard_map.357
  154.6 6.0 shard_map.358
  162.2 7.4 %shard_map.359 = (bf16[512,576]{1,0:T(8,128)(2,1)S(1)}, f32[512,8]{1,0:T(8,128)S(1)}) custom-call(bf16[512,576]{1,0:T(8,128)(2,1)S(1)} %fusion.31.q_ref, bf16[512,576]{1,0:T(8,128)(2,1)S(1)} %convolution_convert_fusion.10.k_ref, bf16[512,576]{1,0:T(8,128)(2,1)S(1)} %fusion.32.v_ref), custom_call_target="tpu_custom_call" | custom-call | flops 1207959552 | bytes 2359296 | tf_op jit(solution)/shard_map/pallas_call | solution.py:175
  172.6 8.7 %collective-permute-done.23 = bf16[2,1,72,2304]{3,2,1,0:T(8,128)(2,1)S(1)} collective-permute-done((bf16[2,1,72,2304]{3,2,1,0:T(8,128)(2,1)S(1)}, bf16[2,1,72,2304]{3,2,1,0:T(8,128)(2,1)S(1)}, u32[]{:S(2)}, u32[]{:S(2)}) %collective-permute-start.23) | collective-permute-done | bytes 663584 | tf_op jit(solution)/shard_map/ppermute | solution.py:239
  190.1 3.5 shard_map.360
  196.0 4.9 multiply_convert_fusion.1
  200.9 4.1 slice.340
  205.0 3.2 collective-permute-done.26
  208.2 4.9 multiply_convert_fusion
  213.1 10.5 %collective-permute-done.27.refs_1_ = bf16[4,1,72,2304]{3,2,1,0:T(8,128)(2,1)} collective-permute-done((bf16[4,1,72,2304]{3,2,1,0:T(8,128)(2,1)}, bf16[4,1,72,2304]{3,2,1,0:T(8,128)(2,1)}, u32[]{:S(2)}, u32[]{:S(2)}) %collective-permute-start.27) | collective-permute-done | bytes 1327136 | tf_op jit(solution)/shard_map/ppermute | solution.py:239
  229.0 3.9 shard_map.361
  237.9 8.4 %slice.344 = bf16[32,64,2048]{2,1,0:T(8,128)(2,1)} slice(bf16[32,88,2048]{2,1,0:T(8,128)(2,1)} %bitcast.588), slice={[0:32], [0:64], [0:2048]} | slice | bytes 16777216 | tf_op jit(solution)/shard_map/slice | solution.py:556
  246.4 4.3 fusion.162
  255.4 5.5 multiply_convert_fusion.3
  260.9 6.2 multiply_convert_fusion.2
  285.4 7.3 %fusion.160 = (bf16[2048]{0:T(1024)(128)(2,1)}, bf16[256,2048]{1,0:T(8,128)(2,1)S(1)}) fusion(f32[256,2048]{1,0:T(8,128)} %get-tuple-element.365, bf16[256,2048]{1,0:T(8,128)(2,1)S(1)} %copy-done.62, bf16[2048,2048]{1,0:T(8,128)(2,1)} %bitcast.594), kind=kOutput, calls=%fused_computation.435 | convolution fusion | flops 2152724480 | bytes 12587008 | tf_op jit(solution)/shard_map/dot_general | solution.py:501
  292.7 3.3 fusion.146
  298.0 5.1 collective-permute-done.35
  310.1 4.6 convert_reduce_fusion.2
  314.6 4.0 collective-permute-done.37
  332.2 5.7 convert_reduce_fusion.1
  355.0 5.0 convolution_convert_fusion.1
  360.2 4.4 collective-permute-done.43
  370.5 7.5 %collective-permute-start.45 = (bf16[1,24,2048]{2,1,0:T(8,128)(2,1)S(1)}, bf16[1,24,2048]{2,1,0:T(8,128)(2,1)S(1)}, u32[]{:S(2)}, u32[]{:S(2)}) collective-permute-start(bf16[1,24,2048]{2,1,0:T(8,128)(2,1)S(1)} %fusion.92), channel_id=1, source_target_pairs={{0,16},{2,18},{4,20},{6,22},{8,24},{10,26},{12,28},{14,30},{16,0},... | collective-permute-start | bytes 294920 | tf_op jit(solution)/shard_map/ppermute | solution.py:239
  379.8 3.0 fusion.147
  387.1 5.4 convolution_convert_fusion
  392.6 3.4 collective-permute-done.46
  404.2 12.6 %collective-permute-done.47 = bf16[1,2,1,64,2048]{4,3,1,2,0:T(8,128)(2,1)S(1)} collective-permute-done((bf16[1,2,1,64,2048]{4,3,1,2,0:T(8,128)(2,1)S(1)}, bf16[1,2,1,64,2048]{4,3,1,2,0:T(8,128)(2,1)S(1)}, u32[]{:S(2)}, u32[]{:S(2)}) %collective-permute-start.47) | collective-permute-done | bytes 524320 | tf_op jit(solution)/shard_map/ppermute | solution.py:236
  420.3 11.7 %shard_map.363.right_ref = bf16[3,512,576]{2,1,0:T(8,128)(2,1)S(1)} custom-call(bf16[512,576]{1,0:T(8,128)(2,1)S(1)} %copy-done.14, bf16[512,576]{1,0:T(8,128)(2,1)S(1)} %copy-done.16, bf16[512,576]{1,0:T(8,128)(2,1)S(1)} %copy-done.18, f32[512,8]{1,0:T(8,128)S(1)} %get-tuple-element.205.lse_ref, bf16[512,576]{1,0:T(8,128)(2,1)S(1)} %convolution_convert_fusion.9.in_ref), custom_call_target="tpu_custom_call" | custom-call | flops 2415919104 | bytes 4718592 | tf_op jit(solution)/shard_map/pallas_call | solution.py:212
  442.6 10.8 %collective-permute-done.51 = bf16[1,2,64,2048]{3,2,1,0:T(8,128)(2,1)S(1)} collective-permute-done((bf16[1,2,64,2048]{3,2,1,0:T(8,128)(2,1)S(1)}, bf16[1,2,64,2048]{3,2,1,0:T(8,128)(2,1)S(1)}, u32[]{:S(2)}, u32[]{:S(2)}) %collective-permute-start.51) | collective-permute-done | bytes 524320 | tf_op jit(solution)/shard_map/ppermute | solution.py:239
  456.5 4.9 shard_map.364
  478.1 6.4 %collective-permute-done.52 = bf16[256,1152]{1,0:T(8,128)(2,1)} collective-permute-done((bf16[256,1152]{1,0:T(8,128)(2,1)}, bf16[256,1152]{1,0:T(8,128)(2,1)}, u32[]{:S(2)}, u32[]{:S(2)}) %collective-permute-start.52) | collective-permute-done | bytes 589856 | tf_op jit(solution)/shard_map/ppermute | solution.py:236
  499.0 7.2 %collective-permute-done.57 = bf16[16,1152]{1,0:T(8,128)(2,1)S(1)} collective-permute-done((bf16[16,1152]{1,0:T(8,128)(2,1)S(1)}, bf16[16,1152]{1,0:T(8,128)(2,1)S(1)}, u32[]{:S(2)}, u32[]{:S(2)}) %collective-permute-start.57) | collective-permute-done | bytes 36896 | tf_op jit(solution)/shard_map/ppermute | solution.py:239
  521.9 8.5 %collective-permute-done.59 = bf16[16,4,1152]{2,1,0:T(4,128)(2,1)S(1)} collective-permute-done((bf16[16,4,1152]{2,1,0:T(4,128)(2,1)}, bf16[16,4,1152]{2,1,0:T(4,128)(2,1)S(1)}, u32[]{:S(2)}, u32[]{:S(2)}) %collective-permute-start.59) | collective-permute-done | bytes 147488 | tf_op jit(solution)/shard_map/ppermute | solution.py:239
  530.6 10.8 %collective-permute-done.60 = bf16[3,2,2,72,576]{4,3,2,1,0:T(8,128)(2,1)} collective-permute-done((bf16[3,2,2,72,576]{4,3,2,1,0:T(8,128)(2,1)}, bf16[3,2,2,72,576]{4,3,2,1,0:T(8,128)(2,1)}, u32[]{:S(2)}, u32[]{:S(2)}) %collective-permute-start.60) | collective-permute-done | bytes 995360 | tf_op jit(solution)/shard_map/ppermute | solution.py:239
  552.5 14.9 %collective-permute-done.66 = bf16[1,72,576]{2,1,0:T(8,128)(2,1)S(1)} collective-permute-done((bf16[1,72,576]{2,1,0:T(8,128)(2,1)S(1)}, bf16[1,72,576]{2,1,0:T(8,128)(2,1)S(1)}, u32[]{:S(2)}, u32[]{:S(2)}) %collective-permute-start.66) | collective-permute-done | bytes 82976 | tf_op jit(solution)/shard_map/ppermute | solution.py:239
  567.4 7.7 %collective-permute-done.65 = bf16[3,2,72,576]{3,2,1,0:T(8,128)(2,1)S(1)} collective-permute-done((bf16[3,2,72,576]{3,2,1,0:T(8,128)(2,1)S(1)}, bf16[3,2,72,576]{3,2,1,0:T(8,128)(2,1)S(1)}, u32[]{:S(2)}, u32[]{:S(2)}) %collective-permute-start.65) | collective-permute-done | bytes 497696 | tf_op jit(solution)/shard_map/ppermute | solution.py:239
  583.0 10.4 %collective-permute-done.69 = bf16[3,72,576]{2,1,0:T(8,128)(2,1)S(1)} collective-permute-done((bf16[3,72,576]{2,1,0:T(8,128)(2,1)S(1)}, bf16[3,72,576]{2,1,0:T(8,128)(2,1)S(1)}, u32[]{:S(2)}, u32[]{:S(2)}) %collective-permute-start.69) | collective-permute-done | bytes 248864 | tf_op jit(solution)/shard_map/ppermute | solution.py:239
  (614 shorter events, 253.5 us)
Async XLA Ops:
  7.2 193.7 %all-gather.6.cloned.1.call-start = ((), (), s32[]{:S(2)}) async-start(), calls=%async_computation.5 | async-start | bytes 11894784 | tf_op jit(solution)/shard_map/all_gather | solution.py:456
  35.4 220.0 %all-gather.4.cloned.1.call-start = ((), (), s32[]{:S(2)}) async-start(), calls=%async_computation.2 | async-start | bytes 4866048 | tf_op jit(solution)/shard_map/all_gather | solution.py:457
  45.8 26.1 %collective-permute-start.12 = (bf16[4,2,72,576]{3,2,1,0:T(8,128)(2,1)S(1)}, bf16[4,2,72,576]{3,2,1,0:T(8,128)(2,1)S(1)}, u32[]{:S(2)}, u32[]{:S(2)}) collective-permute-start(bf16[4,2,72,576]{3,2,1,0:T(8,128)(2,1)S(1)} %constant_dynamic-update-slice_fusion.4.refs_0_), channel_id=1, source_target_pairs={{0,4},{2,6},{4,0},{6,2},{8,12},{10,14},{12,8},{14,10},{16,20},{18,... | collective-permute-start | bytes 1990664 | tf_op jit(solution)/shard_map/ppermute | solution.py:239
  46.3 19.2 %collective-permute-start.9 = (bf16[1,2,72,576]{3,2,1,0:T(8,128)(2,1)S(1)}, bf16[1,2,72,576]{3,2,1,0:T(8,128)(2,1)S(1)}, u32[]{:S(2)}, u32[]{:S(2)}) collective-permute-start(bf16[1,2,72,576]{3,2,1,0:T(8,128)(2,1)S(1)} %maximum_bitcast_fusion), channel_id=1, source_target_pairs={{0,16},{2,18},{4,20},{6,22},{8,24},{10,26},{12,28},{14,30},{16,0},... | collective-permute-start | bytes 497672 | tf_op jit(solution)/shard_map/ppermute | solution.py:239
  68.2 541.8 %reduce-scatter.5.cloned.1.call-start = ((), (), s32[]{:S(2)}) async-start(), calls=%async_computation.4 | async-start | bytes 5640192 | tf_op jit(solution)/shard_map/reduce_scatter | solution.py:636
  68.5 40.7 %collective-permute-start.16 = (bf16[2,2,72,576]{3,2,1,0:T(8,128)(2,1)S(1)}, bf16[2,2,72,576]{3,2,1,0:T(8,128)(2,1)S(1)}, u32[]{:S(2)}, u32[]{:S(2)}) collective-permute-start(bf16[2,2,72,576]{3,2,1,0:T(8,128)(2,1)S(1)} %constant_dynamic-update-slice_fusion.6), channel_id=1, source_target_pairs={{0,8},{2,10},{4,12},{6,14},{8,0},{10,2},{12,4},{14,6},{16,24},{18,... | collective-permute-start | bytes 995336 | tf_op jit(solution)/shard_map/ppermute | solution.py:239
  68.5 31.5 %collective-permute-start.11 = (bf16[1,1,72,2304]{3,2,1,0:T(8,128)(2,1)}, bf16[1,1,72,2304]{3,2,1,0:T(8,128)(2,1)S(1)}, u32[]{:S(2)}, u32[]{:S(2)}) collective-permute-start(bf16[1,1,72,2304]{3,2,1,0:T(8,128)(2,1)} %bitcast.663), channel_id=1, source_target_pairs={{0,16},{2,18},{4,20},{6,22},{8,24},{10,26},{12,28},{14,30},{16,0},... | collective-permute-start | bytes 995336 | tf_op jit(solution)/shard_map/ppermute | solution.py:239
  101.1 40.8 %collective-permute-start.18 = (bf16[2,1,72,2304]{3,2,1,0:T(8,128)(2,1)S(1)}, bf16[2,1,72,2304]{3,2,1,0:T(8,128)(2,1)S(1)}, u32[]{:S(2)}, u32[]{:S(2)}) collective-permute-start(bf16[2,1,72,2304]{3,2,1,0:T(8,128)(2,1)S(1)} %constant_dynamic-update-slice_fusion.8), channel_id=1, source_target_pairs={{0,8},{2,10},{4,12},{6,14},{8,0},{10,2},{12,4},{14,6},{16,24},{18,... | collective-permute-start | bytes 1990664 | tf_op jit(solution)/shard_map/ppermute | solution.py:239
  105.7 39.9 %collective-permute-start.14 = (bf16[4,2,72,576]{3,2,1,0:T(8,128)(2,1)S(1)}, bf16[4,2,72,576]{3,2,1,0:T(8,128)(2,1)S(1)}, u32[]{:S(2)}, u32[]{:S(2)}) collective-permute-start(bf16[4,2,72,576]{3,2,1,0:T(8,128)(2,1)S(1)} %collective-permute-done.12.refs_1_), channel_id=1, source_target_pairs={{0,2},{2,0},{4,6},{6,4},{8,10},{10,8},{12,14},{14,12},{16,18},{18,... | collective-permute-start | bytes 1990664 | tf_op jit(solution)/shard_map/ppermute | solution.py:239
  105.7 39.6 %collective-permute-start.13 = (bf16[4,2,72,576]{3,2,1,0:T(8,128)(2,1)S(1)}, bf16[4,2,72,576]{3,2,1,0:T(8,128)(2,1)S(1)}, u32[]{:S(2)}, u32[]{:S(2)}) collective-permute-start(bf16[4,2,72,576]{3,2,1,0:T(8,128)(2,1)S(1)} %constant_dynamic-update-slice_fusion.4.refs_0_), channel_id=1, source_target_pairs={{0,2},{2,0},{4,6},{6,4},{8,10},{10,8},{12,14},{14,12},{16,18},{18,... | collective-permute-start | bytes 1990664 | tf_op jit(solution)/shard_map/ppermute | solution.py:239
  106.2 55.7 %collective-permute-start.15 = (bf16[1,1,72,2304]{3,2,1,0:T(8,128)(2,1)S(1)}, bf16[1,1,72,2304]{3,2,1,0:T(8,128)(2,1)S(1)}, u32[]{:S(2)}, u32[]{:S(2)}) collective-permute-start(bf16[1,1,72,2304]{3,2,1,0:T(8,128)(2,1)S(1)} %bitcast.665), channel_id=1, source_target_pairs={{0,16},{2,18},{4,20},{6,22},{8,24},{10,26},{12,28},{14,30},{16,0},... | collective-permute-start | bytes 995336 | tf_op jit(solution)/shard_map/ppermute | solution.py:239
  110.2 34.7 %collective-permute-start.17 = (bf16[4,2,72,576]{3,2,1,0:T(8,128)(2,1)S(1)}, bf16[4,2,72,576]{3,2,1,0:T(8,128)(2,1)S(1)}, u32[]{:S(2)}, u32[]{:S(2)}) collective-permute-start(bf16[4,2,72,576]{3,2,1,0:T(8,128)(2,1)S(1)} %constant_dynamic-update-slice_fusion.10.refs_0_), channel_id=1, source_target_pairs={{0,4},{2,6},{4,0},{6,2},{8,12},{10,14},{12,8},{14,10},{16,20},{18,... | collective-permute-start | bytes 1990664 | tf_op jit(solution)/shard_map/ppermute | solution.py:239
  145.0 38.1 %collective-permute-start.22 = (bf16[4,1,72,2304]{3,2,1,0:T(8,128)(2,1)S(1)}, bf16[4,1,72,2304]{3,2,1,0:T(8,128)(2,1)S(1)}, u32[]{:S(2)}, u32[]{:S(2)}) collective-permute-start(bf16[4,1,72,2304]{3,2,1,0:T(8,128)(2,1)S(1)} %constant_dynamic-update-slice_fusion.12.refs_0_), channel_id=1, source_target_pairs={{0,4},{2,6},{4,0},{6,2},{8,12},{10,14},{12,8},{14,10},{16,20},{18,... | collective-permute-start | bytes 3981320 | tf_op jit(solution)/shard_map/ppermute | solution.py:239
  162.0 19.3 %collective-permute-start.23 = (bf16[2,1,72,2304]{3,2,1,0:T(8,128)(2,1)S(1)}, bf16[2,1,72,2304]{3,2,1,0:T(8,128)(2,1)S(1)}, u32[]{:S(2)}, u32[]{:S(2)}) collective-permute-start(bf16[2,1,72,2304]{3,2,1,0:T(8,128)(2,1)S(1)} %constant_dynamic-update-slice_fusion.14), channel_id=1, source_target_pairs={{0,8},{2,10},{4,12},{6,14},{8,0},{10,2},{12,4},{14,6},{16,24},{18,... | collective-permute-start | bytes 1990664 | tf_op jit(solution)/shard_map/ppermute | solution.py:239
  170.3 16.6 %collective-permute-start.21 = (bf16[256,1152]{1,0:T(8,128)(2,1)S(1)}, bf16[256,1152]{1,0:T(8,128)(2,1)S(1)}, u32[]{:S(2)}, u32[]{:S(2)}) collective-permute-start(bf16[256,1152]{1,0:T(8,128)(2,1)S(1)} %convolution_convert_fusion.5), channel_id=1, source_target_pairs={{0,1},{1,0},{2,3},{3,2},{4,5},{5,4},{6,7},{7,6},{8,9},{9,8},{10,11... | collective-permute-start | bytes 1769480 | tf_op jit(solution)/shard_map/ppermute | solution.py:236
  183.1 40.5 %collective-permute-start.27 = (bf16[4,1,72,2304]{3,2,1,0:T(8,128)(2,1)}, bf16[4,1,72,2304]{3,2,1,0:T(8,128)(2,1)}, u32[]{:S(2)}, u32[]{:S(2)}) collective-permute-start(bf16[4,1,72,2304]{3,2,1,0:T(8,128)(2,1)} %constant_dynamic-update-slice_fusion.16.refs_0_), channel_id=1, source_target_pairs={{0,4},{2,6},{4,0},{6,2},{8,12},{10,14},{12,8},{14,10},{16,20},{18,... | collective-permute-start | bytes 3981320 | tf_op jit(solution)/shard_map/ppermute | solution.py:239
  189.1 19.1 %collective-permute-start.26 = (bf16[256,1152]{1,0:T(8,128)(2,1)}, bf16[256,1152]{1,0:T(8,128)(2,1)}, u32[]{:S(2)}, u32[]{:S(2)}) collective-permute-start(bf16[256,1152]{1,0:T(8,128)(2,1)} %add_convert_fusion.1), channel_id=1, source_target_pairs={{0,1},{1,0},{2,3},{3,2},{4,5},{5,4},{6,7},{7,6},{8,9},{9,8},{10,11... | collective-permute-start | bytes 1769480 | tf_op jit(solution)/shard_map/ppermute | solution.py:236
  235.5 16.0 %collective-permute-start.30 = (bf16[256,1152]{1,0:T(8,128)(2,1)}, bf16[256,1152]{1,0:T(8,128)(2,1)}, u32[]{:S(2)}, u32[]{:S(2)}) collective-permute-start(bf16[256,1152]{1,0:T(8,128)(2,1)} %convolution_convert_fusion.8), channel_id=1, source_target_pairs={{0,1},{1,0},{2,3},{3,2},{4,5},{5,4},{6,7},{7,6},{8,9},{9,8},{10,11... | collective-permute-start | bytes 1769480 | tf_op jit(solution)/shard_map/ppermute | solution.py:236
  253.7 15.9 %collective-permute-start.31 = (bf16[256,1152]{1,0:T(8,128)(2,1)}, bf16[256,1152]{1,0:T(8,128)(2,1)}, u32[]{:S(2)}, u32[]{:S(2)}) collective-permute-start(bf16[256,1152]{1,0:T(8,128)(2,1)} %add_convert_fusion), channel_id=1, source_target_pairs={{0,1},{1,0},{2,3},{3,2},{4,5},{5,4},{6,7},{7,6},{8,9},{9,8},{10,11... | collective-permute-start | bytes 1769480 | tf_op jit(solution)/shard_map/ppermute | solution.py:236
  280.3 22.8 %collective-permute-start.34 = (bf16[1,2,2,2,2,64,2048]{6,5,4,3,2,1,0:T(8,128)(2,1)}, bf16[1,2,2,2,2,64,2048]{6,5,4,3,2,1,0:T(8,128)(2,1)}, u32[]{:S(2)}, u32[]{:S(2)}) collective-permute-start(bf16[1,2,2,2,2,64,2048]{6,5,4,3,2,1,0:T(8,128)(2,1)} %dynamic-slice_bitcast_fusion), channel_id=1, source_target_pairs={{0,2},{2,0},{4,6},{6,4},{8,10},{10,8},{12,14},{14,12},{16,18},{18,... | collective-permute-start | bytes 12582920 | tf_op jit(solution)/shard_map/ppermute | solution.py:239
  282.6 20.4 %collective-permute-start.35 = (bf16[1,2,2,2,24,2048]{5,4,3,2,1,0:T(8,128)(2,1)S(1)}, bf16[1,2,2,2,24,2048]{5,4,3,2,1,0:T(8,128)(2,1)S(1)}, u32[]{:S(2)}, u32[]{:S(2)}) collective-permute-start(bf16[1,2,2,2,24,2048]{5,4,3,2,1,0:T(8,128)(2,1)S(1)} %fusion.30), channel_id=1, source_target_pairs={{0,4},{2,6},{4,0},{6,2},{8,12},{10,14},{12,8},{14,10},{16,20},{18,... | collective-permute-start | bytes 2359304 | tf_op jit(solution)/shard_map/ppermute | solution.py:239
  296.0 18.7 %collective-permute-start.36 = (bf16[256,1152]{1,0:T(8,128)(2,1)S(1)}, bf16[256,1152]{1,0:T(8,128)(2,1)S(1)}, u32[]{:S(2)}, u32[]{:S(2)}) collective-permute-start(bf16[256,1152]{1,0:T(8,128)(2,1)S(1)} %get-tuple-element.220), channel_id=1, source_target_pairs={{0,1},{1,0},{2,3},{3,2},{4,5},{5,4},{6,7},{7,6},{8,9},{9,8},{10,11... | collective-permute-start | bytes 1769480 | tf_op jit(solution)/shard_map/ppermute | solution.py:236
  305.3 13.4 %collective-permute-start.37 = (bf16[1,1,2,64,2048]{4,3,2,1,0:T(8,128)(2,1)S(1)}, bf16[1,1,2,64,2048]{4,3,2,1,0:T(8,128)(2,1)S(1)}, u32[]{:S(2)}, u32[]{:S(2)}) collective-permute-start(bf16[1,1,2,64,2048]{4,3,2,1,0:T(8,128)(2,1)S(1)} %fusion.54), channel_id=1, source_target_pairs={{0,4},{2,6},{4,0},{6,2},{8,12},{10,14},{12,8},{14,10},{16,20},{18,... | collective-permute-start | bytes 1572872 | tf_op jit(solution)/shard_map/ppermute | solution.py:239
  325.3 19.6 %collective-permute-start.40 = (bf16[1,2,2,2,2,64,1152]{6,5,4,3,2,1,0:T(8,128)(2,1)}, bf16[1,2,2,2,2,64,1152]{6,5,4,3,2,1,0:T(8,128)(2,1)}, u32[]{:S(2)}, u32[]{:S(2)}) collective-permute-start(bf16[1,2,2,2,2,64,1152]{6,5,4,3,2,1,0:T(8,128)(2,1)} %dynamic-slice_bitcast_fusion.1), channel_id=1, source_target_pairs={{0,2},{2,0},{4,6},{6,4},{8,10},{10,8},{12,14},{14,12},{16,18},{18,... | collective-permute-start | bytes 7077896 | tf_op jit(solution)/shard_map/ppermute | solution.py:239
  330.8 14.1 %collective-permute-start.39 = (bf16[1,1,2,64,2048]{4,3,2,1,0:T(8,128)(2,1)S(1)}, bf16[1,1,2,64,2048]{4,3,2,1,0:T(8,128)(2,1)S(1)}, u32[]{:S(2)}, u32[]{:S(2)}) collective-permute-start(bf16[1,1,2,64,2048]{4,3,2,1,0:T(8,128)(2,1)S(1)} %copy-done.73), channel_id=1, source_target_pairs={{0,4},{2,6},{4,0},{6,2},{8,12},{10,14},{12,8},{14,10},{16,20},{18,... | collective-permute-start | bytes 1572872 | tf_op jit(solution)/shard_map/ppermute | solution.py:239
  340.5 19.7 %collective-permute-start.42 = (bf16[256,1152]{1,0:T(8,128)(2,1)}, bf16[256,1152]{1,0:T(8,128)(2,1)}, u32[]{:S(2)}, u32[]{:S(2)}) collective-permute-start(bf16[256,1152]{1,0:T(8,128)(2,1)} %convolution_convert_fusion.6), channel_id=1, source_target_pairs={{0,1},{1,0},{2,3},{3,2},{4,5},{5,4},{6,7},{7,6},{8,9},{9,8},{10,11... | collective-permute-start | bytes 1769480 | tf_op jit(solution)/shard_map/ppermute | solution.py:236
  350.9 13.7 %collective-permute-start.43 = (bf16[1,1,2,64,2048]{4,3,2,1,0:T(8,128)(2,1)}, bf16[1,1,2,64,2048]{4,3,2,1,0:T(8,128)(2,1)}, u32[]{:S(2)}, u32[]{:S(2)}) collective-permute-start(bf16[1,1,2,64,2048]{4,3,2,1,0:T(8,128)(2,1)} %fusion.56), channel_id=1, source_target_pairs={{0,4},{2,6},{4,0},{6,2},{8,12},{10,14},{12,8},{14,10},{16,20},{18,... | collective-permute-start | bytes 1572872 | tf_op jit(solution)/shard_map/ppermute | solution.py:239
  360.1 253.7 %reduce-scatter.3.cloned.1.call-start = ((), (), s32[]{:S(2)}) async-start(), calls=%async_computation.3 | async-start | bytes 5640192 | tf_op jit(solution)/shard_map/reduce_scatter | solution.py:656
  367.7 16.8 %collective-permute-start.44 = (bf16[1,1,2,64,2048]{4,3,2,1,0:T(8,128)(2,1)S(1)}, bf16[1,1,2,64,2048]{4,3,2,1,0:T(8,128)(2,1)S(1)}, u32[]{:S(2)}, u32[]{:S(2)}) collective-permute-start(bf16[1,1,2,64,2048]{4,3,2,1,0:T(8,128)(2,1)S(1)} %fusion.57), channel_id=1, source_target_pairs={{0,4},{2,6},{4,0},{6,2},{8,12},{10,14},{12,8},{14,10},{16,20},{18,... | collective-permute-start | bytes 1572872 | tf_op jit(solution)/shard_map/ppermute | solution.py:239
  370.5 16.6 %collective-permute-start.45 = (bf16[1,24,2048]{2,1,0:T(8,128)(2,1)S(1)}, bf16[1,24,2048]{2,1,0:T(8,128)(2,1)S(1)}, u32[]{:S(2)}, u32[]{:S(2)}) collective-permute-start(bf16[1,24,2048]{2,1,0:T(8,128)(2,1)S(1)} %fusion.92), channel_id=1, source_target_pairs={{0,16},{2,18},{4,20},{6,22},{8,24},{10,26},{12,28},{14,30},{16,0},... | collective-permute-start | bytes 294920 | tf_op jit(solution)/shard_map/ppermute | solution.py:239
  402.4 14.4 %collective-permute-start.48 = (bf16[1,8,72,576]{3,2,1,0:T(8,128)(2,1)S(1)}, bf16[1,8,72,576]{3,2,1,0:T(8,128)(2,1)S(1)}, u32[]{:S(2)}, u32[]{:S(2)}) collective-permute-start(bf16[1,8,72,576]{3,2,1,0:T(8,128)(2,1)S(1)} %get-tuple-element.238), channel_id=1, source_target_pairs={{0,2},{2,0},{4,6},{6,4},{8,10},{10,8},{12,14},{14,12},{16,18},{18,... | collective-permute-start | bytes 1990664 | tf_op jit(solution)/shard_map/ppermute | solution.py:239
  402.5 14.3 %collective-permute-start.47 = (bf16[1,2,1,64,2048]{4,3,1,2,0:T(8,128)(2,1)S(1)}, bf16[1,2,1,64,2048]{4,3,1,2,0:T(8,128)(2,1)S(1)}, u32[]{:S(2)}, u32[]{:S(2)}) collective-permute-start(bf16[1,2,1,64,2048]{4,3,1,2,0:T(8,128)(2,1)S(1)} %fusion.45), channel_id=1, source_target_pairs={{0,1},{1,0},{2,3},{3,2},{4,5},{5,4},{6,7},{7,6},{8,9},{9,8},{10,11... | collective-permute-start | bytes 1572872 | tf_op jit(solution)/shard_map/ppermute | solution.py:236
  418.6 13.7 %collective-permute-start.49 = (bf16[1,2,1,64,2048]{4,3,1,2,0:T(8,128)(2,1)S(1)}, bf16[1,2,1,64,2048]{4,3,1,2,0:T(8,128)(2,1)S(1)}, u32[]{:S(2)}, u32[]{:S(2)}) collective-permute-start(bf16[1,2,1,64,2048]{4,3,1,2,0:T(8,128)(2,1)S(1)} %fusion.43), channel_id=1, source_target_pairs={{0,1},{1,0},{2,3},{3,2},{4,5},{5,4},{6,7},{7,6},{8,9},{9,8},{10,11... | collective-permute-start | bytes 1572872 | tf_op jit(solution)/shard_map/ppermute | solution.py:236
  434.8 18.6 %collective-permute-start.51 = (bf16[1,2,64,2048]{3,2,1,0:T(8,128)(2,1)S(1)}, bf16[1,2,64,2048]{3,2,1,0:T(8,128)(2,1)S(1)}, u32[]{:S(2)}, u32[]{:S(2)}) collective-permute-start(bf16[1,2,64,2048]{3,2,1,0:T(8,128)(2,1)S(1)} %fusion.41), channel_id=1, source_target_pairs={{0,8},{2,10},{4,12},{6,14},{8,0},{10,2},{12,4},{14,6},{16,24},{18,... | collective-permute-start | bytes 1572872 | tf_op jit(solution)/shard_map/ppermute | solution.py:239
  462.8 23.0 %collective-permute-start.54 = (bf16[3,8,72,576]{3,2,1,0:T(8,128)(2,1)}, bf16[3,8,72,576]{3,2,1,0:T(8,128)(2,1)}, u32[]{:S(2)}, u32[]{:S(2)}) collective-permute-start(bf16[3,8,72,576]{3,2,1,0:T(8,128)(2,1)} %get-tuple-element.248), channel_id=1, source_target_pairs={{0,2},{2,0},{4,6},{6,4},{8,10},{10,8},{12,14},{14,12},{16,18},{18,... | collective-permute-start | bytes 5971976 | tf_op jit(solution)/shard_map/ppermute | solution.py:239
  468.5 16.0 %collective-permute-start.52 = (bf16[256,1152]{1,0:T(8,128)(2,1)}, bf16[256,1152]{1,0:T(8,128)(2,1)}, u32[]{:S(2)}, u32[]{:S(2)}) collective-permute-start(bf16[256,1152]{1,0:T(8,128)(2,1)} %fusion.6), channel_id=1, source_target_pairs={{0,1},{1,0},{2,3},{3,2},{4,5},{5,4},{6,7},{7,6},{8,9},{9,8},{10,11... | collective-permute-start | bytes 1769480 | tf_op jit(solution)/shard_map/ppermute | solution.py:236
  470.0 15.7 %collective-permute-start.53 = (bf16[1,2,2,64,1152]{4,3,2,1,0:T(8,128)(2,1)}, bf16[1,2,2,64,1152]{4,3,2,1,0:T(8,128)(2,1)}, u32[]{:S(2)}, u32[]{:S(2)}) collective-permute-start(bf16[1,2,2,64,1152]{4,3,2,1,0:T(8,128)(2,1)} %fusion.39), channel_id=1, source_target_pairs={{0,4},{2,6},{4,0},{6,2},{8,12},{10,14},{12,8},{14,10},{16,20},{18,... | collective-permute-start | bytes 1769480 | tf_op jit(solution)/shard_map/ppermute | solution.py:239
  487.8 18.4 %collective-permute-start.55 = (bf16[1,2,2,64,1152]{4,3,2,1,0:T(8,128)(2,1)}, bf16[1,2,2,64,1152]{4,3,2,1,0:T(8,128)(2,1)}, u32[]{:S(2)}, u32[]{:S(2)}) collective-permute-start(bf16[1,2,2,64,1152]{4,3,2,1,0:T(8,128)(2,1)} %fusion.38), channel_id=1, source_target_pairs={{0,4},{2,6},{4,0},{6,2},{8,12},{10,14},{12,8},{14,10},{16,20},{18,... | collective-permute-start | bytes 1769480 | tf_op jit(solution)/shard_map/ppermute | solution.py:239
  490.9 15.3 %collective-permute-start.56 = (bf16[1,2,72,576]{3,2,1,0:T(8,128)(2,1)}, bf16[1,2,72,576]{3,2,1,0:T(8,128)(2,1)S(1)}, u32[]{:S(2)}, u32[]{:S(2)}) collective-permute-start(bf16[1,2,72,576]{3,2,1,0:T(8,128)(2,1)} %fusion.69), channel_id=1, source_target_pairs={{0,8},{2,10},{4,12},{6,14},{8,0},{10,2},{12,4},{14,6},{16,24},{18,... | collective-permute-start | bytes 497672 | tf_op jit(solution)/shard_map/ppermute | solution.py:239
  507.5 33.9 %collective-permute-start.60 = (bf16[3,2,2,72,576]{4,3,2,1,0:T(8,128)(2,1)}, bf16[3,2,2,72,576]{4,3,2,1,0:T(8,128)(2,1)}, u32[]{:S(2)}, u32[]{:S(2)}) collective-permute-start(bf16[3,2,2,72,576]{4,3,2,1,0:T(8,128)(2,1)} %pad_maximum_fusion.6), channel_id=1, source_target_pairs={{0,4},{2,6},{4,0},{6,2},{8,12},{10,14},{12,8},{14,10},{16,20},{18,... | collective-permute-start | bytes 2985992 | tf_op jit(solution)/shard_map/ppermute | solution.py:239
  510.1 33.3 %collective-permute-start.61 = (bf16[256,1152]{1,0:T(8,128)(2,1)}, bf16[256,1152]{1,0:T(8,128)(2,1)S(1)}, u32[]{:S(2)}, u32[]{:S(2)}) collective-permute-start(bf16[256,1152]{1,0:T(8,128)(2,1)} %get-tuple-element.258), channel_id=1, source_target_pairs={{0,1},{1,0},{2,3},{3,2},{4,5},{5,4},{6,7},{7,6},{8,9},{9,8},{10,11... | collective-permute-start | bytes 1769480 | tf_op jit(solution)/shard_map/ppermute | solution.py:236
  519.0 24.5 %collective-permute-start.62 = (bf16[1,64,2048]{2,1,0:T(8,128)(2,1)S(1)}, bf16[1,64,2048]{2,1,0:T(8,128)(2,1)S(1)}, u32[]{:S(2)}, u32[]{:S(2)}) collective-permute-start(bf16[1,64,2048]{2,1,0:T(8,128)(2,1)S(1)} %fusion.60), channel_id=1, source_target_pairs={{0,16},{2,18},{4,20},{6,22},{8,24},{10,26},{12,28},{14,30},{16,0},... | collective-permute-start | bytes 786440 | tf_op jit(solution)/shard_map/ppermute | solution.py:239
  530.6 21.9 %collective-permute-start.63 = (bf16[16,8,1152]{2,1,0:T(8,128)(2,1)S(1)}, bf16[16,8,1152]{2,1,0:T(8,128)(2,1)S(1)}, u32[]{:S(2)}, u32[]{:S(2)}) collective-permute-start(bf16[16,8,1152]{2,1,0:T(8,128)(2,1)S(1)} %pad_maximum_fusion.11), channel_id=1, source_target_pairs={{0,8},{2,10},{4,12},{6,14},{8,0},{10,2},{12,4},{14,6},{16,24},{18,... | collective-permute-start | bytes 884744 | tf_op jit(solution)/shard_map/ppermute | solution.py:239
  545.1 29.9 %collective-permute-start.64 = (bf16[1,2,2,64,1152]{4,3,2,1,0:T(8,128)(2,1)S(1)}, bf16[1,2,2,64,1152]{4,3,2,1,0:T(8,128)(2,1)S(1)}, u32[]{:S(2)}, u32[]{:S(2)}) collective-permute-start(bf16[1,2,2,64,1152]{4,3,2,1,0:T(8,128)(2,1)S(1)} %fusion.37), channel_id=1, source_target_pairs={{0,1},{1,0},{2,3},{3,2},{4,5},{5,4},{6,7},{7,6},{8,9},{9,8},{10,11... | collective-permute-start | bytes 1769480 | tf_op jit(solution)/shard_map/ppermute | solution.py:236
  545.6 29.4 %collective-permute-start.65 = (bf16[3,2,72,576]{3,2,1,0:T(8,128)(2,1)S(1)}, bf16[3,2,72,576]{3,2,1,0:T(8,128)(2,1)S(1)}, u32[]{:S(2)}, u32[]{:S(2)}) collective-permute-start(bf16[3,2,72,576]{3,2,1,0:T(8,128)(2,1)S(1)} %pad_maximum_fusion.8), channel_id=1, source_target_pairs={{0,8},{2,10},{4,12},{6,14},{8,0},{10,2},{12,4},{14,6},{16,24},{18,... | collective-permute-start | bytes 1493000 | tf_op jit(solution)/shard_map/ppermute | solution.py:239
  547.8 19.5 %collective-permute-start.66 = (bf16[1,72,576]{2,1,0:T(8,128)(2,1)S(1)}, bf16[1,72,576]{2,1,0:T(8,128)(2,1)S(1)}, u32[]{:S(2)}, u32[]{:S(2)}) collective-permute-start(bf16[1,72,576]{2,1,0:T(8,128)(2,1)S(1)} %fusion.103), channel_id=1, source_target_pairs={{0,16},{2,18},{4,20},{6,22},{8,24},{10,26},{12,28},{14,30},{16,0},... | collective-permute-start | bytes 248840 | tf_op jit(solution)/shard_map/ppermute | solution.py:239
  578.7 14.6 %collective-permute-start.69 = (bf16[3,72,576]{2,1,0:T(8,128)(2,1)S(1)}, bf16[3,72,576]{2,1,0:T(8,128)(2,1)S(1)}, u32[]{:S(2)}, u32[]{:S(2)}) collective-permute-start(bf16[3,72,576]{2,1,0:T(8,128)(2,1)S(1)} %pad_maximum_fusion.12), channel_id=1, source_target_pairs={{0,16},{2,18},{4,20},{6,22},{8,24},{10,26},{12,28},{14,30},{16,0},... | collective-permute-start | bytes 746504 | tf_op jit(solution)/shard_map/ppermute | solution.py:239
  582.0 14.9 %collective-permute-start.68 = (bf16[1,2,64,1152]{3,2,1,0:T(8,128)(2,1)S(1)}, bf16[1,2,64,1152]{3,2,1,0:T(8,128)(2,1)S(1)}, u32[]{:S(2)}, u32[]{:S(2)}) collective-permute-start(bf16[1,2,64,1152]{3,2,1,0:T(8,128)(2,1)S(1)} %fusion.53), channel_id=1, source_target_pairs={{0,8},{2,10},{4,12},{6,14},{8,0},{10,2},{12,4},{14,6},{16,24},{18,... | collective-permute-start | bytes 884744 | tf_op jit(solution)/shard_map/ppermute | solution.py:239
  (153 other events, 1319.5 us)
Sparse Core Ops, SparseCore 0:
  35.6 125.5 all-gather.5
  164.1 71.7 all-gather.3
  360.2 87.4 reduce-scatter.4
  473.4 101.1 reduce-scatter.2

commit v3 on v2

--- a/solution.py
+++ b/solution.py
@@ -442,6 +442,13 @@
             bin_onehot.astype(bf16), time_table, preferred_element_type=f32
         ) + jnp.dot(class_onehot.astype(bf16), class_table, preferred_element_type=f32)
         cond_act = jax.nn.silu(condition).astype(bf16)
+        def near_rows(values):
+            cut = values.reshape((-1, ROWS, image_count) + values.shape[1:])
+            return cut.swapaxes(1, 2).reshape(values.shape)
+
+        end_rows = [
+            near_rows(values) for values in (cond_act, condition, bin_onehot, class_onehot)
+        ]
         local_rows = w_ada.shape[1]
         wide_bias = lax.dynamic_update_slice(
             jnp.zeros((b_ada.shape[0], width), f32), b_ada, (0, me * local_rows)
@@ -492,6 +499,7 @@
         wide_up = Wide(tie(w_up[None, None], pair_b))
         normed_one, inverse_one = layer_norm(inputs)
         act_one = mark((normed_one * (1.0 + scale_one) + shift_one).astype(bf16))
+        last.extend(end_rows)
 
         def four(near, with_row):
             with_row = mark(after(with_row))
@@ -583,7 +591,7 @@
                 * (target * inv_map * inv_target - cosine * inv_map * inv_map * mapped)
             ).astype(bf16)
         )
-        grad_bthird = jnp.sum(grad_mapped.astype(f32), axis=0)
+        grad_bthird = jnp.sum(grad_mapped.astype(f32), axis=0, keepdims=True)
         three = Scatter([mark(dot(after(grad_mapped), act_ptwo, 0, 0).astype(bf16))], True)
         fly(other_out)
         land()
@@ -591,7 +599,7 @@
         grad_pre_two = mark(
             (dot(after(grad_mapped), proj_three, 1, 0) * silu_grad(pre_two)).astype(bf16)
         )
-        grad_bsecond = jnp.sum(grad_pre_two.astype(f32), axis=0)
+        grad_bsecond = jnp.sum(grad_pre_two.astype(f32), axis=0, keepdims=True)
         two = Scatter([mark(dot(after(grad_pre_two), act_pone, 0, 0).astype(bf16))], True)
         land()
         two.send(1)
@@ -599,13 +607,13 @@
         grad_pre_one = mark(
             (dot(after(grad_pre_two), proj_two, 1, 0) * silu_grad(pre_one)).astype(bf16)
         )
-        grad_bfirst = jnp.sum(grad_pre_one.astype(f32), axis=0)
+        grad_bfirst = jnp.sum(grad_pre_one.astype(f32), axis=0, keepdims=True)
         grad_feed = mark(dot(after(grad_pre_one), proj_one, 1, 0))
 
         grad_output = pick(cotangent, side).astype(f32) + grad_feed.astype(bf16).astype(f32)
         grad_branch = mark((gate_two * grad_output).astype(bf16))
-        grad_gate_two = jnp.sum(grad_output * branch, axis=0)
-        grad_bdown = jnp.sum(grad_branch.astype(f32), axis=0)
+        grad_gate_two = jnp.sum(grad_output * branch, axis=0, keepdims=True)
+        grad_bdown = jnp.sum(grad_branch.astype(f32), axis=0, keepdims=True)
         land()
         other_branch = fly(swap_x(grad_branch))
         two.send(CORES, 0, 4)
@@ -627,8 +635,8 @@
         three.send(far[-1])
         two.send(CORES, 2, 4)
         grad_act_two = mark(dot(after(hidden_grad_own), full_up, 1, 1))
-        grad_bunits = jnp.sum(hidden_grad_own.astype(f32), axis=0) + jnp.sum(
-            hidden_grad_other.astype(f32), axis=0
+        grad_bunits = jnp.sum(hidden_grad_own.astype(f32), axis=0, keepdims=True) + jnp.sum(
+            hidden_grad_other.astype(f32), axis=0, keepdims=True
         )
         branch_both = jnp.concatenate((grad_branch, other_branch), axis=0)
         active_both = jnp.concatenate((active_own, active_other), axis=0)
@@ -639,23 +647,25 @@
         for mask in far[-2::-1]:
             three.send(mask)
         grad_act_two = after(grad_act_two) + arrived.astype(f32)
-        grad_shift_two = jnp.sum(grad_act_two, axis=0)
-        grad_scale_two = jnp.sum(grad_act_two * normed_two, axis=0)
+        grad_shift_two = jnp.sum(grad_act_two, axis=0, keepdims=True)
+        grad_scale_two = jnp.sum(grad_act_two * normed_two, axis=0, keepdims=True)
         grad_first_sum = grad_output + norm_back(
             grad_act_two * (1.0 + scale_two), normed_two, inverse_two
         )
 
         grad_attention = mark((gate_one * grad_first_sum).astype(bf16))
-        grad_gate_one = jnp.sum(grad_first_sum * attention, axis=0)
-        grad_bout = jnp.sum(grad_attention.astype(f32), axis=0)
+        grad_gate_one = jnp.sum(grad_first_sum * attention, axis=0, keepdims=True)
+        grad_bout = jnp.sum(grad_attention.astype(f32), axis=0, keepdims=True)
         land()
         other_attention = fly(swap_x(grad_attention))
+        one.send(CORES, 0, 2)
         act_both = jnp.concatenate((act_two, other_two), axis=0)
         hidden_both = jnp.concatenate((hidden_grad_own, hidden_grad_other), axis=0)
         grad_wup = mark(dot(after(act_both), hidden_both, 0, 0).astype(bf16))
         own_up = lax.psum_scatter(grad_wup, "dp", scatter_dimension=0, tiled=True)
         land()
         two.send(0, 0, 2)
+        one.send(CORES, 1, 2)
         attention_both = mark(
             jnp.concatenate((after(grad_attention), other_attention), axis=0)
         )
@@ -670,9 +680,10 @@
         grad_three = mark(
             attend_back(queries, key_heads, val_heads, log_total, after(grad_mixed), seq_len)
         )
-        grad_bquery = jnp.sum(grad_three[0].astype(f32), axis=0)
-        grad_bvalue = jnp.sum(grad_three[2].astype(f32), axis=0)
-        land()
+        grad_bquery = jnp.sum(grad_three[0].astype(f32), axis=0, keepdims=True)
+        grad_bvalue = jnp.sum(grad_three[2].astype(f32), axis=0, keepdims=True)
+        land()
+        one.send(0)
         out.send(CORES)
         two.send(far[-1])
 
@@ -687,104 +698,86 @@
         grad_act_one = mark(part_one(0))
         land()
         arrived = fly(swap_x(outgoing))
-        one.send(CORES, 0, 2)
         halves = split_grads(act_flat, after(grad_three), my_core, planes * ROWS)
         qkv = Scatter.from_halves(halves[0], mark(halves[1]))
-        land()
-        one.send(CORES, 1, 2)
+        for mask in far[-2::-1]:
+            two.send(mask)
+        land()
+        one.send(far[-1])
         out.send(far[-1])
         normed_own, inverse_own = normed_one[0], inverse_one[0]
         grad_act_one = after(grad_act_one) + arrived.astype(f32)
-        grad_shift_one = jnp.sum(grad_act_one, axis=0)
-        grad_scale_one = jnp.sum(grad_act_one * normed_own, axis=0)
+        grad_shift_one = jnp.sum(grad_act_one, axis=0, keepdims=True)
+        grad_scale_one = jnp.sum(grad_act_one * normed_own, axis=0, keepdims=True)
         grad_own = grad_first_sum + norm_back(
             grad_act_one * (1.0 + scale_own), normed_own, inverse_own
         )
-        def rows_of(values):
-            short = -values.size % width
-            return jnp.pad(values, (0, short)).reshape(-1, width)
-
-        grad_inner = jnp.concatenate((grad_bquery, grad_bvalue, grad_bunits))
         sent = [
-            jnp.stack(
-                (
-                    grad_shift_one,
-                    grad_scale_one,
-                    grad_gate_one,
-                    grad_shift_two,
-                    grad_scale_two,
-                    grad_gate_two,
-                ),
-                axis=0,
-            )
-        ] + [
-            rows_of(values)
-            for values in (
-                grad_bout,
-                grad_bdown,
-                grad_bfirst,
-                grad_bsecond,
-                grad_bthird,
-                grad_inner,
-            )
+            grad_shift_one,
+            grad_scale_one,
+            grad_gate_one,
+            grad_shift_two,
+            grad_scale_two,
+            grad_gate_two,
+            grad_bout,
+            grad_bdown,
+            grad_bfirst,
+            grad_bsecond,
+            grad_bthird,
+            grad_bquery,
+            grad_bvalue,
+            grad_bunits,
         ]
-        heights = [piece.shape[0] for piece in sent]
-        sent = jnp.concatenate(sent, axis=0).astype(bf16)
+        starts = [0]
+        for piece in sent:
+            starts.append(starts[-1] + piece.shape[1])
+        sent = jnp.concatenate([piece.astype(bf16) for piece in sent], axis=1)
         mark(sent)
         land()
-        row_sent = fly(swap(sent, near_order[0]))
-        land()
+        row_sent = swap(sent, near_order[0])
         qkv.send(CORES)
-        near_sent = mark(jnp.stack((after(sent), row_sent), axis=1))
+        for mask in far[-2::-1]:
+            one.send(mask)
+            out.send(mask)
+        near_sent = mark(jnp.concatenate((sent, after(row_sent)), axis=0))
         side_sent = swap_x(near_sent)
-        grad_other = fly(swap_x(tie(grad_own.astype(bf16), near_sent)))
-        near_sent = ordered(near_sent, after(side_sent))
-        near_sent = mark(jnp.moveaxis(near_sent, 0, 2).reshape(sent.shape[0], -1, width))
-        arrived = swap(near_sent, near_order[1])
-        for mask in far[-2::-1]:
-            two.send(mask)
-        near_sent = mark(jnp.concatenate((near_sent, after(arrived)), axis=1))
-        land()
-        arrived = fly(swap(near_sent, near_order[2]))
-        one.send(0)
-        qkv.send(far[-1])
-        for mask in far[-2::-1]:
-            out.send(mask)
-        land()
-        near_sent = mark(jnp.concatenate((after(near_sent), arrived), axis=1))
-        for mask in near_order[3:]:
-            arrived = fly(swap(near_sent, mask))
-            near_sent = mark(jnp.concatenate((near_sent, after(arrived)), axis=1))
-        one.send(far[-1])
+        grad_other = swap_x(tie(grad_own.astype(bf16), near_sent))
+        near_sent = mark(ordered(near_sent, after(side_sent)).reshape(-1, sent.shape[1]))
+        for k, mask in enumerate(near_order[1:]):
+            arrived = swap(near_sent, mask)
+            near_sent = mark(jnp.concatenate((near_sent, after(arrived)), axis=0))
+            if k == 0:
+                land()
+                qkv.send(far[-1])
+        land()
         for mask in far[-2::-1]:
             qkv.send(mask)
-        land()
-        for mask in far[-2::-1]:
-            one.send(mask)
         near_sent = after(near_sent)
-        every_mods = near_sent[: heights[0]]
-        totals = jnp.sum(near_sent.astype(f32), axis=1)
-        by_side = near_sent.reshape(near_sent.shape[0], dp, mp, width)[-heights[-1] :]
-        inner_total = jnp.sum(pick(by_side, side, 2).astype(f32), axis=1).reshape(-1)
-        sum_bada = lax.dynamic_slice_in_dim(
-            totals[: heights[0]], me * local_rows, local_rows, 1
-        )
-
-        def own_part(index, count, parts):
-            start = sum(heights[: index + 1])
-            values = totals[start : start + heights[index + 1]].reshape(-1)
+        def own_part(index, count, parts, values):
+            held = values[:, starts[index] : starts[index] + count * parts]
             at = me if parts == dp else me * mp + side
-            return lax.dynamic_slice_in_dim(values, at * count, count, 0)
-
-        sum_bout = own_part(0, thin, dp)
-        sum_bdown = own_part(1, thin, dp)
-        sum_bfirst = own_part(2, hidden_size, dp * mp)
-        sum_bsecond = own_part(3, hidden_size, dp * mp)
-        sum_bthird = own_part(4, b_third.shape[0], dp * mp)
-        sum_inner = lax.dynamic_slice_in_dim(inner_total, me * inner_size, inner_size, 0)[None]
-        sum_wada = jnp.einsum("bd,tbe->tde", cond_act, every_mods, preferred_element_type=f32)
-        grad_cond = jnp.einsum("tbe,tde->bd", every_mods, w_ada, preferred_element_type=f32)
+            return lax.dynamic_slice_in_dim(held, at * count, count, 1)
+
+        totals = jnp.sum(near_sent.astype(f32), axis=0, keepdims=True)
+        same_side = jnp.arange(near_sent.shape[0]) // ROWS % image_count == side
+        inner_total = jnp.sum(
+            jnp.where(same_side[:, None], near_sent[:, starts[11] :].astype(f32), 0.0),
+            axis=0,
+            keepdims=True,
+        )
+        sum_bada = jnp.concatenate([own_part(t, thin, dp, totals) for t in range(6)], axis=0)
+        sum_bout = own_part(6, thin, dp, totals)[0]
+        sum_bdown = own_part(7, thin, dp, totals)[0]
+        sum_bfirst = own_part(8, hidden_size, dp * mp, totals)[0]
+        sum_bsecond = own_part(9, hidden_size, dp * mp, totals)[0]
+        sum_bthird = own_part(10, b_third.shape[0], dp * mp, totals)[0]
+        sum_inner = lax.dynamic_slice_in_dim(inner_total, me * inner_size, inner_size, 1)
+        cond_act, condition, bin_onehot, class_onehot = end_rows
+        every_mods = [near_sent[:, starts[t] : starts[t + 1]] for t in range(6)]
+        sum_wada = jnp.stack([dot(cond_act, mods, 0, 0) for mods in every_mods], axis=0)
+        grad_cond = sum(dot(mods, w_ada[t], 1, 1) for t, mods in enumerate(every_mods))
         grad_cond = grad_cond * silu_grad(condition)
+        mark(sum_wada)
         sum_time = jnp.einsum(
             "bn,bd->nd", bin_onehot.astype(f32), grad_cond, precision=lax.Precision.HIGHEST
         )

time: 627 us -> 620 us (0.989)
  waiting for transfers between devices: 239 us -> 221 us
  local copies, waits for them, and re-layouts: 69.3 us -> 81.6 us
    ppermute x56, waiting for transfers between devices: 207 us -> 187 us  [swap(): return lax.ppermute(value, 'dp', [(k, k ^ mask) for k in range(dp)])]
    convert_element_type x0 -> x14, local copies, waits for them, and re-layouts: none -> 7.7 us  [shards(): sent = jnp.concatenate([piece.astype(bf16) for piece in sent], axis=1)]
    dot_general x31 -> x43, matrix products: 86 us -> 83.4 us  [dot(): lax.dot_general(left, right, (((left_axis,), (right_axis,)), ((), ())), p...]
    unnamed x263 -> x318, local copies, waits for them, and re-layouts: 16.4 us -> 18.6 us
  transfers between devices with their start and end apart: 75 -> 75, of which waited for: 37 -> 34; matrix products, arithmetic and copies ran while one was open for 35% -> 37% of each run, Pallas kernels for 7% -> 7%
where the time goes in v3:
time: 620 us; the launch traced here: 613 us
  waiting for transfers between devices  221 us (36%)
  matrix products  87.7 us (14%)
  other arithmetic  83.7 us (14%)
  local copies, waits for them, and re-layouts  81.6 us (13%)
  starting transfers between devices  78.3 us (13%)
  Pallas kernels  45.1 us (7%)
  between operations  16.4 us (3%)
    ppermute x56, waiting for transfers between devices, swap(): return lax.ppermute(value, 'dp', [(k, k ^ mask) for k in range(dp)])  187 us
    dot_general x43, matrix products, dot(): lax.dot_general(left, right, (((left_axis,), (right_axis,)), ((), ())), p...  83.4 us
    ppermute x56, starting transfers between devices, swap(): return lax.ppermute(value, 'dp', [(k, k ^ mask) for k in range(dp)])  60 us
    ppermute x15, waiting for transfers between devices, swap_x(): return lax.ppermute(value, 'mp', [(k, k ^ 1) for k in range(mp)])  33.3 us
    convert_element_type x25, other arithmetic, send(): outgoing.append(sum((half.astype(f32) for half in halves)).astype(bf16))  30.6 us
    pallas_call x4, Pallas kernels, place_pieces(): pl.pallas_call(body, in_specs=[pl.BlockSpec(memory_space=pltpu.SMEM)] + [...  19.3 us
    unnamed x318, local copies, waits for them, and re-layouts  18.6 us
    ppermute x15, starting transfers between devices, swap_x(): return lax.ppermute(value, 'mp', [(k, k ^ 1) for k in range(mp)])  18 us
  transfers between devices with their start and end apart: 75, of which 34 were waited for; matrix products, arithmetic and copies ran while one was open for 37% of the time, Pallas kernels for 7%

profile of v3, /device:TPU:0, one launch (start us, length us, event | category | flops | bytes accessed | tf_op | source)
XLA Modules:
  0.0 613.5 jit_solution(12382019911942287213)
XLA Ops:
  16.6 7.4 %collective-permute-done.1 = f32[2,640]{1,0:T(2,128)S(1)} collective-permute-done((f32[2,640]{1,0:T(2,128)S(1)}, f32[2,640]{1,0:T(2,128)S(1)}, u32[]{:S(2)}, u32[]{:S(2)}) %collective-permute-start.1) | collective-permute-done | bytes 5152 | tf_op jit(solution)/shard_map/ppermute | solution.py:239
  29.7 5.6 collective-permute-done.5
  46.0 3.4 collective-permute-start.9
  49.4 8.0 %collective-permute-done.7 = bf16[6,8,1152]{2,1,0:T(8,128)(2,1)S(1)} collective-permute-done((bf16[6,8,1152]{2,1,0:T(8,128)(2,1)S(1)}, bf16[6,8,1152]{2,1,0:T(8,128)(2,1)S(1)}, u32[]{:S(2)}, u32[]{:S(2)}) %collective-permute-start.7) | collective-permute-done | bytes 110624 | tf_op jit(solution)/shard_map/ppermute | solution.py:239
  57.5 8.0 %collective-permute-done.9 = bf16[1,2,72,576]{3,2,1,0:T(8,128)(2,1)S(1)} collective-permute-done((bf16[1,2,72,576]{3,2,1,0:T(8,128)(2,1)S(1)}, bf16[1,2,72,576]{3,2,1,0:T(8,128)(2,1)S(1)}, u32[]{:S(2)}, u32[]{:S(2)}) %collective-permute-start.9) | collective-permute-done | bytes 165920 | tf_op jit(solution)/shard_map/ppermute | solution.py:239
  73.1 26.5 %collective-permute-done.11 = bf16[1,1,72,2304]{3,2,1,0:T(8,128)(2,1)S(1)} collective-permute-done((bf16[1,1,72,2304]{3,2,1,0:T(8,128)(2,1)S(1)}, bf16[1,1,72,2304]{3,2,1,0:T(8,128)(2,1)S(1)}, u32[]{:S(2)}, u32[]{:S(2)}) %collective-permute-start.11) | collective-permute-done | bytes 331808 | tf_op jit(solution)/shard_map/ppermute | solution.py:239
  99.6 3.9 collective-permute-start.18
  110.1 28.8 %collective-permute-done.18 = bf16[2,1,72,2304]{3,2,1,0:T(8,128)(2,1)S(1)} collective-permute-done((bf16[2,1,72,2304]{3,2,1,0:T(8,128)(2,1)S(1)}, bf16[2,1,72,2304]{3,2,1,0:T(8,128)(2,1)S(1)}, u32[]{:S(2)}, u32[]{:S(2)}) %collective-permute-start.18) | collective-permute-done | bytes 663584 | tf_op jit(solution)/shard_map/ppermute | solution.py:239
  139.1 3.9 collective-permute-done.17.refs_1_
  145.1 6.0 shard_map.357
  154.2 6.0 shard_map.358
  161.6 7.4 %shard_map.359 = (bf16[512,576]{1,0:T(8,128)(2,1)S(1)}, f32[512,8]{1,0:T(8,128)S(1)}) custom-call(bf16[512,576]{1,0:T(8,128)(2,1)S(1)} %fusion.37.q_ref, bf16[512,576]{1,0:T(8,128)(2,1)S(1)} %convolution_convert_fusion.10.k_ref, bf16[512,576]{1,0:T(8,128)(2,1)S(1)} %fusion.38.v_ref), custom_call_target="tpu_custom_call" | custom-call | flops 1207959552 | bytes 2359296 | tf_op jit(solution)/shard_map/pallas_call | solution.py:175
  172.1 7.8 %collective-permute-done.23 = bf16[2,1,72,2304]{3,2,1,0:T(8,128)(2,1)S(1)} collective-permute-done((bf16[2,1,72,2304]{3,2,1,0:T(8,128)(2,1)S(1)}, bf16[2,1,72,2304]{3,2,1,0:T(8,128)(2,1)S(1)}, u32[]{:S(2)}, u32[]{:S(2)}) %collective-permute-start.23) | collective-permute-done | bytes 663584 | tf_op jit(solution)/shard_map/ppermute | solution.py:239
  181.7 4.7 collective-permute-done.21
  189.5 3.4 shard_map.360
  195.3 3.9 multiply_convert_fusion.1
  199.3 4.1 slice.385
  203.3 4.1 collective-permute-done.26
  207.5 4.9 multiply_convert_fusion
  212.4 4.9 collective-permute-done.27.refs_1_
  222.6 3.9 shard_map.361
  241.1 8.4 %slice.389 = bf16[32,64,2048]{2,1,0:T(8,128)(2,1)} slice(bf16[32,88,2048]{2,1,0:T(8,128)(2,1)} %bitcast.635), slice={[0:32], [0:64], [0:2048]} | slice | bytes 16777216 | tf_op jit(solution)/shard_map/slice | solution.py:564
  249.5 4.3 fusion.196
  256.6 5.3 multiply_convert_fusion.3
  262.0 6.3 %multiply_convert_fusion.2 = (bf16[256,2048]{1,0:T(8,128)(2,1)S(1)}, f32[256,2048]{1,0:T(8,128)S(1)}) fusion(f32[2048]{0:T(1024)S(1)} %copy-done.126, bf16[256,2048]{1,0:T(8,128)(2,1)S(1)} %get-tuple-element.210, bf16[2048,2048]{1,0:T(8,128)(2,1)} %bitcast.640), kind=kOutput, calls=%fused_computation.80 | convolution fusion | flops 2150629376 | bytes 12591104 | tf_op jit(solution)/shard_map/dot_general | solution.py:509
  276.2 3.4 copy-done.21
  284.6 7.3 %fusion.194 = (bf16[2048]{0:T(1024)(128)(2,1)}, bf16[256,2048]{1,0:T(8,128)(2,1)S(1)}) fusion(f32[256,2048]{1,0:T(8,128)} %get-tuple-element.370, bf16[256,2048]{1,0:T(8,128)(2,1)S(1)} %copy-done.68, bf16[2048,2048]{1,0:T(8,128)(2,1)} %bitcast.641), kind=kOutput, calls=%fused_computation.489 | convolution fusion | flops 2152724480 | bytes 12587008 | tf_op jit(solution)/shard_map/dot_general | solution.py:509
  292.0 3.2 fusion.180
  298.5 5.2 collective-permute-done.35
  309.0 3.6 convert_reduce_fusion.1
  312.6 6.3 %collective-permute-done.37 = bf16[1,1,2,64,2048]{4,3,2,1,0:T(8,128)(2,1)S(1)} collective-permute-done((bf16[1,1,2,64,2048]{4,3,2,1,0:T(8,128)(2,1)S(1)}, bf16[1,1,2,64,2048]{4,3,2,1,0:T(8,128)(2,1)S(1)}, u32[]{:S(2)}, u32[]{:S(2)}) %collective-permute-start.37) | collective-permute-done | bytes 524320 | tf_op jit(solution)/shard_map/ppermute | solution.py:239
  330.4 3.6 convert_reduce_fusion
  339.6 3.6 collective-permute-done.39
  351.5 5.0 convolution_convert_fusion.1
  356.6 4.3 collective-permute-done.43
  365.8 11.8 %collective-permute-start.45 = (bf16[1,24,2048]{2,1,0:T(8,128)(2,1)S(1)}, bf16[1,24,2048]{2,1,0:T(8,128)(2,1)S(1)}, u32[]{:S(2)}, u32[]{:S(2)}) collective-permute-start(bf16[1,24,2048]{2,1,0:T(8,128)(2,1)S(1)} %fusion.98), channel_id=1, source_target_pairs={{0,16},{2,18},{4,20},{6,22},{8,24},{10,26},{12,28},{14,30},{16,0},... | collective-permute-start | bytes 294920 | tf_op jit(solution)/shard_map/ppermute | solution.py:239
  378.7 3.3 fusion.181
  389.5 5.3 convolution_convert_fusion
  394.9 5.6 collective-permute-done.47
  410.9 12.9 %collective-permute-done.48 = bf16[1,2,1,64,2048]{4,3,1,2,0:T(8,128)(2,1)S(1)} collective-permute-done((bf16[1,2,1,64,2048]{4,3,1,2,0:T(8,128)(2,1)S(1)}, bf16[1,2,1,64,2048]{4,3,1,2,0:T(8,128)(2,1)S(1)}, u32[]{:S(2)}, u32[]{:S(2)}) %collective-permute-start.48) | collective-permute-done | bytes 524320 | tf_op jit(solution)/shard_map/ppermute | solution.py:236
  428.9 12.2 %shard_map.363.right_ref = bf16[3,512,576]{2,1,0:T(8,128)(2,1)S(1)} custom-call(bf16[512,576]{1,0:T(8,128)(2,1)S(1)} %copy-done.14, bf16[512,576]{1,0:T(8,128)(2,1)S(1)} %copy-done.16, bf16[512,576]{1,0:T(8,128)(2,1)S(1)} %copy-done.18, f32[512,8]{1,0:T(8,128)S(1)} %copy-done.20, bf16[512,576]{1,0:T(8,128)(2,1)S(1)} %convolution_convert_fusion.9.in_ref), custom_call_target="tpu_custom_call" | custom-call | flops 2415919104 | bytes 4718592 | tf_op jit(solution)/shard_map/pallas_call | solution.py:212
  454.3 5.5 collective-permute-done.54
  460.5 4.9 shard_map.364
  484.9 8.5 %collective-permute-done.55 = bf16[256,1152]{1,0:T(8,128)(2,1)S(1)} collective-permute-done((bf16[256,1152]{1,0:T(8,128)(2,1)}, bf16[256,1152]{1,0:T(8,128)(2,1)S(1)}, u32[]{:S(2)}, u32[]{:S(2)}) %collective-permute-start.55) | collective-permute-done | bytes 589856 | tf_op jit(solution)/shard_map/ppermute | solution.py:236
  510.6 14.9 %collective-permute-done.60 = bf16[1,2,64,1152]{3,2,1,0:T(8,128)(2,1)} collective-permute-done((bf16[1,2,64,1152]{3,2,1,0:T(8,128)(2,1)}, bf16[1,2,64,1152]{3,2,1,0:T(8,128)(2,1)}, u32[]{:S(2)}, u32[]{:S(2)}) %collective-permute-start.60) | collective-permute-done | bytes 294944 | tf_op jit(solution)/shard_map/ppermute | solution.py:239
  539.1 11.6 %collective-permute-done.66 = bf16[1,72,576]{2,1,0:T(8,128)(2,1)} collective-permute-done((bf16[1,72,576]{2,1,0:T(8,128)(2,1)}, bf16[1,72,576]{2,1,0:T(8,128)(2,1)}, u32[]{:S(2)}, u32[]{:S(2)}) %collective-permute-start.66) | collective-permute-done | bytes 82976 | tf_op jit(solution)/shard_map/ppermute | solution.py:239
  562.7 7.7 %collective-permute-done.63 = bf16[8,17536]{1,0:T(8,128)(2,1)S(1)} collective-permute-done((bf16[8,17536]{1,0:T(8,128)(2,1)S(1)}, bf16[8,17536]{1,0:T(8,128)(2,1)S(1)}, u32[]{:S(2)}, u32[]{:S(2)}) %collective-permute-start.63) | collective-permute-done | bytes 280608 | tf_op jit(solution)/shard_map/ppermute | solution.py:239
  572.3 10.4 %collective-permute-done.68 = bf16[3,2,72,576]{3,2,1,0:T(8,128)(2,1)S(1)} collective-permute-done((bf16[3,2,72,576]{3,2,1,0:T(8,128)(2,1)S(1)}, bf16[3,2,72,576]{3,2,1,0:T(8,128)(2,1)S(1)}, u32[]{:S(2)}, u32[]{:S(2)}) %collective-permute-start.68) | collective-permute-done | bytes 497696 | tf_op jit(solution)/shard_map/ppermute | solution.py:239
  (683 shorter events, 255.9 us)
Async XLA Ops:
  7.2 192.1 %all-gather.6.cloned.1.call-start = ((), (), s32[]{:S(2)}) async-start(), calls=%async_computation.5 | async-start | bytes 11894784 | tf_op jit(solution)/shard_map/all_gather | solution.py:463
  35.4 221.2 %all-gather.4.cloned.1.call-start = ((), (), s32[]{:S(2)}) async-start(), calls=%async_computation.2 | async-start | bytes 4866048 | tf_op jit(solution)/shard_map/all_gather | solution.py:464
  45.3 27.7 %collective-permute-start.12 = (bf16[4,2,72,576]{3,2,1,0:T(8,128)(2,1)S(1)}, bf16[4,2,72,576]{3,2,1,0:T(8,128)(2,1)S(1)}, u32[]{:S(2)}, u32[]{:S(2)}) collective-permute-start(bf16[4,2,72,576]{3,2,1,0:T(8,128)(2,1)S(1)} %constant_dynamic-update-slice_fusion.4.refs_0_), channel_id=1, source_target_pairs={{0,4},{2,6},{4,0},{6,2},{8,12},{10,14},{12,8},{14,10},{16,20},{18,... | collective-permute-start | bytes 1990664 | tf_op jit(solution)/shard_map/ppermute | solution.py:239
  46.0 19.5 %collective-permute-start.9 = (bf16[1,2,72,576]{3,2,1,0:T(8,128)(2,1)S(1)}, bf16[1,2,72,576]{3,2,1,0:T(8,128)(2,1)S(1)}, u32[]{:S(2)}, u32[]{:S(2)}) collective-permute-start(bf16[1,2,72,576]{3,2,1,0:T(8,128)(2,1)S(1)} %maximum_bitcast_fusion), channel_id=1, source_target_pairs={{0,16},{2,18},{4,20},{6,22},{8,24},{10,26},{12,28},{14,30},{16,0},... | collective-permute-start | bytes 497672 | tf_op jit(solution)/shard_map/ppermute | solution.py:239
  69.7 533.3 %reduce-scatter.5.cloned.1.call-start = ((), (), s32[]{:S(2)}) async-start(), calls=%async_computation.4 | async-start | bytes 5640192 | tf_op jit(solution)/shard_map/reduce_scatter | solution.py:644
  70.0 38.3 %collective-permute-start.16 = (bf16[2,2,72,576]{3,2,1,0:T(8,128)(2,1)S(1)}, bf16[2,2,72,576]{3,2,1,0:T(8,128)(2,1)S(1)}, u32[]{:S(2)}, u32[]{:S(2)}) collective-permute-start(bf16[2,2,72,576]{3,2,1,0:T(8,128)(2,1)S(1)} %constant_dynamic-update-slice_fusion.6), channel_id=1, source_target_pairs={{0,8},{2,10},{4,12},{6,14},{8,0},{10,2},{12,4},{14,6},{16,24},{18,... | collective-permute-start | bytes 995336 | tf_op jit(solution)/shard_map/ppermute | solution.py:239
  70.1 29.5 %collective-permute-start.11 = (bf16[1,1,72,2304]{3,2,1,0:T(8,128)(2,1)S(1)}, bf16[1,1,72,2304]{3,2,1,0:T(8,128)(2,1)S(1)}, u32[]{:S(2)}, u32[]{:S(2)}) collective-permute-start(bf16[1,1,72,2304]{3,2,1,0:T(8,128)(2,1)S(1)} %bitcast.717), channel_id=1, source_target_pairs={{0,16},{2,18},{4,20},{6,22},{8,24},{10,26},{12,28},{14,30},{16,0},... | collective-permute-start | bytes 995336 | tf_op jit(solution)/shard_map/ppermute | solution.py:239
  99.6 39.4 %collective-permute-start.18 = (bf16[2,1,72,2304]{3,2,1,0:T(8,128)(2,1)S(1)}, bf16[2,1,72,2304]{3,2,1,0:T(8,128)(2,1)S(1)}, u32[]{:S(2)}, u32[]{:S(2)}) collective-permute-start(bf16[2,1,72,2304]{3,2,1,0:T(8,128)(2,1)S(1)} %constant_dynamic-update-slice_fusion.8), channel_id=1, source_target_pairs={{0,8},{2,10},{4,12},{6,14},{8,0},{10,2},{12,4},{14,6},{16,24},{18,... | collective-permute-start | bytes 1990664 | tf_op jit(solution)/shard_map/ppermute | solution.py:239
  106.7 38.4 %collective-permute-start.14 = (bf16[4,2,72,576]{3,2,1,0:T(8,128)(2,1)S(1)}, bf16[4,2,72,576]{3,2,1,0:T(8,128)(2,1)S(1)}, u32[]{:S(2)}, u32[]{:S(2)}) collective-permute-start(bf16[4,2,72,576]{3,2,1,0:T(8,128)(2,1)S(1)} %collective-permute-done.12.refs_1_), channel_id=1, source_target_pairs={{0,2},{2,0},{4,6},{6,4},{8,10},{10,8},{12,14},{14,12},{16,18},{18,... | collective-permute-start | bytes 1990664 | tf_op jit(solution)/shard_map/ppermute | solution.py:239
  106.7 38.2 %collective-permute-start.13 = (bf16[4,2,72,576]{3,2,1,0:T(8,128)(2,1)S(1)}, bf16[4,2,72,576]{3,2,1,0:T(8,128)(2,1)S(1)}, u32[]{:S(2)}, u32[]{:S(2)}) collective-permute-start(bf16[4,2,72,576]{3,2,1,0:T(8,128)(2,1)S(1)} %constant_dynamic-update-slice_fusion.4.refs_0_), channel_id=1, source_target_pairs={{0,2},{2,0},{4,6},{6,4},{8,10},{10,8},{12,14},{14,12},{16,18},{18,... | collective-permute-start | bytes 1990664 | tf_op jit(solution)/shard_map/ppermute | solution.py:239
  107.2 54.3 %collective-permute-start.15 = (bf16[1,1,72,2304]{3,2,1,0:T(8,128)(2,1)S(1)}, bf16[1,1,72,2304]{3,2,1,0:T(8,128)(2,1)S(1)}, u32[]{:S(2)}, u32[]{:S(2)}) collective-permute-start(bf16[1,1,72,2304]{3,2,1,0:T(8,128)(2,1)S(1)} %bitcast.719), channel_id=1, source_target_pairs={{0,16},{2,18},{4,20},{6,22},{8,24},{10,26},{12,28},{14,30},{16,0},... | collective-permute-start | bytes 995336 | tf_op jit(solution)/shard_map/ppermute | solution.py:239
  108.4 34.6 %collective-permute-start.17 = (bf16[4,2,72,576]{3,2,1,0:T(8,128)(2,1)S(1)}, bf16[4,2,72,576]{3,2,1,0:T(8,128)(2,1)S(1)}, u32[]{:S(2)}, u32[]{:S(2)}) collective-permute-start(bf16[4,2,72,576]{3,2,1,0:T(8,128)(2,1)S(1)} %constant_dynamic-update-slice_fusion.10.refs_0_), channel_id=1, source_target_pairs={{0,4},{2,6},{4,0},{6,2},{8,12},{10,14},{12,8},{14,10},{16,20},{18,... | collective-permute-start | bytes 1990664 | tf_op jit(solution)/shard_map/ppermute | solution.py:239
  143.0 38.6 %collective-permute-start.22 = (bf16[4,1,72,2304]{3,2,1,0:T(8,128)(2,1)S(1)}, bf16[4,1,72,2304]{3,2,1,0:T(8,128)(2,1)S(1)}, u32[]{:S(2)}, u32[]{:S(2)}) collective-permute-start(bf16[4,1,72,2304]{3,2,1,0:T(8,128)(2,1)S(1)} %constant_dynamic-update-slice_fusion.12.refs_0_), channel_id=1, source_target_pairs={{0,4},{2,6},{4,0},{6,2},{8,12},{10,14},{12,8},{14,10},{16,20},{18,... | collective-permute-start | bytes 3981320 | tf_op jit(solution)/shard_map/ppermute | solution.py:239
  161.5 18.3 %collective-permute-start.23 = (bf16[2,1,72,2304]{3,2,1,0:T(8,128)(2,1)S(1)}, bf16[2,1,72,2304]{3,2,1,0:T(8,128)(2,1)S(1)}, u32[]{:S(2)}, u32[]{:S(2)}) collective-permute-start(bf16[2,1,72,2304]{3,2,1,0:T(8,128)(2,1)S(1)} %constant_dynamic-update-slice_fusion.14), channel_id=1, source_target_pairs={{0,8},{2,10},{4,12},{6,14},{8,0},{10,2},{12,4},{14,6},{16,24},{18,... | collective-permute-start | bytes 1990664 | tf_op jit(solution)/shard_map/ppermute | solution.py:239
  169.8 16.6 %collective-permute-start.21 = (bf16[256,1152]{1,0:T(8,128)(2,1)S(1)}, bf16[256,1152]{1,0:T(8,128)(2,1)S(1)}, u32[]{:S(2)}, u32[]{:S(2)}) collective-permute-start(bf16[256,1152]{1,0:T(8,128)(2,1)S(1)} %convolution_convert_fusion.5), channel_id=1, source_target_pairs={{0,1},{1,0},{2,3},{3,2},{4,5},{5,4},{6,7},{7,6},{8,9},{9,8},{10,11... | collective-permute-start | bytes 1769480 | tf_op jit(solution)/shard_map/ppermute | solution.py:236
  181.6 35.6 %collective-permute-start.27 = (bf16[4,1,72,2304]{3,2,1,0:T(8,128)(2,1)}, bf16[4,1,72,2304]{3,2,1,0:T(8,128)(2,1)}, u32[]{:S(2)}, u32[]{:S(2)}) collective-permute-start(bf16[4,1,72,2304]{3,2,1,0:T(8,128)(2,1)} %constant_dynamic-update-slice_fusion.16.refs_0_), channel_id=1, source_target_pairs={{0,4},{2,6},{4,0},{6,2},{8,12},{10,14},{12,8},{14,10},{16,20},{18,... | collective-permute-start | bytes 3981320 | tf_op jit(solution)/shard_map/ppermute | solution.py:239
  187.8 19.6 %collective-permute-start.26 = (bf16[256,1152]{1,0:T(8,128)(2,1)S(1)}, bf16[256,1152]{1,0:T(8,128)(2,1)}, u32[]{:S(2)}, u32[]{:S(2)}) collective-permute-start(bf16[256,1152]{1,0:T(8,128)(2,1)S(1)} %add_convert_fusion.1), channel_id=1, source_target_pairs={{0,1},{1,0},{2,3},{3,2},{4,5},{5,4},{6,7},{7,6},{8,9},{9,8},{10,11... | collective-permute-start | bytes 1769480 | tf_op jit(solution)/shard_map/ppermute | solution.py:236
  231.4 22.5 %collective-permute-start.30 = (bf16[256,1152]{1,0:T(8,128)(2,1)}, bf16[256,1152]{1,0:T(8,128)(2,1)S(1)}, u32[]{:S(2)}, u32[]{:S(2)}) collective-permute-start(bf16[256,1152]{1,0:T(8,128)(2,1)} %convolution_convert_fusion.8), channel_id=1, source_target_pairs={{0,1},{1,0},{2,3},{3,2},{4,5},{5,4},{6,7},{7,6},{8,9},{9,8},{10,11... | collective-permute-start | bytes 1769480 | tf_op jit(solution)/shard_map/ppermute | solution.py:236
  256.1 15.3 %collective-permute-start.31 = (bf16[256,1152]{1,0:T(8,128)(2,1)S(1)}, bf16[256,1152]{1,0:T(8,128)(2,1)}, u32[]{:S(2)}, u32[]{:S(2)}) collective-permute-start(bf16[256,1152]{1,0:T(8,128)(2,1)S(1)} %add_convert_fusion), channel_id=1, source_target_pairs={{0,1},{1,0},{2,3},{3,2},{4,5},{5,4},{6,7},{7,6},{8,9},{9,8},{10,11... | collective-permute-start | bytes 1769480 | tf_op jit(solution)/shard_map/ppermute | solution.py:236
  281.8 21.8 %collective-permute-start.34 = (bf16[1,2,2,2,2,64,2048]{6,5,4,3,2,1,0:T(8,128)(2,1)}, bf16[1,2,2,2,2,64,2048]{6,5,4,3,2,1,0:T(8,128)(2,1)}, u32[]{:S(2)}, u32[]{:S(2)}) collective-permute-start(bf16[1,2,2,2,2,64,2048]{6,5,4,3,2,1,0:T(8,128)(2,1)} %dynamic-slice_bitcast_fusion), channel_id=1, source_target_pairs={{0,2},{2,0},{4,6},{6,4},{8,10},{10,8},{12,14},{14,12},{16,18},{18,... | collective-permute-start | bytes 12582920 | tf_op jit(solution)/shard_map/ppermute | solution.py:239
  284.1 19.5 %collective-permute-start.35 = (bf16[1,2,2,2,24,2048]{5,4,3,2,1,0:T(8,128)(2,1)S(1)}, bf16[1,2,2,2,24,2048]{5,4,3,2,1,0:T(8,128)(2,1)S(1)}, u32[]{:S(2)}, u32[]{:S(2)}) collective-permute-start(bf16[1,2,2,2,24,2048]{5,4,3,2,1,0:T(8,128)(2,1)S(1)} %fusion.36), channel_id=1, source_target_pairs={{0,4},{2,6},{4,0},{6,2},{8,12},{10,14},{12,8},{14,10},{16,20},{18,... | collective-permute-start | bytes 2359304 | tf_op jit(solution)/shard_map/ppermute | solution.py:239
  295.1 17.5 %collective-permute-start.36 = (bf16[256,1152]{1,0:T(8,128)(2,1)S(1)}, bf16[256,1152]{1,0:T(8,128)(2,1)S(1)}, u32[]{:S(2)}, u32[]{:S(2)}) collective-permute-start(bf16[256,1152]{1,0:T(8,128)(2,1)S(1)} %get-tuple-element.222), channel_id=1, source_target_pairs={{0,1},{1,0},{2,3},{3,2},{4,5},{5,4},{6,7},{7,6},{8,9},{9,8},{10,11... | collective-permute-start | bytes 1769480 | tf_op jit(solution)/shard_map/ppermute | solution.py:236
  322.5 20.7 %collective-permute-start.40 = (bf16[1,2,2,2,2,64,1152]{6,5,4,3,2,1,0:T(8,128)(2,1)S(1)}, bf16[1,2,2,2,2,64,1152]{6,5,4,3,2,1,0:T(8,128)(2,1)S(1)}, u32[]{:S(2)}, u32[]{:S(2)}) collective-permute-start(bf16[1,2,2,2,2,64,1152]{6,5,4,3,2,1,0:T(8,128)(2,1)S(1)} %dynamic-slice_bitcast_fusion.1), channel_id=1, source_target_pairs={{0,2},{2,0},{4,6},{6,4},{8,10},{10,8},{12,14},{14,12},{16,18},{18,... | collective-permute-start | bytes 7077896 | tf_op jit(solution)/shard_map/ppermute | solution.py:239
  329.9 13.3 %collective-permute-start.39 = (bf16[1,1,2,64,2048]{4,3,2,1,0:T(8,128)(2,1)S(1)}, bf16[1,1,2,64,2048]{4,3,2,1,0:T(8,128)(2,1)S(1)}, u32[]{:S(2)}, u32[]{:S(2)}) collective-permute-start(bf16[1,1,2,64,2048]{4,3,2,1,0:T(8,128)(2,1)S(1)} %fusion.61), channel_id=1, source_target_pairs={{0,4},{2,6},{4,0},{6,2},{8,12},{10,14},{12,8},{14,10},{16,20},{18,... | collective-permute-start | bytes 1572872 | tf_op jit(solution)/shard_map/ppermute | solution.py:239
  336.6 20.0 %collective-permute-start.42 = (bf16[256,1152]{1,0:T(8,128)(2,1)}, bf16[256,1152]{1,0:T(8,128)(2,1)S(1)}, u32[]{:S(2)}, u32[]{:S(2)}) collective-permute-start(bf16[256,1152]{1,0:T(8,128)(2,1)} %convolution_convert_fusion.6), channel_id=1, source_target_pairs={{0,1},{1,0},{2,3},{3,2},{4,5},{5,4},{6,7},{7,6},{8,9},{9,8},{10,11... | collective-permute-start | bytes 1769480 | tf_op jit(solution)/shard_map/ppermute | solution.py:236
  356.5 248.4 %reduce-scatter.3.cloned.1.call-start = ((), (), s32[]{:S(2)}) async-start(), calls=%async_computation.3 | async-start | bytes 5640192 | tf_op jit(solution)/shard_map/reduce_scatter | solution.py:665
  364.1 18.5 %collective-permute-start.44 = (bf16[1,1,2,64,2048]{4,3,2,1,0:T(8,128)(2,1)S(1)}, bf16[1,1,2,64,2048]{4,3,2,1,0:T(8,128)(2,1)S(1)}, u32[]{:S(2)}, u32[]{:S(2)}) collective-permute-start(bf16[1,1,2,64,2048]{4,3,2,1,0:T(8,128)(2,1)S(1)} %fusion.63), channel_id=1, source_target_pairs={{0,4},{2,6},{4,0},{6,2},{8,12},{10,14},{12,8},{14,10},{16,20},{18,... | collective-permute-start | bytes 1572872 | tf_op jit(solution)/shard_map/ppermute | solution.py:239
  365.8 16.8 %collective-permute-start.45 = (bf16[1,24,2048]{2,1,0:T(8,128)(2,1)S(1)}, bf16[1,24,2048]{2,1,0:T(8,128)(2,1)S(1)}, u32[]{:S(2)}, u32[]{:S(2)}) collective-permute-start(bf16[1,24,2048]{2,1,0:T(8,128)(2,1)S(1)} %fusion.98), channel_id=1, source_target_pairs={{0,16},{2,18},{4,20},{6,22},{8,24},{10,26},{12,28},{14,30},{16,0},... | collective-permute-start | bytes 294920 | tf_op jit(solution)/shard_map/ppermute | solution.py:239
  385.6 15.0 %collective-permute-start.47 = (bf16[1,2,2,64,1152]{4,3,2,1,0:T(8,128)(2,1)}, bf16[1,2,2,64,1152]{4,3,2,1,0:T(8,128)(2,1)}, u32[]{:S(2)}, u32[]{:S(2)}) collective-permute-start(bf16[1,2,2,64,1152]{4,3,2,1,0:T(8,128)(2,1)} %fusion.45), channel_id=1, source_target_pairs={{0,4},{2,6},{4,0},{6,2},{8,12},{10,14},{12,8},{14,10},{16,20},{18,... | collective-permute-start | bytes 1769480 | tf_op jit(solution)/shard_map/ppermute | solution.py:239
  407.2 17.1 %collective-permute-start.50 = (bf16[1,8,72,576]{3,2,1,0:T(8,128)(2,1)S(1)}, bf16[1,8,72,576]{3,2,1,0:T(8,128)(2,1)S(1)}, u32[]{:S(2)}, u32[]{:S(2)}) collective-permute-start(bf16[1,8,72,576]{3,2,1,0:T(8,128)(2,1)S(1)} %get-tuple-element.242), channel_id=1, source_target_pairs={{0,2},{2,0},{4,6},{6,4},{8,10},{10,8},{12,14},{14,12},{16,18},{18,... | collective-permute-start | bytes 1990664 | tf_op jit(solution)/shard_map/ppermute | solution.py:239
  407.2 17.1 %collective-permute-start.49 = (bf16[1,2,2,64,1152]{4,3,2,1,0:T(8,128)(2,1)S(1)}, bf16[1,2,2,64,1152]{4,3,2,1,0:T(8,128)(2,1)S(1)}, u32[]{:S(2)}, u32[]{:S(2)}) collective-permute-start(bf16[1,2,2,64,1152]{4,3,2,1,0:T(8,128)(2,1)S(1)} %fusion.44), channel_id=1, source_target_pairs={{0,4},{2,6},{4,0},{6,2},{8,12},{10,14},{12,8},{14,10},{16,20},{18,... | collective-permute-start | bytes 1769480 | tf_op jit(solution)/shard_map/ppermute | solution.py:239
  409.8 14.0 %collective-permute-start.48 = (bf16[1,2,1,64,2048]{4,3,1,2,0:T(8,128)(2,1)S(1)}, bf16[1,2,1,64,2048]{4,3,1,2,0:T(8,128)(2,1)S(1)}, u32[]{:S(2)}, u32[]{:S(2)}) collective-permute-start(bf16[1,2,1,64,2048]{4,3,1,2,0:T(8,128)(2,1)S(1)} %fusion.51), channel_id=1, source_target_pairs={{0,1},{1,0},{2,3},{3,2},{4,5},{5,4},{6,7},{7,6},{8,9},{9,8},{10,11... | collective-permute-start | bytes 1572872 | tf_op jit(solution)/shard_map/ppermute | solution.py:236
  426.1 15.0 %collective-permute-start.51 = (bf16[1,2,1,64,2048]{4,3,1,2,0:T(8,128)(2,1)S(1)}, bf16[1,2,1,64,2048]{4,3,1,2,0:T(8,128)(2,1)S(1)}, u32[]{:S(2)}, u32[]{:S(2)}) collective-permute-start(bf16[1,2,1,64,2048]{4,3,1,2,0:T(8,128)(2,1)S(1)} %fusion.49), channel_id=1, source_target_pairs={{0,1},{1,0},{2,3},{3,2},{4,5},{5,4},{6,7},{7,6},{8,9},{9,8},{10,11... | collective-permute-start | bytes 1572872 | tf_op jit(solution)/shard_map/ppermute | solution.py:236
  442.6 17.9 %collective-permute-start.53 = (bf16[1,2,2,64,1152]{4,3,2,1,0:T(8,128)(2,1)S(1)}, bf16[1,2,2,64,1152]{4,3,2,1,0:T(8,128)(2,1)}, u32[]{:S(2)}, u32[]{:S(2)}) collective-permute-start(bf16[1,2,2,64,1152]{4,3,2,1,0:T(8,128)(2,1)S(1)} %fusion.43), channel_id=1, source_target_pairs={{0,1},{1,0},{2,3},{3,2},{4,5},{5,4},{6,7},{7,6},{8,9},{9,8},{10,11... | collective-permute-start | bytes 1769480 | tf_op jit(solution)/shard_map/ppermute | solution.py:236
  466.9 29.7 %collective-permute-start.56 = (bf16[3,8,72,576]{3,2,1,0:T(8,128)(2,1)}, bf16[3,8,72,576]{3,2,1,0:T(8,128)(2,1)}, u32[]{:S(2)}, u32[]{:S(2)}) collective-permute-start(bf16[3,8,72,576]{3,2,1,0:T(8,128)(2,1)} %get-tuple-element.252), channel_id=1, source_target_pairs={{0,2},{2,0},{4,6},{6,4},{8,10},{10,8},{12,14},{14,12},{16,18},{18,... | collective-permute-start | bytes 5971976 | tf_op jit(solution)/shard_map/ppermute | solution.py:239
  477.4 16.0 %collective-permute-start.55 = (bf16[256,1152]{1,0:T(8,128)(2,1)}, bf16[256,1152]{1,0:T(8,128)(2,1)S(1)}, u32[]{:S(2)}, u32[]{:S(2)}) collective-permute-start(bf16[256,1152]{1,0:T(8,128)(2,1)} %fusion.6), channel_id=1, source_target_pairs={{0,1},{1,0},{2,3},{3,2},{4,5},{5,4},{6,7},{7,6},{8,9},{9,8},{10,11... | collective-permute-start | bytes 1769480 | tf_op jit(solution)/shard_map/ppermute | solution.py:236
  481.9 14.7 %collective-permute-start.57 = (bf16[1,64,2048]{2,1,0:T(8,128)(2,1)S(1)}, bf16[1,64,2048]{2,1,0:T(8,128)(2,1)S(1)}, u32[]{:S(2)}, u32[]{:S(2)}) collective-permute-start(bf16[1,64,2048]{2,1,0:T(8,128)(2,1)S(1)} %fusion.66), channel_id=1, source_target_pairs={{0,16},{2,18},{4,20},{6,22},{8,24},{10,26},{12,28},{14,30},{16,0},... | collective-permute-start | bytes 786440 | tf_op jit(solution)/shard_map/ppermute | solution.py:239
  500.6 25.0 %collective-permute-start.60 = (bf16[1,2,64,1152]{3,2,1,0:T(8,128)(2,1)}, bf16[1,2,64,1152]{3,2,1,0:T(8,128)(2,1)}, u32[]{:S(2)}, u32[]{:S(2)}) collective-permute-start(bf16[1,2,64,1152]{3,2,1,0:T(8,128)(2,1)} %fusion.59), channel_id=1, source_target_pairs={{0,8},{2,10},{4,12},{6,14},{8,0},{10,2},{12,4},{14,6},{16,24},{18,... | collective-permute-start | bytes 884744 | tf_op jit(solution)/shard_map/ppermute | solution.py:239
  507.5 22.9 %collective-permute-start.58 = (bf16[1,17536]{1,0:T(2,128)(2,1)S(1)}, bf16[1,17536]{1,0:T(2,128)(2,1)S(1)}, u32[]{:S(2)}, u32[]{:S(2)}) collective-permute-start(bf16[1,17536]{1,0:T(2,128)(2,1)S(1)} %concatenate.116), channel_id=1, source_target_pairs={{0,4},{2,6},{4,0},{6,2},{8,12},{10,14},{12,8},{14,10},{16,20},{18,... | collective-permute-start | bytes 105224 | tf_op jit(solution)/shard_map/ppermute | solution.py:239
  532.9 25.8 %collective-permute-start.64 = (bf16[3,2,2,72,576]{4,3,2,1,0:T(8,128)(2,1)}, bf16[3,2,2,72,576]{4,3,2,1,0:T(8,128)(2,1)}, u32[]{:S(2)}, u32[]{:S(2)}) collective-permute-start(bf16[3,2,2,72,576]{4,3,2,1,0:T(8,128)(2,1)} %pad_maximum_fusion.7), channel_id=1, source_target_pairs={{0,4},{2,6},{4,0},{6,2},{8,12},{10,14},{12,8},{14,10},{16,20},{18,... | collective-permute-start | bytes 2985992 | tf_op jit(solution)/shard_map/ppermute | solution.py:239
  533.2 19.3 %collective-permute-start.65 = (bf16[1,64,1152]{2,1,0:T(8,128)(2,1)}, bf16[1,64,1152]{2,1,0:T(8,128)(2,1)S(1)}, u32[]{:S(2)}, u32[]{:S(2)}) collective-permute-start(bf16[1,64,1152]{2,1,0:T(8,128)(2,1)} %fusion.95), channel_id=1, source_target_pairs={{0,16},{2,18},{4,20},{6,22},{8,24},{10,26},{12,28},{14,30},{16,0},... | collective-permute-start | bytes 442376 | tf_op jit(solution)/shard_map/ppermute | solution.py:239
  535.4 15.4 %collective-permute-start.66 = (bf16[1,72,576]{2,1,0:T(8,128)(2,1)}, bf16[1,72,576]{2,1,0:T(8,128)(2,1)}, u32[]{:S(2)}, u32[]{:S(2)}) collective-permute-start(bf16[1,72,576]{2,1,0:T(8,128)(2,1)} %fusion.109), channel_id=1, source_target_pairs={{0,16},{2,18},{4,20},{6,22},{8,24},{10,26},{12,28},{14,30},{16,0},... | collective-permute-start | bytes 248840 | tf_op jit(solution)/shard_map/ppermute | solution.py:239
  536.1 18.5 %collective-permute-start.69 = (bf16[256,1152]{1,0:T(8,128)(2,1)}, bf16[256,1152]{1,0:T(8,128)(2,1)}, u32[]{:S(2)}, u32[]{:S(2)}) collective-permute-start(bf16[256,1152]{1,0:T(8,128)(2,1)} %get-tuple-element.270), channel_id=1, source_target_pairs={{0,1},{1,0},{2,3},{3,2},{4,5},{5,4},{6,7},{7,6},{8,9},{9,8},{10,11... | collective-permute-start | bytes 1769480 | tf_op jit(solution)/shard_map/ppermute | solution.py:236
  538.8 15.6 %collective-permute-start.62 = (bf16[4,17536]{1,0:T(4,128)(2,1)S(1)}, bf16[4,17536]{1,0:T(4,128)(2,1)S(1)}, u32[]{:S(2)}, u32[]{:S(2)}) collective-permute-start(bf16[4,17536]{1,0:T(4,128)(2,1)S(1)} %reshape.2110), channel_id=1, source_target_pairs={{0,16},{2,18},{4,20},{6,22},{8,24},{10,26},{12,28},{14,30},{16,0},... | collective-permute-start | bytes 420872 | tf_op jit(solution)/shard_map/ppermute | solution.py:239
  554.6 15.8 %collective-permute-start.63 = (bf16[8,17536]{1,0:T(8,128)(2,1)S(1)}, bf16[8,17536]{1,0:T(8,128)(2,1)S(1)}, u32[]{:S(2)}, u32[]{:S(2)}) collective-permute-start(bf16[8,17536]{1,0:T(8,128)(2,1)S(1)} %pad_maximum_fusion.13), channel_id=1, source_target_pairs={{0,8},{2,10},{4,12},{6,14},{8,0},{10,2},{12,4},{14,6},{16,24},{18,... | collective-permute-start | bytes 841736 | tf_op jit(solution)/shard_map/ppermute | solution.py:239
  562.6 20.1 %collective-permute-start.68 = (bf16[3,2,72,576]{3,2,1,0:T(8,128)(2,1)S(1)}, bf16[3,2,72,576]{3,2,1,0:T(8,128)(2,1)S(1)}, u32[]{:S(2)}, u32[]{:S(2)}) collective-permute-start(bf16[3,2,72,576]{3,2,1,0:T(8,128)(2,1)S(1)} %pad_maximum_fusion.10), channel_id=1, source_target_pairs={{0,8},{2,10},{4,12},{6,14},{8,0},{10,2},{12,4},{14,6},{16,24},{18,... | collective-permute-start | bytes 1493000 | tf_op jit(solution)/shard_map/ppermute | solution.py:239
  570.6 13.2 %collective-permute-start.67 = (bf16[16,17536]{1,0:T(8,128)(2,1)S(1)}, bf16[16,17536]{1,0:T(8,128)(2,1)S(1)}, u32[]{:S(2)}, u32[]{:S(2)}) collective-permute-start(bf16[16,17536]{1,0:T(8,128)(2,1)S(1)} %pad_maximum_fusion.9), channel_id=1, source_target_pairs={{0,2},{2,0},{4,6},{6,4},{8,10},{10,8},{12,14},{14,12},{16,18},{18,... | collective-permute-start | bytes 1683464 | tf_op jit(solution)/shard_map/ppermute | solution.py:239
  585.8 14.9 %collective-permute-start.70 = (bf16[3,72,576]{2,1,0:T(8,128)(2,1)}, bf16[3,72,576]{2,1,0:T(8,128)(2,1)}, u32[]{:S(2)}, u32[]{:S(2)}) collective-permute-start(bf16[3,72,576]{2,1,0:T(8,128)(2,1)} %pad_maximum_fusion.14), channel_id=1, source_target_pairs={{0,16},{2,18},{4,20},{6,22},{8,24},{10,26},{12,28},{14,30},{16,0},... | collective-permute-start | bytes 746504 | tf_op jit(solution)/shard_map/ppermute | solution.py:239
  (182 other events, 1844.7 us)
Sparse Core Ops, SparseCore 0:
  35.5 126.8 all-gather.5
  165.3 71.4 all-gather.3
  356.6 92.3 reduce-scatter.4
  477.5 95.6 reduce-scatter.2

commit v4 on v3

--- a/solution.py
+++ b/solution.py
@@ -307,6 +307,9 @@
         def fly(value):
             air.append(value)
             return value
+
+        def hold():
+            return air.pop()
 
         def land():
             last.extend(air)
@@ -616,7 +619,8 @@
         grad_bdown = jnp.sum(grad_branch.astype(f32), axis=0, keepdims=True)
         land()
         other_branch = fly(swap_x(grad_branch))
-        two.send(CORES, 0, 4)
+        two.send(CORES, 0, 2)
+        early_two = hold()
         one = Scatter([mark(dot(after(grad_pre_one), block_out, 0, 0).astype(bf16))], True)
 
         def feed_back(incoming, hidden):
@@ -626,14 +630,15 @@
         hidden_grad_own = feed_back(grad_branch, hidden_own)
         land()
         three.send(0)
-        two.send(CORES, 1, 4)
         one.send(1)
         hidden_grad_other = feed_back(other_branch, hidden_other)
         outgoing = mark(dot(after(hidden_grad_other), full_up, 1, 1).astype(bf16))
         land()
         arrived = fly(swap_x(outgoing))
         three.send(far[-1])
-        two.send(CORES, 2, 4)
+        two.send(CORES, 1, 2)
+        slow = hold()
+        fly(early_two)
         grad_act_two = mark(dot(after(hidden_grad_own), full_up, 1, 1))
         grad_bunits = jnp.sum(hidden_grad_own.astype(f32), axis=0, keepdims=True) + jnp.sum(
             hidden_grad_other.astype(f32), axis=0, keepdims=True
@@ -643,7 +648,6 @@
         grad_wdown = mark(dot(after(branch_both), active_both, 0, 0).astype(bf16))
         own_down = lax.psum_scatter(grad_wdown, "dp", scatter_dimension=0, tiled=True)
         land()
-        two.send(CORES, 3, 4)
         for mask in far[-2::-1]:
             three.send(mask)
         grad_act_two = after(grad_act_two) + arrived.astype(f32)
@@ -656,16 +660,19 @@
         grad_attention = mark((gate_one * grad_first_sum).astype(bf16))
         grad_gate_one = jnp.sum(grad_first_sum * attention, axis=0, keepdims=True)
         grad_bout = jnp.sum(grad_attention.astype(f32), axis=0, keepdims=True)
+        late_two = slow
         land()
         other_attention = fly(swap_x(grad_attention))
-        one.send(CORES, 0, 2)
+        one.send(CORES)
+        slow = hold()
         act_both = jnp.concatenate((act_two, other_two), axis=0)
         hidden_both = jnp.concatenate((hidden_grad_own, hidden_grad_other), axis=0)
         grad_wup = mark(dot(after(act_both), hidden_both, 0, 0).astype(bf16))
         own_up = lax.psum_scatter(grad_wup, "dp", scatter_dimension=0, tiled=True)
-        land()
-        two.send(0, 0, 2)
-        one.send(CORES, 1, 2)
+        fly(late_two)
+        land()
+        two.send(0)
+        slower = hold()
         attention_both = mark(
             jnp.concatenate((after(grad_attention), other_attention), axis=0)
         )
@@ -676,12 +683,13 @@
         )
         out = Scatter.from_halves(halves[0], mark(halves[1]))
         land()
-        two.send(0, 1, 2)
         grad_three = mark(
             attend_back(queries, key_heads, val_heads, log_total, after(grad_mixed), seq_len)
         )
         grad_bquery = jnp.sum(grad_three[0].astype(f32), axis=0, keepdims=True)
         grad_bvalue = jnp.sum(grad_three[2].astype(f32), axis=0, keepdims=True)
+        fly(slow)
+        fly(slower)
         land()
         one.send(0)
         out.send(CORES)
@@ -696,13 +704,12 @@
 
         outgoing = mark(part_one(seq_len).astype(bf16))
         grad_act_one = mark(part_one(0))
-        land()
         arrived = fly(swap_x(outgoing))
         halves = split_grads(act_flat, after(grad_three), my_core, planes * ROWS)
         qkv = Scatter.from_halves(halves[0], mark(halves[1]))
+        land()
         for mask in far[-2::-1]:
             two.send(mask)
-        land()
         one.send(far[-1])
         out.send(far[-1])
         normed_own, inverse_own = normed_one[0], inverse_one[0]
@@ -733,12 +740,8 @@
             starts.append(starts[-1] + piece.shape[1])
         sent = jnp.concatenate([piece.astype(bf16) for piece in sent], axis=1)
         mark(sent)
-        land()
         row_sent = swap(sent, near_order[0])
         qkv.send(CORES)
-        for mask in far[-2::-1]:
-            one.send(mask)
-            out.send(mask)
         near_sent = mark(jnp.concatenate((sent, after(row_sent)), axis=0))
         side_sent = swap_x(near_sent)
         grad_other = swap_x(tie(grad_own.astype(bf16), near_sent))
@@ -752,6 +755,8 @@
         land()
         for mask in far[-2::-1]:
             qkv.send(mask)
+            one.send(mask)
+            out.send(mask)
         near_sent = after(near_sent)
         def own_part(index, count, parts, values):
             held = values[:, starts[index] : starts[index] + count * parts]

time: 620 us -> 597 us (0.963)
  waiting for transfers between devices: 221 us -> 184 us
  matrix products: 87.7 us -> 102 us
  Pallas kernels: 45.1 us -> 55.8 us
  starting transfers between devices: 78.3 us -> 68 us
  other arithmetic: 83.7 us -> 92.7 us
  local copies, waits for them, and re-layouts: 81.6 us -> 72.6 us
    ppermute x15 -> x14, waiting for transfers between devices: 33.3 us -> 10.4 us  [swap_x(): return lax.ppermute(value, 'mp', [(k, k ^ 1) for k in range(mp)])]
    dot_general x43, matrix products: 83.4 us -> 98.2 us  [dot(): lax.dot_general(left, right, (((left_axis,), (right_axis,)), ((), ())), p...]
    ppermute x56 -> x53, waiting for transfers between devices: 187 us -> 173 us  [swap(): return lax.ppermute(value, 'dp', [(k, k ^ mask) for k in range(dp)])]
    convert_element_type x25, other arithmetic: 30.6 us -> 41.9 us  [send(): outgoing.append(sum((half.astype(f32) for half in halves)).astype(bf16))]
    ppermute x56 -> x53, starting transfers between devices: 60 us -> 48.7 us  [swap(): return lax.ppermute(value, 'dp', [(k, k ^ mask) for k in range(dp)])]
    pallas_call x4, Pallas kernels: 19.3 us -> 30.5 us  [place_pieces(): pl.pallas_call(body, in_specs=[pl.BlockSpec(memory_space=pltpu.SMEM)] + [...]
    dynamic_slice x9 -> x3, local copies, waits for them, and re-layouts: 12.8 us -> 1.88 us  [pick(): return lax.dynamic_index_in_dim(values, index, axis, keepdims=False)]
    convert_element_type x14, local copies, waits for them, and re-layouts: 7.7 us -> 0.09 us  [shards(): sent = jnp.concatenate([piece.astype(bf16) for piece in sent], axis=1)]
  transfers between devices with their start and end apart: 75 -> 71, of which waited for: 34 -> 26; matrix products, arithmetic and copies ran while one was open for 37% -> 40% of each run, Pallas kernels for 7% -> 9%
where the time goes in v4:
time: 597 us; the launch traced here: 592 us
  waiting for transfers between devices  184 us (31%)
  matrix products  102 us (17%)
  other arithmetic  92.7 us (16%)
  local copies, waits for them, and re-layouts  72.6 us (12%)
  starting transfers between devices  68 us (11%)
  Pallas kernels  55.8 us (9%)
  between operations  16.2 us (3%)
    ppermute x53, waiting for transfers between devices, swap(): return lax.ppermute(value, 'dp', [(k, k ^ mask) for k in range(dp)])  173 us
    dot_general x43, matrix products, dot(): lax.dot_general(left, right, (((left_axis,), (right_axis,)), ((), ())), p...  98.2 us
    ppermute x53, starting transfers between devices, swap(): return lax.ppermute(value, 'dp', [(k, k ^ mask) for k in range(dp)])  48.7 us
    convert_element_type x25, other arithmetic, send(): outgoing.append(sum((half.astype(f32) for half in halves)).astype(bf16))  41.9 us
    pallas_call x4, Pallas kernels, place_pieces(): pl.pallas_call(body, in_specs=[pl.BlockSpec(memory_space=pltpu.SMEM)] + [...  30.5 us
    unnamed x304, local copies, waits for them, and re-layouts  24.2 us
    ppermute x14, starting transfers between devices, swap_x(): return lax.ppermute(value, 'mp', [(k, k ^ 1) for k in range(mp)])  18.8 us
  transfers between devices with their start and end apart: 71, of which 26 were waited for; matrix products, arithmetic and copies ran while one was open for 40% of the time, Pallas kernels for 9%

profile of v4, /device:TPU:0, one launch (start us, length us, event | category | flops | bytes accessed | tf_op | source)
XLA Modules:
  0.0 591.6 jit_solution(3747150648616812273)
XLA Ops:
  8.9 3.0 collective-permute-start
  16.6 7.4 %collective-permute-done.1 = f32[2,640]{1,0:T(2,128)S(1)} collective-permute-done((f32[2,640]{1,0:T(2,128)S(1)}, f32[2,640]{1,0:T(2,128)S(1)}, u32[]{:S(2)}, u32[]{:S(2)}) %collective-permute-start.1) | collective-permute-done | bytes 5152 | tf_op jit(solution)/shard_map/ppermute | solution.py:239
  29.7 5.6 collective-permute-done.5
  45.9 3.4 collective-permute-start.9
  49.3 7.9 %collective-permute-done.7 = bf16[6,8,1152]{2,1,0:T(8,128)(2,1)S(1)} collective-permute-done((bf16[6,8,1152]{2,1,0:T(8,128)(2,1)S(1)}, bf16[6,8,1152]{2,1,0:T(8,128)(2,1)S(1)}, u32[]{:S(2)}, u32[]{:S(2)}) %collective-permute-start.7) | collective-permute-done | bytes 110624 | tf_op jit(solution)/shard_map/ppermute | solution.py:239
  57.4 8.1 %collective-permute-done.9 = bf16[1,2,72,576]{3,2,1,0:T(8,128)(2,1)S(1)} collective-permute-done((bf16[1,2,72,576]{3,2,1,0:T(8,128)(2,1)S(1)}, bf16[1,2,72,576]{3,2,1,0:T(8,128)(2,1)S(1)}, u32[]{:S(2)}, u32[]{:S(2)}) %collective-permute-start.9) | collective-permute-done | bytes 165920 | tf_op jit(solution)/shard_map/ppermute | solution.py:239
  70.3 2.9 collective-permute-start.11
  73.2 25.6 %collective-permute-done.11 = bf16[1,1,72,2304]{3,2,1,0:T(8,128)(2,1)S(1)} collective-permute-done((bf16[1,1,72,2304]{3,2,1,0:T(8,128)(2,1)S(1)}, bf16[1,1,72,2304]{3,2,1,0:T(8,128)(2,1)S(1)}, u32[]{:S(2)}, u32[]{:S(2)}) %collective-permute-start.11) | collective-permute-done | bytes 331808 | tf_op jit(solution)/shard_map/ppermute | solution.py:239
  98.9 4.7 collective-permute-start.18
  109.0 32.8 %collective-permute-done.18 = bf16[2,1,72,2304]{3,2,1,0:T(8,128)(2,1)S(1)} collective-permute-done((bf16[2,1,72,2304]{3,2,1,0:T(8,128)(2,1)S(1)}, bf16[2,1,72,2304]{3,2,1,0:T(8,128)(2,1)S(1)}, u32[]{:S(2)}, u32[]{:S(2)}) %collective-permute-start.18) | collective-permute-done | bytes 663584 | tf_op jit(solution)/shard_map/ppermute | solution.py:239
  143.9 6.0 %shard_map.357 = bf16[2,4,2,2,72,576]{5,4,3,2,1,0:T(8,128)(2,1)S(1)} custom-call(s32[7]{0:T(128)S(1)} %stack.149.place_ref, bf16[4,2,72,576]{3,2,1,0:T(8,128)(2,1)S(1)} %constant_dynamic-update-slice_fusion.4.refs_0_, bf16[4,2,72,576]{3,2,1,0:T(8,128)(2,1)S(1)} %collective-permute-done.12.refs_1_, ...), custom_call_target="tpu_custom_call" | custom-call | bytes 5308416 | tf_op jit(solution)/shard_map/pallas_call | solution.py:87
  153.0 6.0 %shard_map.358 = (bf16[1,4,2,2,72,576]{5,4,3,2,1,0:T(8,128)(2,1)S(1)}, bf16[1,4,2,2,72,576]{5,4,3,2,1,0:T(8,128)(2,1)S(1)}) custom-call(s32[7]{0:T(128)S(1)} %stack.149.place_ref, bf16[4,2,72,576]{3,2,1,0:T(8,128)(2,1)S(1)} %constant_dynamic-update-slice_fusion.10.refs_0_, bf16[4,2,72,576]{3,2,1,0:T(8,128)(2,1)S(1)} %collective-permute-done.17.refs_1_, ...), custom_call_target="tpu_custom_call" | custom-call | bytes 5308416 | tf_op jit(solution)/shard_map/pallas_call | solution.py:87
  160.9 7.4 %shard_map.359 = (bf16[512,576]{1,0:T(8,128)(2,1)S(1)}, f32[512,8]{1,0:T(8,128)S(1)}) custom-call(bf16[512,576]{1,0:T(8,128)(2,1)S(1)} %fusion.41.q_ref, bf16[512,576]{1,0:T(8,128)(2,1)S(1)} %convolution_convert_fusion.10.k_ref, bf16[512,576]{1,0:T(8,128)(2,1)S(1)} %fusion.42.v_ref), custom_call_target="tpu_custom_call" | custom-call | flops 1207959552 | bytes 2359296 | tf_op jit(solution)/shard_map/pallas_call | solution.py:175
  171.4 7.1 %collective-permute-done.23 = bf16[2,1,72,2304]{3,2,1,0:T(8,128)(2,1)S(1)} collective-permute-done((bf16[2,1,72,2304]{3,2,1,0:T(8,128)(2,1)S(1)}, bf16[2,1,72,2304]{3,2,1,0:T(8,128)(2,1)S(1)}, u32[]{:S(2)}, u32[]{:S(2)}) %collective-permute-start.23) | collective-permute-done | bytes 663584 | tf_op jit(solution)/shard_map/ppermute | solution.py:239
  180.7 4.9 collective-permute-done.21
  188.6 14.6 %shard_map.360 = bf16[1,4,2,2,72,2304]{5,4,3,2,1,0:T(8,128)(2,1)S(1)} custom-call(s32[7]{0:T(128)S(1)} %stack.149.place_ref, bf16[4,1,72,2304]{3,2,1,0:T(8,128)(2,1)S(1)} %constant_dynamic-update-slice_fusion.12.refs_0_, bf16[4,1,72,2304]{3,2,1,0:T(8,128)(2,1)S(1)} %collective-permute-done.22.refs_1_, ...), custom_call_target="tpu_custom_call" | custom-call | bytes 10616832 | tf_op jit(solution)/shard_map/pallas_call | solution.py:87
  205.6 3.9 multiply_convert_fusion.1
  209.5 4.3 slice.337
  214.7 4.9 multiply_convert_fusion
  224.9 3.9 shard_map.361
  241.2 8.4 %slice.341 = bf16[32,64,2048]{2,1,0:T(8,128)(2,1)} slice(bf16[32,88,2048]{2,1,0:T(8,128)(2,1)} %bitcast.614), slice={[0:32], [0:64], [0:2048]} | slice | bytes 16777216 | tf_op jit(solution)/shard_map/slice | solution.py:567
  249.6 4.3 fusion.190
  256.6 5.3 multiply_convert_fusion.3
  262.0 6.3 %multiply_convert_fusion.2 = (bf16[256,2048]{1,0:T(8,128)(2,1)S(1)}, f32[256,2048]{1,0:T(8,128)S(1)}) fusion(f32[2048]{0:T(1024)S(1)} %copy-done.120, bf16[256,2048]{1,0:T(8,128)(2,1)S(1)} %get-tuple-element.206, bf16[2048,2048]{1,0:T(8,128)(2,1)} %bitcast.615), kind=kOutput, calls=%fused_computation.90 | convolution fusion | flops 2150629376 | bytes 12591104 | tf_op jit(solution)/shard_map/dot_general | solution.py:512
  275.0 2.8 convolution_convert_fusion.3
  277.8 3.4 copy-done.23
  285.9 7.3 %fusion.188 = (bf16[2048]{0:T(1024)(128)(2,1)}, bf16[256,2048]{1,0:T(8,128)(2,1)S(1)}) fusion(f32[256,2048]{1,0:T(8,128)} %get-tuple-element.362, bf16[256,2048]{1,0:T(8,128)(2,1)S(1)} %copy-done.59, bf16[2048,2048]{1,0:T(8,128)(2,1)} %bitcast.616), kind=kOutput, calls=%fused_computation.468 | convolution fusion | flops 2152724480 | bytes 12587008 | tf_op jit(solution)/shard_map/dot_general | solution.py:512
  293.2 3.1 fusion.174
  299.7 5.6 collective-permute-done.35
  305.3 2.9 fusion.39
  310.2 4.5 convert_reduce_fusion.1
  324.5 6.6 %convert_reduce_fusion = (f32[2304]{0:T(1024)}, bf16[256,2304]{1,0:T(8,128)(2,1)S(1)}) fusion(f32[256,2304]{1,0:T(8,128)} %get-tuple-element.360, bf16[256,1152]{1,0:T(8,128)(2,1)} %copy-done.77, bf16[1152,2304]{1,0:T(8,128)(2,1)} %bitcast.579), kind=kOutput, calls=%fused_computation.62 | convolution fusion | flops 1371338496 | bytes 9446400 | tf_op jit(solution)/shard_map/dot_general | solution.py:512
  337.7 2.9 fusion.38
  345.2 5.0 convolution_convert_fusion.1
  354.0 2.8 multiply_reduce_fusion.3
  356.9 3.3 fusion.175
  361.6 3.1 fusion.28
  365.5 5.5 convolution_convert_fusion
  374.7 3.8 fusion.37
  392.8 11.6 %shard_map.363.right_ref = bf16[3,512,576]{2,1,0:T(8,128)(2,1)S(1)} custom-call(bf16[512,576]{1,0:T(8,128)(2,1)S(1)} %copy-done.15, bf16[512,576]{1,0:T(8,128)(2,1)S(1)} %copy-done.17, bf16[512,576]{1,0:T(8,128)(2,1)S(1)} %copy-done.19, f32[512,8]{1,0:T(8,128)S(1)} %copy-done.22, bf16[512,576]{1,0:T(8,128)(2,1)S(1)} %copy-done.20), custom_call_target="tpu_custom_call" | custom-call | flops 2415919104 | bytes 4718592 | tf_op jit(solution)/shard_map/pallas_call | solution.py:212
  418.1 4.9 shard_map.364
  432.5 8.3 %collective-permute-done.48 = bf16[1,2,2,72,576]{4,3,2,1,0:T(8,128)(2,1)S(1)} collective-permute-done((bf16[1,2,2,72,576]{4,3,2,1,0:T(8,128)(2,1)}, bf16[1,2,2,72,576]{4,3,2,1,0:T(8,128)(2,1)S(1)}, u32[]{:S(2)}, u32[]{:S(2)}) %collective-permute-start.48) | collective-permute-done | bytes 331808 | tf_op jit(solution)/shard_map/ppermute | solution.py:239
  440.8 11.5 %collective-permute-done.50 = bf16[1,2,64,2048]{3,2,1,0:T(8,128)(2,1)S(1)} collective-permute-done((bf16[1,2,64,2048]{3,2,1,0:T(8,128)(2,1)S(1)}, bf16[1,2,64,2048]{3,2,1,0:T(8,128)(2,1)S(1)}, u32[]{:S(2)}, u32[]{:S(2)}) %collective-permute-start.50) | collective-permute-done | bytes 524320 | tf_op jit(solution)/shard_map/ppermute | solution.py:239
  482.1 4.1 collective-permute-done.55
  488.3 5.0 collective-permute-done.58
  496.6 6.1 %collective-permute-done.57 = bf16[3,2,2,72,576]{4,3,2,1,0:T(8,128)(2,1)S(1)} collective-permute-done((bf16[3,2,2,72,576]{4,3,2,1,0:T(8,128)(2,1)}, bf16[3,2,2,72,576]{4,3,2,1,0:T(8,128)(2,1)S(1)}, u32[]{:S(2)}, u32[]{:S(2)}) %collective-permute-start.57) | collective-permute-done | bytes 995360 | tf_op jit(solution)/shard_map/ppermute | solution.py:239
  510.1 29.4 %collective-permute-done.62 = bf16[3,2,72,576]{3,2,1,0:T(8,128)(2,1)S(1)} collective-permute-done((bf16[3,2,72,576]{3,2,1,0:T(8,128)(2,1)S(1)}, bf16[3,2,72,576]{3,2,1,0:T(8,128)(2,1)S(1)}, u32[]{:S(2)}, u32[]{:S(2)}) %collective-permute-start.62) | collective-permute-done | bytes 497696 | tf_op jit(solution)/shard_map/ppermute | solution.py:239
  547.2 2.9 collective-permute-start.65
  (649 shorter events, 240.1 us)
Async XLA Ops:
  7.2 202.3 %all-gather.6.cloned.1.call-start = ((), (), s32[]{:S(2)}) async-start(), calls=%async_computation.5 | async-start | bytes 11894784 | tf_op jit(solution)/shard_map/all_gather | solution.py:466
  12.8 12.0 %collective-permute-start.3 = (bf16[1,2,72,576]{3,2,1,0:T(8,128)(2,1)S(1)}, bf16[1,2,72,576]{3,2,1,0:T(8,128)(2,1)S(1)}, u32[]{:S(2)}, u32[]{:S(2)}) collective-permute-start(bf16[1,2,72,576]{3,2,1,0:T(8,128)(2,1)S(1)} %slice_bitcast_fusion.4), channel_id=1, source_target_pairs={{0,16},{2,18},{4,20},{6,22},{8,24},{10,26},{12,28},{14,30},{16,0},... | collective-permute-start | bytes 497672 | tf_op jit(solution)/shard_map/ppermute | solution.py:239
  35.4 221.2 %all-gather.4.cloned.1.call-start = ((), (), s32[]{:S(2)}) async-start(), calls=%async_computation.2 | async-start | bytes 4866048 | tf_op jit(solution)/shard_map/all_gather | solution.py:467
  44.2 13.1 %collective-permute-start.7 = (bf16[6,8,1152]{2,1,0:T(8,128)(2,1)S(1)}, bf16[6,8,1152]{2,1,0:T(8,128)(2,1)S(1)}, u32[]{:S(2)}, u32[]{:S(2)}) collective-permute-start(bf16[6,8,1152]{2,1,0:T(8,128)(2,1)S(1)} %slice.405), channel_id=1, source_target_pairs={{0,8},{2,10},{4,12},{6,14},{8,0},{10,2},{12,4},{14,6},{16,24},{18,... | collective-permute-start | bytes 331784 | tf_op jit(solution)/shard_map/ppermute | solution.py:239
  45.4 27.9 %collective-permute-start.12 = (bf16[4,2,72,576]{3,2,1,0:T(8,128)(2,1)S(1)}, bf16[4,2,72,576]{3,2,1,0:T(8,128)(2,1)S(1)}, u32[]{:S(2)}, u32[]{:S(2)}) collective-permute-start(bf16[4,2,72,576]{3,2,1,0:T(8,128)(2,1)S(1)} %constant_dynamic-update-slice_fusion.4.refs_0_), channel_id=1, source_target_pairs={{0,4},{2,6},{4,0},{6,2},{8,12},{10,14},{12,8},{14,10},{16,20},{18,... | collective-permute-start | bytes 1990664 | tf_op jit(solution)/shard_map/ppermute | solution.py:239
  45.9 19.5 %collective-permute-start.9 = (bf16[1,2,72,576]{3,2,1,0:T(8,128)(2,1)S(1)}, bf16[1,2,72,576]{3,2,1,0:T(8,128)(2,1)S(1)}, u32[]{:S(2)}, u32[]{:S(2)}) collective-permute-start(bf16[1,2,72,576]{3,2,1,0:T(8,128)(2,1)S(1)} %maximum_bitcast_fusion), channel_id=1, source_target_pairs={{0,16},{2,18},{4,20},{6,22},{8,24},{10,26},{12,28},{14,30},{16,0},... | collective-permute-start | bytes 497672 | tf_op jit(solution)/shard_map/ppermute | solution.py:239
  69.8 511.4 %reduce-scatter.5.cloned.1.call-start = ((), (), s32[]{:S(2)}) async-start(), calls=%async_computation.4 | async-start | bytes 5640192 | tf_op jit(solution)/shard_map/reduce_scatter | solution.py:649
  70.2 37.1 %collective-permute-start.16 = (bf16[2,2,72,576]{3,2,1,0:T(8,128)(2,1)S(1)}, bf16[2,2,72,576]{3,2,1,0:T(8,128)(2,1)S(1)}, u32[]{:S(2)}, u32[]{:S(2)}) collective-permute-start(bf16[2,2,72,576]{3,2,1,0:T(8,128)(2,1)S(1)} %constant_dynamic-update-slice_fusion.6), channel_id=1, source_target_pairs={{0,8},{2,10},{4,12},{6,14},{8,0},{10,2},{12,4},{14,6},{16,24},{18,... | collective-permute-start | bytes 995336 | tf_op jit(solution)/shard_map/ppermute | solution.py:239
  70.3 28.5 %collective-permute-start.11 = (bf16[1,1,72,2304]{3,2,1,0:T(8,128)(2,1)S(1)}, bf16[1,1,72,2304]{3,2,1,0:T(8,128)(2,1)S(1)}, u32[]{:S(2)}, u32[]{:S(2)}) collective-permute-start(bf16[1,1,72,2304]{3,2,1,0:T(8,128)(2,1)S(1)} %bitcast.677), channel_id=1, source_target_pairs={{0,16},{2,18},{4,20},{6,22},{8,24},{10,26},{12,28},{14,30},{16,0},... | collective-permute-start | bytes 995336 | tf_op jit(solution)/shard_map/ppermute | solution.py:239
  98.9 43.0 %collective-permute-start.18 = (bf16[2,1,72,2304]{3,2,1,0:T(8,128)(2,1)S(1)}, bf16[2,1,72,2304]{3,2,1,0:T(8,128)(2,1)S(1)}, u32[]{:S(2)}, u32[]{:S(2)}) collective-permute-start(bf16[2,1,72,2304]{3,2,1,0:T(8,128)(2,1)S(1)} %constant_dynamic-update-slice_fusion.8), channel_id=1, source_target_pairs={{0,8},{2,10},{4,12},{6,14},{8,0},{10,2},{12,4},{14,6},{16,24},{18,... | collective-permute-start | bytes 1990664 | tf_op jit(solution)/shard_map/ppermute | solution.py:239
  106.8 37.1 %collective-permute-start.14 = (bf16[4,2,72,576]{3,2,1,0:T(8,128)(2,1)S(1)}, bf16[4,2,72,576]{3,2,1,0:T(8,128)(2,1)S(1)}, u32[]{:S(2)}, u32[]{:S(2)}) collective-permute-start(bf16[4,2,72,576]{3,2,1,0:T(8,128)(2,1)S(1)} %collective-permute-done.12.refs_1_), channel_id=1, source_target_pairs={{0,2},{2,0},{4,6},{6,4},{8,10},{10,8},{12,14},{14,12},{16,18},{18,... | collective-permute-start | bytes 1990664 | tf_op jit(solution)/shard_map/ppermute | solution.py:239
  106.8 36.9 %collective-permute-start.13 = (bf16[4,2,72,576]{3,2,1,0:T(8,128)(2,1)S(1)}, bf16[4,2,72,576]{3,2,1,0:T(8,128)(2,1)S(1)}, u32[]{:S(2)}, u32[]{:S(2)}) collective-permute-start(bf16[4,2,72,576]{3,2,1,0:T(8,128)(2,1)S(1)} %constant_dynamic-update-slice_fusion.4.refs_0_), channel_id=1, source_target_pairs={{0,2},{2,0},{4,6},{6,4},{8,10},{10,8},{12,14},{14,12},{16,18},{18,... | collective-permute-start | bytes 1990664 | tf_op jit(solution)/shard_map/ppermute | solution.py:239
  107.3 53.0 %collective-permute-start.15 = (bf16[1,1,72,2304]{3,2,1,0:T(8,128)(2,1)S(1)}, bf16[1,1,72,2304]{3,2,1,0:T(8,128)(2,1)S(1)}, u32[]{:S(2)}, u32[]{:S(2)}) collective-permute-start(bf16[1,1,72,2304]{3,2,1,0:T(8,128)(2,1)S(1)} %bitcast.679), channel_id=1, source_target_pairs={{0,16},{2,18},{4,20},{6,22},{8,24},{10,26},{12,28},{14,30},{16,0},... | collective-permute-start | bytes 995336 | tf_op jit(solution)/shard_map/ppermute | solution.py:239
  107.4 34.6 %collective-permute-start.17 = (bf16[4,2,72,576]{3,2,1,0:T(8,128)(2,1)S(1)}, bf16[4,2,72,576]{3,2,1,0:T(8,128)(2,1)S(1)}, u32[]{:S(2)}, u32[]{:S(2)}) collective-permute-start(bf16[4,2,72,576]{3,2,1,0:T(8,128)(2,1)S(1)} %constant_dynamic-update-slice_fusion.10.refs_0_), channel_id=1, source_target_pairs={{0,4},{2,6},{4,0},{6,2},{8,12},{10,14},{12,8},{14,10},{16,20},{18,... | collective-permute-start | bytes 1990664 | tf_op jit(solution)/shard_map/ppermute | solution.py:239
  142.1 38.3 %collective-permute-start.22 = (bf16[4,1,72,2304]{3,2,1,0:T(8,128)(2,1)S(1)}, bf16[4,1,72,2304]{3,2,1,0:T(8,128)(2,1)S(1)}, u32[]{:S(2)}, u32[]{:S(2)}) collective-permute-start(bf16[4,1,72,2304]{3,2,1,0:T(8,128)(2,1)S(1)} %constant_dynamic-update-slice_fusion.12.refs_0_), channel_id=1, source_target_pairs={{0,4},{2,6},{4,0},{6,2},{8,12},{10,14},{12,8},{14,10},{16,20},{18,... | collective-permute-start | bytes 3981320 | tf_op jit(solution)/shard_map/ppermute | solution.py:239
  160.3 18.2 %collective-permute-start.23 = (bf16[2,1,72,2304]{3,2,1,0:T(8,128)(2,1)S(1)}, bf16[2,1,72,2304]{3,2,1,0:T(8,128)(2,1)S(1)}, u32[]{:S(2)}, u32[]{:S(2)}) collective-permute-start(bf16[2,1,72,2304]{3,2,1,0:T(8,128)(2,1)S(1)} %constant_dynamic-update-slice_fusion.14), channel_id=1, source_target_pairs={{0,8},{2,10},{4,12},{6,14},{8,0},{10,2},{12,4},{14,6},{16,24},{18,... | collective-permute-start | bytes 1990664 | tf_op jit(solution)/shard_map/ppermute | solution.py:239
  169.2 16.3 %collective-permute-start.21 = (bf16[256,1152]{1,0:T(8,128)(2,1)S(1)}, bf16[256,1152]{1,0:T(8,128)(2,1)S(1)}, u32[]{:S(2)}, u32[]{:S(2)}) collective-permute-start(bf16[256,1152]{1,0:T(8,128)(2,1)S(1)} %convolution_convert_fusion.5), channel_id=1, source_target_pairs={{0,1},{1,0},{2,3},{3,2},{4,5},{5,4},{6,7},{7,6},{8,9},{9,8},{10,11... | collective-permute-start | bytes 1769480 | tf_op jit(solution)/shard_map/ppermute | solution.py:236
  180.3 39.2 %collective-permute-start.27 = (bf16[4,1,72,2304]{3,2,1,0:T(8,128)(2,1)}, bf16[4,1,72,2304]{3,2,1,0:T(8,128)(2,1)}, u32[]{:S(2)}, u32[]{:S(2)}) collective-permute-start(bf16[4,1,72,2304]{3,2,1,0:T(8,128)(2,1)} %constant_dynamic-update-slice_fusion.16.refs_0_), channel_id=1, source_target_pairs={{0,4},{2,6},{4,0},{6,2},{8,12},{10,14},{12,8},{14,10},{16,20},{18,... | collective-permute-start | bytes 3981320 | tf_op jit(solution)/shard_map/ppermute | solution.py:239
  186.9 26.9 %collective-permute-start.26 = (bf16[256,1152]{1,0:T(8,128)(2,1)S(1)}, bf16[256,1152]{1,0:T(8,128)(2,1)}, u32[]{:S(2)}, u32[]{:S(2)}) collective-permute-start(bf16[256,1152]{1,0:T(8,128)(2,1)S(1)} %add_convert_fusion.1), channel_id=1, source_target_pairs={{0,1},{1,0},{2,3},{3,2},{4,5},{5,4},{6,7},{7,6},{8,9},{9,8},{10,11... | collective-permute-start | bytes 1769480 | tf_op jit(solution)/shard_map/ppermute | solution.py:236
  231.4 22.5 %collective-permute-start.30 = (bf16[256,1152]{1,0:T(8,128)(2,1)}, bf16[256,1152]{1,0:T(8,128)(2,1)S(1)}, u32[]{:S(2)}, u32[]{:S(2)}) collective-permute-start(bf16[256,1152]{1,0:T(8,128)(2,1)} %convolution_convert_fusion.8), channel_id=1, source_target_pairs={{0,1},{1,0},{2,3},{3,2},{4,5},{5,4},{6,7},{7,6},{8,9},{9,8},{10,11... | collective-permute-start | bytes 1769480 | tf_op jit(solution)/shard_map/ppermute | solution.py:236
  256.1 15.3 %collective-permute-start.31 = (bf16[256,1152]{1,0:T(8,128)(2,1)S(1)}, bf16[256,1152]{1,0:T(8,128)(2,1)}, u32[]{:S(2)}, u32[]{:S(2)}) collective-permute-start(bf16[256,1152]{1,0:T(8,128)(2,1)S(1)} %add_convert_fusion), channel_id=1, source_target_pairs={{0,1},{1,0},{2,3},{3,2},{4,5},{5,4},{6,7},{7,6},{8,9},{9,8},{10,11... | collective-permute-start | bytes 1769480 | tf_op jit(solution)/shard_map/ppermute | solution.py:236
  283.5 21.8 %collective-permute-start.34 = (bf16[1,2,2,2,2,64,2048]{6,5,4,3,2,1,0:T(8,128)(2,1)}, bf16[1,2,2,2,2,64,2048]{6,5,4,3,2,1,0:T(8,128)(2,1)}, u32[]{:S(2)}, u32[]{:S(2)}) collective-permute-start(bf16[1,2,2,2,2,64,2048]{6,5,4,3,2,1,0:T(8,128)(2,1)} %dynamic-slice_bitcast_fusion), channel_id=1, source_target_pairs={{0,2},{2,0},{4,6},{6,4},{8,10},{10,8},{12,14},{14,12},{16,18},{18,... | collective-permute-start | bytes 12582920 | tf_op jit(solution)/shard_map/ppermute | solution.py:239
  285.8 19.5 %collective-permute-start.35 = (bf16[1,2,2,2,24,2048]{5,4,3,2,1,0:T(8,128)(2,1)S(1)}, bf16[1,2,2,2,24,2048]{5,4,3,2,1,0:T(8,128)(2,1)S(1)}, u32[]{:S(2)}, u32[]{:S(2)}) collective-permute-start(bf16[1,2,2,2,24,2048]{5,4,3,2,1,0:T(8,128)(2,1)S(1)} %fusion.40), channel_id=1, source_target_pairs={{0,4},{2,6},{4,0},{6,2},{8,12},{10,14},{12,8},{14,10},{16,20},{18,... | collective-permute-start | bytes 2359304 | tf_op jit(solution)/shard_map/ppermute | solution.py:239
  296.4 18.4 %collective-permute-start.36 = (bf16[256,1152]{1,0:T(8,128)(2,1)S(1)}, bf16[256,1152]{1,0:T(8,128)(2,1)S(1)}, u32[]{:S(2)}, u32[]{:S(2)}) collective-permute-start(bf16[256,1152]{1,0:T(8,128)(2,1)S(1)} %get-tuple-element.218), channel_id=1, source_target_pairs={{0,1},{1,0},{2,3},{3,2},{4,5},{5,4},{6,7},{7,6},{8,9},{9,8},{10,11... | collective-permute-start | bytes 1769480 | tf_op jit(solution)/shard_map/ppermute | solution.py:236
  318.8 15.4 %collective-permute-start.38 = (bf16[1,2,2,2,2,64,1152]{6,5,4,3,2,1,0:T(8,128)(2,1)}, bf16[1,2,2,2,2,64,1152]{6,5,4,3,2,1,0:T(8,128)(2,1)}, u32[]{:S(2)}, u32[]{:S(2)}) collective-permute-start(bf16[1,2,2,2,2,64,1152]{6,5,4,3,2,1,0:T(8,128)(2,1)} %dynamic-slice_bitcast_fusion.1), channel_id=1, source_target_pairs={{0,2},{2,0},{4,6},{6,4},{8,10},{10,8},{12,14},{14,12},{16,18},{18,... | collective-permute-start | bytes 7077896 | tf_op jit(solution)/shard_map/ppermute | solution.py:239
  324.2 26.3 %collective-permute-start.41 = (bf16[1,2,2,64,2048]{4,3,2,1,0:T(8,128)(2,1)}, bf16[1,2,2,64,2048]{4,3,2,1,0:T(8,128)(2,1)}, u32[]{:S(2)}, u32[]{:S(2)}) collective-permute-start(bf16[1,2,2,64,2048]{4,3,2,1,0:T(8,128)(2,1)} %fusion.39), channel_id=1, source_target_pairs={{0,4},{2,6},{4,0},{6,2},{8,12},{10,14},{12,8},{14,10},{16,20},{18,... | collective-permute-start | bytes 3145736 | tf_op jit(solution)/shard_map/ppermute | solution.py:239
  333.6 16.6 %collective-permute-start.40 = (bf16[256,1152]{1,0:T(8,128)(2,1)}, bf16[256,1152]{1,0:T(8,128)(2,1)S(1)}, u32[]{:S(2)}, u32[]{:S(2)}) collective-permute-start(bf16[256,1152]{1,0:T(8,128)(2,1)} %convolution_convert_fusion.6), channel_id=1, source_target_pairs={{0,1},{1,0},{2,3},{3,2},{4,5},{5,4},{6,7},{7,6},{8,9},{9,8},{10,11... | collective-permute-start | bytes 1769480 | tf_op jit(solution)/shard_map/ppermute | solution.py:236
  336.2 14.3 %collective-permute-start.39 = (bf16[1,2,24,2048]{3,2,1,0:T(8,128)(2,1)}, bf16[1,2,24,2048]{3,2,1,0:T(8,128)(2,1)}, u32[]{:S(2)}, u32[]{:S(2)}) collective-permute-start(bf16[1,2,24,2048]{3,2,1,0:T(8,128)(2,1)} %fusion.61), channel_id=1, source_target_pairs={{0,8},{2,10},{4,12},{6,14},{8,0},{10,2},{12,4},{14,6},{16,24},{18,... | collective-permute-start | bytes 589832 | tf_op jit(solution)/shard_map/ppermute | solution.py:239
  340.7 32.3 %collective-permute-start.42 = (bf16[1,2,2,64,2048]{4,3,2,1,0:T(8,128)(2,1)}, bf16[1,2,2,64,2048]{4,3,2,1,0:T(8,128)(2,1)}, u32[]{:S(2)}, u32[]{:S(2)}) collective-permute-start(bf16[1,2,2,64,2048]{4,3,2,1,0:T(8,128)(2,1)} %fusion.38), channel_id=1, source_target_pairs={{0,4},{2,6},{4,0},{6,2},{8,12},{10,14},{12,8},{14,10},{16,20},{18,... | collective-permute-start | bytes 3145736 | tf_op jit(solution)/shard_map/ppermute | solution.py:239
  360.1 14.6 %collective-permute-start.44 = (bf16[256,1152]{1,0:T(8,128)(2,1)S(1)}, bf16[256,1152]{1,0:T(8,128)(2,1)}, u32[]{:S(2)}, u32[]{:S(2)}) collective-permute-start(bf16[256,1152]{1,0:T(8,128)(2,1)S(1)} %get-tuple-element.232), channel_id=1, source_target_pairs={{0,1},{1,0},{2,3},{3,2},{4,5},{5,4},{6,7},{7,6},{8,9},{9,8},{10,11... | collective-permute-start | bytes 1769480 | tf_op jit(solution)/shard_map/ppermute | solution.py:236
  364.7 39.9 %collective-permute-start.47 = (bf16[1,2,2,2,64,1152]{5,4,3,2,1,0:T(8,128)(2,1)}, bf16[1,2,2,2,64,1152]{5,4,3,2,1,0:T(8,128)(2,1)}, u32[]{:S(2)}, u32[]{:S(2)}) collective-permute-start(bf16[1,2,2,2,64,1152]{5,4,3,2,1,0:T(8,128)(2,1)} %fusion.28), channel_id=1, source_target_pairs={{0,4},{2,6},{4,0},{6,2},{8,12},{10,14},{12,8},{14,10},{16,20},{18,... | collective-permute-start | bytes 3538952 | tf_op jit(solution)/shard_map/ppermute | solution.py:239
  378.6 26.0 %collective-permute-start.46 = (bf16[1,2,2,64,2048]{4,3,2,1,0:T(8,128)(2,1)}, bf16[1,2,2,64,2048]{4,3,2,1,0:T(8,128)(2,1)}, u32[]{:S(2)}, u32[]{:S(2)}) collective-permute-start(bf16[1,2,2,64,2048]{4,3,2,1,0:T(8,128)(2,1)} %fusion.37), channel_id=1, source_target_pairs={{0,1},{1,0},{2,3},{3,2},{4,5},{5,4},{6,7},{7,6},{8,9},{9,8},{10,11... | collective-permute-start | bytes 3145736 | tf_op jit(solution)/shard_map/ppermute | solution.py:236
  384.4 198.7 %reduce-scatter.3.cloned.1.call-start = ((), (), s32[]{:S(2)}) async-start(), calls=%async_computation.3 | async-start | bytes 5640192 | tf_op jit(solution)/shard_map/reduce_scatter | solution.py:671
  424.5 30.5 %collective-permute-start.52 = (bf16[3,8,72,576]{3,2,1,0:T(8,128)(2,1)}, bf16[3,8,72,576]{3,2,1,0:T(8,128)(2,1)}, u32[]{:S(2)}, u32[]{:S(2)}) collective-permute-start(bf16[3,8,72,576]{3,2,1,0:T(8,128)(2,1)} %get-tuple-element.244), channel_id=1, source_target_pairs={{0,2},{2,0},{4,6},{6,4},{8,10},{10,8},{12,14},{14,12},{16,18},{18,... | collective-permute-start | bytes 5971976 | tf_op jit(solution)/shard_map/ppermute | solution.py:239
  426.7 25.6 %collective-permute-start.49 = (bf16[1,2,2,64,1152]{4,3,2,1,0:T(8,128)(2,1)S(1)}, bf16[1,2,2,64,1152]{4,3,2,1,0:T(8,128)(2,1)S(1)}, u32[]{:S(2)}, u32[]{:S(2)}) collective-permute-start(bf16[1,2,2,64,1152]{4,3,2,1,0:T(8,128)(2,1)S(1)} %copy-done.76), channel_id=1, source_target_pairs={{0,1},{1,0},{2,3},{3,2},{4,5},{5,4},{6,7},{7,6},{8,9},{9,8},{10,11... | collective-permute-start | bytes 1769480 | tf_op jit(solution)/shard_map/ppermute | solution.py:236
  428.4 23.9 %collective-permute-start.50 = (bf16[1,2,64,2048]{3,2,1,0:T(8,128)(2,1)S(1)}, bf16[1,2,64,2048]{3,2,1,0:T(8,128)(2,1)S(1)}, u32[]{:S(2)}, u32[]{:S(2)}) collective-permute-start(bf16[1,2,64,2048]{3,2,1,0:T(8,128)(2,1)S(1)} %copy-done.79), channel_id=1, source_target_pairs={{0,8},{2,10},{4,12},{6,14},{8,0},{10,2},{12,4},{14,6},{16,24},{18,... | collective-permute-start | bytes 1572872 | tf_op jit(solution)/shard_map/ppermute | solution.py:239
  428.9 26.1 %collective-permute-start.51 = (bf16[256,1152]{1,0:T(8,128)(2,1)S(1)}, bf16[256,1152]{1,0:T(8,128)(2,1)S(1)}, u32[]{:S(2)}, u32[]{:S(2)}) collective-permute-start(bf16[256,1152]{1,0:T(8,128)(2,1)S(1)} %copy-done.74), channel_id=1, source_target_pairs={{0,1},{1,0},{2,3},{3,2},{4,5},{5,4},{6,7},{7,6},{8,9},{9,8},{10,11... | collective-permute-start | bytes 1769480 | tf_op jit(solution)/shard_map/ppermute | solution.py:236
  473.9 12.3 %collective-permute-start.55 = (bf16[4,17536]{1,0:T(4,128)(2,1)S(1)}, bf16[4,17536]{1,0:T(4,128)(2,1)S(1)}, u32[]{:S(2)}, u32[]{:S(2)}) collective-permute-start(bf16[4,17536]{1,0:T(4,128)(2,1)S(1)} %reshape.2063), channel_id=1, source_target_pairs={{0,16},{2,18},{4,20},{6,22},{8,24},{10,26},{12,28},{14,30},{16,0},... | collective-permute-start | bytes 420872 | tf_op jit(solution)/shard_map/ppermute | solution.py:239
  478.0 24.7 %collective-permute-start.57 = (bf16[3,2,2,72,576]{4,3,2,1,0:T(8,128)(2,1)}, bf16[3,2,2,72,576]{4,3,2,1,0:T(8,128)(2,1)S(1)}, u32[]{:S(2)}, u32[]{:S(2)}) collective-permute-start(bf16[3,2,2,72,576]{4,3,2,1,0:T(8,128)(2,1)} %pad_maximum_fusion.6), channel_id=1, source_target_pairs={{0,4},{2,6},{4,0},{6,2},{8,12},{10,14},{12,8},{14,10},{16,20},{18,... | collective-permute-start | bytes 2985992 | tf_op jit(solution)/shard_map/ppermute | solution.py:239
  479.6 13.6 %collective-permute-start.58 = (bf16[1,64,2048]{2,1,0:T(8,128)(2,1)S(1)}, bf16[1,64,2048]{2,1,0:T(8,128)(2,1)S(1)}, u32[]{:S(2)}, u32[]{:S(2)}) collective-permute-start(bf16[1,64,2048]{2,1,0:T(8,128)(2,1)S(1)} %fusion.60), channel_id=1, source_target_pairs={{0,16},{2,18},{4,20},{6,22},{8,24},{10,26},{12,28},{14,30},{16,0},... | collective-permute-start | bytes 786440 | tf_op jit(solution)/shard_map/ppermute | solution.py:239
  480.1 22.7 %collective-permute-start.59 = (bf16[1,2,64,1152]{3,2,1,0:T(8,128)(2,1)}, bf16[1,2,64,1152]{3,2,1,0:T(8,128)(2,1)S(1)}, u32[]{:S(2)}, u32[]{:S(2)}) collective-permute-start(bf16[1,2,64,1152]{3,2,1,0:T(8,128)(2,1)} %fusion.57), channel_id=1, source_target_pairs={{0,8},{2,10},{4,12},{6,14},{8,0},{10,2},{12,4},{14,6},{16,24},{18,... | collective-permute-start | bytes 884744 | tf_op jit(solution)/shard_map/ppermute | solution.py:239
  481.7 21.1 %collective-permute-start.60 = (bf16[1,2,72,576]{3,2,1,0:T(8,128)(2,1)}, bf16[1,2,72,576]{3,2,1,0:T(8,128)(2,1)S(1)}, u32[]{:S(2)}, u32[]{:S(2)}) collective-permute-start(bf16[1,2,72,576]{3,2,1,0:T(8,128)(2,1)} %fusion.69), channel_id=1, source_target_pairs={{0,8},{2,10},{4,12},{6,14},{8,0},{10,2},{12,4},{14,6},{16,24},{18,... | collective-permute-start | bytes 497672 | tf_op jit(solution)/shard_map/ppermute | solution.py:239
  493.2 15.0 %collective-permute-start.56 = (bf16[8,17536]{1,0:T(8,128)(2,1)S(1)}, bf16[8,17536]{1,0:T(8,128)(2,1)S(1)}, u32[]{:S(2)}, u32[]{:S(2)}) collective-permute-start(bf16[8,17536]{1,0:T(8,128)(2,1)S(1)} %pad_maximum_fusion.11), channel_id=1, source_target_pairs={{0,8},{2,10},{4,12},{6,14},{8,0},{10,2},{12,4},{14,6},{16,24},{18,... | collective-permute-start | bytes 841736 | tf_op jit(solution)/shard_map/ppermute | solution.py:239
  506.5 32.9 %collective-permute-start.62 = (bf16[3,2,72,576]{3,2,1,0:T(8,128)(2,1)S(1)}, bf16[3,2,72,576]{3,2,1,0:T(8,128)(2,1)S(1)}, u32[]{:S(2)}, u32[]{:S(2)}) collective-permute-start(bf16[3,2,72,576]{3,2,1,0:T(8,128)(2,1)S(1)} %pad_maximum_fusion.8), channel_id=1, source_target_pairs={{0,8},{2,10},{4,12},{6,14},{8,0},{10,2},{12,4},{14,6},{16,24},{18,... | collective-permute-start | bytes 1493000 | tf_op jit(solution)/shard_map/ppermute | solution.py:239
  508.5 33.3 %collective-permute-start.61 = (bf16[16,17536]{1,0:T(8,128)(2,1)S(1)}, bf16[16,17536]{1,0:T(8,128)(2,1)S(1)}, u32[]{:S(2)}, u32[]{:S(2)}) collective-permute-start(bf16[16,17536]{1,0:T(8,128)(2,1)S(1)} %pad_maximum_fusion.7), channel_id=1, source_target_pairs={{0,2},{2,0},{4,6},{6,4},{8,10},{10,8},{12,14},{14,12},{16,18},{18,... | collective-permute-start | bytes 1683464 | tf_op jit(solution)/shard_map/ppermute | solution.py:239
  543.7 35.1 %collective-permute-start.64 = (bf16[3,72,576]{2,1,0:T(8,128)(2,1)}, bf16[3,72,576]{2,1,0:T(8,128)(2,1)}, u32[]{:S(2)}, u32[]{:S(2)}) collective-permute-start(bf16[3,72,576]{2,1,0:T(8,128)(2,1)} %pad_maximum_fusion.12), channel_id=1, source_target_pairs={{0,16},{2,18},{4,20},{6,22},{8,24},{10,26},{12,28},{14,30},{16,0},... | collective-permute-start | bytes 746504 | tf_op jit(solution)/shard_map/ppermute | solution.py:239
  547.2 27.9 %collective-permute-start.65 = (bf16[1,72,576]{2,1,0:T(8,128)(2,1)}, bf16[1,72,576]{2,1,0:T(8,128)(2,1)}, u32[]{:S(2)}, u32[]{:S(2)}) collective-permute-start(bf16[1,72,576]{2,1,0:T(8,128)(2,1)} %fusion.103), channel_id=1, source_target_pairs={{0,16},{2,18},{4,20},{6,22},{8,24},{10,26},{12,28},{14,30},{16,0},... | collective-permute-start | bytes 248840 | tf_op jit(solution)/shard_map/ppermute | solution.py:239
  550.1 26.6 %collective-permute-start.66 = (bf16[1,64,1152]{2,1,0:T(8,128)(2,1)}, bf16[1,64,1152]{2,1,0:T(8,128)(2,1)}, u32[]{:S(2)}, u32[]{:S(2)}) collective-permute-start(bf16[1,64,1152]{2,1,0:T(8,128)(2,1)} %fusion.89), channel_id=1, source_target_pairs={{0,16},{2,18},{4,20},{6,22},{8,24},{10,26},{12,28},{14,30},{16,0},... | collective-permute-start | bytes 442376 | tf_op jit(solution)/shard_map/ppermute | solution.py:239
  (171 other events, 1305.7 us)
Sparse Core Ops, SparseCore 0:
  35.5 127.0 all-gather.5
  165.6 66.6 all-gather.3
  384.5 88.9 reduce-scatter.4
  477.4 93.7 reduce-scatter.2
